TPU v7x, 32 devices: a whole 2x2x4 slice. The times are simulated.
32 devices in a mesh: rows: 8 (over y, x, core), heads: 4 (over z).
Axes of the slice: x: 2, y: 2, z: 4, core: 2. Of those that a mesh axis runs over, the one named last changes fastest.
Arguments:
- tokens: bfloat16 [32, 512, 1024], P('rows', 'heads'), may hold values from -6 to 6
- doc_lengths: int32 [32, 4], P('rows'), may hold values from 1 to 509, as said below
- cotangent: bfloat16 [32, 512, 1024], P('rows', 'heads'), may hold values from -6 to 6
- w_query: bfloat16 [1024, 1024], P('rows'), may hold values from -0.1875 to 0.1875
- w_key: bfloat16 [1024, 1024], P('rows'), may hold values from -0.1875 to 0.1875
- w_value: bfloat16 [1024, 1024], P('rows'), may hold values from -0.1875 to 0.1875
- w_gate: bfloat16 [1024, 1024], P('rows'), may hold values from -0.1875 to 0.1875
- w_out: bfloat16 [1024, 1024], P('rows'), may hold values from -0.3125 to 0.3125
- w_left: bfloat16 [1024, 2816], P('rows'), may hold values from -0.1875 to 0.1875
- w_right: bfloat16 [1024, 2816], P('rows'), may hold values from -0.1875 to 0.1875
- w_down: bfloat16 [2816, 1024], P('rows'), may hold values from -0.109375 to 0.109375
Outputs:
- activations: bfloat16 [32, 512, 1024], P('rows', 'heads')
- input_grad: float32 [32, 512, 1024], P('rows', 'heads')
- grad_query: float32 [1024, 1024], P('rows', 'heads')
- grad_key: float32 [1024, 1024], P('rows', 'heads')
- grad_value: float32 [1024, 1024], P('rows', 'heads')
- grad_gate: float32 [1024, 1024], P('rows', 'heads')
- grad_out: float32 [1024, 1024], P('rows', 'heads')
- grad_left: float32 [1024, 2816], P('rows', 'heads')
- grad_right: float32 [1024, 2816], P('rows', 'heads')
- grad_down: float32 [2816, 1024], P('rows', 'heads')
Inputs may be any that keep to these rules, and one draw needn't show every extreme that they name: `doc_lengths`: each row holds 4 documents whose lengths sum to 512; in each group of 4 rows along heads, one row, drawn from the seed, holds a document of 509 tokens.
All inputs are finite; a program needn't handle non-finite values.
Results may differ from a plain program's by a relative error of at most 0.012.
Values may be sent and summed in bfloat16 or wider, within the bound.
No kernel may reach another device: no remote copies, remote signals or barrier semaphores. Data moves between devices by JAX's collectives and lax.ppermute only.
A program may use at most 256 MiB of HBM per device.

v0:
```python
import math

import jax
import jax.numpy as jnp
from jax import lax
from jax.sharding import PartitionSpec as P

HEADS = 8
HEAD_DIM = 128


EPS = 1e-06
HIGH = lax.Precision.HIGHEST


def norm_scale(v):
    return lax.rsqrt(jnp.mean(v * v, axis=-1, keepdims=True) + EPS)


def norm_back(v, scale, grad):
    inner = jnp.mean(grad * v, axis=-1, keepdims=True)
    return scale * grad - v * (scale * scale * scale) * inner


def swish_slope(v):
    sig = jax.nn.sigmoid(v)
    return sig * (1.0 + v * (1.0 - sig))


def project(a, w):
    return jnp.einsum("std,de->ste", a, w, preferred_element_type=jnp.float32)


def back_project(g, w):
    return jnp.einsum("ste,de->std", g, w, preferred_element_type=jnp.float32)


def weight_grad(a, g):
    return jnp.einsum("std,ste->de", a, g, preferred_element_type=jnp.float32)


def document_ids(lengths, length):
    ends = jnp.cumsum(lengths, axis=-1, dtype=jnp.int32)[:, :-1]
    places = jnp.arange(length, dtype=jnp.int32)
    return jnp.sum((places[None, :, None] >= ends[:, None, :]).astype(jnp.int32), axis=-1)


def rotate(a):
    width = a.shape[-1]
    places = jnp.arange(a.shape[1], dtype=jnp.float32)
    theta = jnp.exp(-math.log(10000.0) * jnp.arange(width, dtype=jnp.float32) / width)
    angle = places[:, None] * theta[None, :]
    cosine = jnp.cos(angle)[None, :, None, :]
    sine = jnp.sin(angle)[None, :, None, :]
    return jnp.concatenate([a * cosine, a * sine], axis=-1)


def attend(query, keys, values, docs, slopes):
    seqs, length, heads_here, width = query.shape
    block = math.gcd(length, 512)
    count = length // block
    q_rot = (
        rotate(query).reshape(seqs, count, block, heads_here, 2 * width).transpose(1, 0, 3, 2, 4)
    )
    k_rot = rotate(keys).reshape(seqs, count, block, heads_here, 2 * width).transpose(1, 0, 3, 2, 4)
    v_blocks = values.reshape(seqs, count, block, heads_here, width).transpose(1, 0, 3, 2, 4)
    d_blocks = docs.reshape(seqs, count, block).transpose(1, 0, 2)
    places = jnp.arange(block, dtype=jnp.float32)
    gap = places[:, None] - places[None, :]
    intra = jnp.where(
        gap[None] >= 0.0,
        jnp.exp(-slopes[:, None, None] * jnp.maximum(gap, 0.0)[None]),
        jnp.float32(0.0),
    )
    enter = jnp.exp(-slopes[:, None] * (places[None, :] + 1.0))
    leave = jnp.exp(-slopes[:, None] * (block - 1.0 - places[None, :]))
    carry_decay = jnp.exp(-slopes * block)

    def advance(carry, item):
        state, last = carry
        q_block, k_block, v_block, d_block = item
        same = (d_block[:, :, None] == d_block[:, None, :]).astype(jnp.float32)
        scores = jnp.einsum("shie,shje->shij", q_block, k_block, precision=HIGH)
        weights = scores * intra[None] * same[:, None]
        local = jnp.einsum("shij,shje->shie", weights, v_block, precision=HIGH)
        link = (d_block == last[:, None]).astype(jnp.float32)
        carried = jnp.einsum("shie,shef->shif", q_block, state, precision=HIGH)
        carried = carried * (enter[None, :, :, None] * link[:, None, :, None])
        final = d_block[:, -1]
        tail = (d_block == final[:, None]).astype(jnp.float32)
        kept = (final == last).astype(jnp.float32)
        fresh = jnp.einsum(
            "shje,shjf->shef",
            k_block * (leave[None, :, :, None] * tail[:, None, :, None]),
            v_block,
            precision=HIGH,
        )
        state = state * (kept[:, None, None, None] * carry_decay[None, :, None, None]) + fresh
        return ((state, final), local + carried)

    start = (
        jnp.zeros((seqs, heads_here, 2 * width, width), jnp.float32),
        jnp.full((seqs,), -1, jnp.int32),
    )
    _, mixed = lax.scan(advance, start, (q_rot, k_rot, v_blocks, d_blocks))
    return mixed.transpose(1, 0, 3, 2, 4).reshape(seqs, length, heads_here, width)


def on_device(
    tokens, doc_lengths, cotangent, w_query, w_key, w_value, w_gate, w_out, w_left, w_right, w_down
):
    shards = (w_query, w_key, w_value, w_gate, w_out, w_left, w_right, w_down)
    full_q, full_k, full_v, full_u, full_o, full_l, full_r, full_d = (
        lax.all_gather(shards[0], "rows", axis=0, tiled=True),
        lax.all_gather(shards[1], "rows", axis=0, tiled=True),
        lax.all_gather(shards[2], "rows", axis=0, tiled=True),
        lax.all_gather(shards[3], "rows", axis=0, tiled=True),
        lax.all_gather(shards[4], "rows", axis=0, tiled=True),
        lax.all_gather(shards[5], "rows", axis=0, tiled=True),
        lax.all_gather(shards[6], "rows", axis=0, tiled=True),
        lax.all_gather(shards[7], "rows", axis=0, tiled=True),
    )
    x_in = tokens.astype(jnp.float32)
    scale_in = norm_scale(x_in)
    h_in = (x_in * scale_in).astype(jnp.bfloat16)
    q_pre = project(h_in, full_q)
    k_pre = project(h_in, full_k)
    v_pre = project(h_in, full_v)
    u_pre = project(h_in, full_u)
    query = jax.nn.silu(q_pre).astype(jnp.bfloat16)
    key_part = jax.nn.silu(k_pre).astype(jnp.bfloat16)
    value = v_pre.astype(jnp.bfloat16)
    gate = jax.nn.silu(u_pre)
    q_heads, k_heads, v_heads = (
        lax.all_to_all(query, "heads", split_axis=2, concat_axis=1, tiled=True),
        lax.all_to_all(key_part, "heads", split_axis=2, concat_axis=1, tiled=True),
        lax.all_to_all(value, "heads", split_axis=2, concat_axis=1, tiled=True),
    )
    seqs, length, local_width = q_heads.shape
    heads_here = local_width // HEAD_DIM
    docs = document_ids(doc_lengths, length)
    numbers = (
        lax.axis_index("heads") * heads_here + jnp.arange(heads_here, dtype=jnp.int32)
    ).astype(jnp.float32) + 1.0
    slopes = jnp.exp2(-8.0 * numbers / HEADS)

    def mix(q_full, k_full, v_full):
        shape4 = (seqs, length, heads_here, HEAD_DIM)
        result = attend(
            q_full.reshape(shape4), k_full.reshape(shape4), v_full.reshape(shape4), docs, slopes
        )
        return result.reshape(seqs, length, local_width)

    mixed_heads, mix_back = jax.vjp(
        mix, q_heads.astype(jnp.float32), k_heads.astype(jnp.float32), v_heads.astype(jnp.float32)
    )
    mixed = lax.all_to_all(
        mixed_heads.astype(jnp.bfloat16), "heads", split_axis=1, concat_axis=2, tiled=True
    )
    mixed_f = mixed.astype(jnp.float32)
    scale_mix = norm_scale(mixed_f)
    normed = mixed_f * scale_mix
    gated = (normed * gate).astype(jnp.bfloat16)
    x_mid = x_in + project(gated, full_o)
    scale_mid = norm_scale(x_mid)
    h_mid = (x_mid * scale_mid).astype(jnp.bfloat16)
    left = project(h_mid, full_l)
    right = project(h_mid, full_r)
    product = (left * right).astype(jnp.bfloat16)
    activations = (x_mid + project(product, full_d)).astype(jnp.bfloat16)
    g_down = weight_grad(product, cotangent)
    grad_product = back_project(cotangent, full_d)
    d_left = (grad_product * right).astype(jnp.bfloat16)
    d_right = (grad_product * left).astype(jnp.bfloat16)
    g_left = weight_grad(h_mid, d_left)
    g_right = weight_grad(h_mid, d_right)
    grad_hmid = back_project(d_left, full_l) + back_project(d_right, full_r)
    d_mid = cotangent.astype(jnp.float32) + norm_back(x_mid, scale_mid, grad_hmid)
    d_branch = d_mid.astype(jnp.bfloat16)
    g_out = weight_grad(gated, d_branch)
    d_gated = back_project(d_branch, full_o)
    d_u = (d_gated * normed * swish_slope(u_pre)).astype(jnp.bfloat16)
    d_mix = norm_back(mixed_f, scale_mix, d_gated * gate).astype(jnp.bfloat16)
    d_heads = lax.all_to_all(d_mix, "heads", split_axis=2, concat_axis=1, tiled=True)
    gq_heads, gk_heads, gv_heads = mix_back(d_heads.astype(jnp.float32))
    d_query, d_key, d_value = (
        lax.all_to_all(
            gq_heads.astype(jnp.bfloat16), "heads", split_axis=1, concat_axis=2, tiled=True
        ),
        lax.all_to_all(
            gk_heads.astype(jnp.bfloat16), "heads", split_axis=1, concat_axis=2, tiled=True
        ),
        lax.all_to_all(
            gv_heads.astype(jnp.bfloat16), "heads", split_axis=1, concat_axis=2, tiled=True
        ),
    )
    d_q = (d_query.astype(jnp.float32) * swish_slope(q_pre)).astype(jnp.bfloat16)
    d_k = (d_key.astype(jnp.float32) * swish_slope(k_pre)).astype(jnp.bfloat16)
    g_query = weight_grad(h_in, d_q)
    g_key = weight_grad(h_in, d_k)
    g_value = weight_grad(h_in, d_value)
    g_gate = weight_grad(h_in, d_u)
    grad_hin = (
        back_project(d_q, full_q)
        + back_project(d_k, full_k)
        + back_project(d_value, full_v)
        + back_project(d_u, full_u)
    )
    input_grad = d_mid + norm_back(x_in, scale_in, grad_hin)
    row_sums = (
        lax.psum_scatter(g_query, "rows", scatter_dimension=0, tiled=True),
        lax.psum_scatter(g_key, "rows", scatter_dimension=0, tiled=True),
        lax.psum_scatter(g_value, "rows", scatter_dimension=0, tiled=True),
        lax.psum_scatter(g_gate, "rows", scatter_dimension=0, tiled=True),
        lax.psum_scatter(g_out, "rows", scatter_dimension=0, tiled=True),
        lax.psum_scatter(g_left, "rows", scatter_dimension=0, tiled=True),
        lax.psum_scatter(g_right, "rows", scatter_dimension=0, tiled=True),
        lax.psum_scatter(g_down, "rows", scatter_dimension=0, tiled=True),
    )
    g_query, g_key, g_value, g_gate, g_out, g_left, g_right, g_down = (
        lax.psum_scatter(row_sums[0], "heads", scatter_dimension=1, tiled=True),
        lax.psum_scatter(row_sums[1], "heads", scatter_dimension=1, tiled=True),
        lax.psum_scatter(row_sums[2], "heads", scatter_dimension=1, tiled=True),
        lax.psum_scatter(row_sums[3], "heads", scatter_dimension=1, tiled=True),
        lax.psum_scatter(row_sums[4], "heads", scatter_dimension=1, tiled=True),
        lax.psum_scatter(row_sums[5], "heads", scatter_dimension=1, tiled=True),
        lax.psum_scatter(row_sums[6], "heads", scatter_dimension=1, tiled=True),
        lax.psum_scatter(row_sums[7], "heads", scatter_dimension=1, tiled=True),
    )
    return (
        activations,
        input_grad,
        g_query,
        g_key,
        g_value,
        g_gate,
        g_out,
        g_left,
        g_right,
        g_down,
    )


def solution(mesh):
    in_specs = (
        P("rows", "heads", None),
        P("rows", None),
        P("rows", "heads", None),
        P("rows", None),
        P("rows", None),
        P("rows", None),
        P("rows", None),
        P("rows", None),
        P("rows", None),
        P("rows", None),
        P("rows", None),
    )
    out_specs = (
        P("rows", "heads", None),
        P("rows", "heads", None),
        P("rows", "heads"),
        P("rows", "heads"),
        P("rows", "heads"),
        P("rows", "heads"),
        P("rows", "heads"),
        P("rows", "heads"),
        P("rows", "heads"),
        P("rows", "heads"),
    )
    return jax.shard_map(
        on_device, mesh=mesh, in_specs=in_specs, out_specs=out_specs, check_vma=False
    )
```

profile of v0, /device:TPU:0, one launch (start us, length us, event | category | flops | bytes accessed | tf_op | source)
XLA Modules:
  0.0 1107.8 jit_solution(3151782040009321138)
XLA Ops:
  12.8 27.8 %all-gather.9.cloned.1.call-done = bf16[1024,1024]{1,0:T(8,128)(2,1)} async-done(((bf16[128,1024]{1,0:T(8,128)(2,1)}), bf16[1024,1024]{1,0:T(8,128)(2,1)}) %all-gather.9.cloned.1.call-update) | async-done | bytes 2097168 | tf_op jit(solution)/shard_map/all_gather | solution.py:114
  50.9 19.4 %all-gather.11.cloned.1.call-done = bf16[1024,1024]{1,0:T(8,128)(2,1)} async-done(((bf16[128,1024]{1,0:T(8,128)(2,1)}), bf16[1024,1024]{1,0:T(8,128)(2,1)}) %all-gather.11.cloned.1.call-update) | async-done | bytes 2097168 | tf_op jit(solution)/shard_map/all_gather | solution.py:115
  84.2 16.0 %all-gather.13.cloned.1.call-done = bf16[1024,1024]{1,0:T(8,128)(2,1)} async-done(((bf16[128,1024]{1,0:T(8,128)(2,1)}), bf16[1024,1024]{1,0:T(8,128)(2,1)}) %all-gather.13.cloned.1.call-update) | async-done | bytes 2097168 | tf_op jit(solution)/shard_map/all_gather | solution.py:116
  127.1 10.2 all-to-all-done.2
  148.5 9.5 fusion.26
  158.0 10.1 fusion.1
  168.1 8.7 add_convert_fusion.2
  179.1 29.2 %all_to_all.96 = bf16[4,512,256]{2,0,1:T(4,128)(2,1)S(1)} all-to-all(bf16[4,512,256]{2,0,1:T(4,128)(2,1)} %copy.203), channel_id=1, replica_groups=mesh['rows'=8,'heads'=4] {'heads'}, dimensions={1} | all-to-all | bytes 2097152 | tf_op jit(solution)/shard_map/all_to_all | solution.py:157
  222.3 8.7 fusion.10
  231.1 18.8 %all-gather.19.cloned.1.call-done = bf16[1024,2816]{1,0:T(8,128)(2,1)} async-done(((bf16[128,2816]{1,0:T(8,128)(2,1)}), bf16[1024,2816]{1,0:T(8,128)(2,1)}) %all-gather.19.cloned.1.call-update) | async-done | bytes 5767184 | tf_op jit(solution)/shard_map/all_gather | solution.py:119
  249.8 8.6 fusion.14
  258.5 36.6 %all-gather.23.cloned.1.call-done = bf16[2816,1024]{1,0:T(8,128)(2,1)} async-done(((bf16[352,1024]{1,0:T(8,128)(2,1)}), bf16[2816,1024]{1,0:T(8,128)(2,1)}) %all-gather.23.cloned.1.call-update) | async-done | bytes 5767184 | tf_op jit(solution)/shard_map/all_gather | solution.py:121
  295.1 11.2 %multiply_convert_fusion.1 = (bf16[4,128,2816]{2,1,0:T(8,128)(2,1)S(1)}, bf16[4,128,2816]{2,1,0:T(8,128)(2,1)}, bf16[4,128,2816]{2,1,0:T(8,128)(2,1)S(1)}) fusion(f32[4,128,2816]{2,1,0:T(8,128)} %fusion.10, f32[4,128,2816]{2,1,0:T(8,128)} %fusion.14, bf16[4,128,1024]{2,1,0:T(8,128)(2,1)} %param.13, bf16[2816,1024]{1,0:T(8,128)(2,1)} %all-gather.23.cloned.1.call-done), kind=kOutput, calls=%fused_computation.22 | convolution fusion | flops 2961440768 | bytes 27000832 | tf_op jit(solution)/shard_map/ste,de->std/dot_general | solution.py:35
  342.2 21.3 %all-to-all-done.4 = bf16[4,128,1024]{1,0,2:T(4,128)(2,1)} async-done(((bf16[4,128,1024]{1,0,2:T(4,128)(2,1)}), bf16[4,128,1024]{1,0,2:T(4,128)(2,1)}, u32[]{:S(2)}, u32[]{:S(2)}) %all-to-all-start.4) | async-done | bytes 1048608 | tf_op jit(solution)/shard_map/all_to_all | solution.py:184
  372.6 9.7 fusion.3
  389.3 15.8 %fusion.2 = f32[4,2,512,256]{3,2,1,0:T(8,128)} fusion(f32[4,2,512,512]{3,2,1,0:T(8,128)S(1)} %fusion.75, f32[4,512,512]{2,1,0:T(8,128)S(1)} %copy-done.1, f32[2,512,512]{2,1,0:T(8,128)S(1)} %exponential_select_fusion, f32[4,512,2,128]{3,1,2,0:T(8,128)S(1)} %copy-done.7, f32[4,512,2,128]{3,1,2,0:T(8,128)S(1)} %copy-done.9), kind=kOutput, calls=%fused_computation.4 | convolution fusion | flops 6447693824 | bytes 23068672 | tf_op jit(solution)/shard_map/transpose(jvp())/while/body/eval_jaxpr/shie,shje->shij/dot_general | solution.py:83
  413.6 28.7 %all_to_all.97 = bf16[4,512,256]{2,0,1:T(4,128)(2,1)S(1)} all-to-all(bf16[4,512,256]{2,0,1:T(4,128)(2,1)} %copy.216), channel_id=1, replica_groups=mesh['rows'=8,'heads'=4] {'heads'}, dimensions={1} | all-to-all | bytes 2097152 | tf_op jit(solution)/shard_map/all_to_all | solution.py:187
  454.1 28.5 %all_to_all.98 = bf16[4,512,256]{2,0,1:T(4,128)(2,1)S(1)} all-to-all(bf16[4,512,256]{2,0,1:T(4,128)(2,1)} %copy.225), channel_id=1, replica_groups=mesh['rows'=8,'heads'=4] {'heads'}, dimensions={1} | all-to-all | bytes 2097152 | tf_op jit(solution)/shard_map/all_to_all | solution.py:190
  498.1 10.0 add_convert_fusion
  509.7 27.7 %all_to_all.99 = bf16[4,512,256]{2,0,1:T(4,128)(2,1)S(1)} all-to-all(bf16[4,512,256]{2,0,1:T(4,128)(2,1)S(1)} %copy.228), channel_id=1, replica_groups=mesh['rows'=8,'heads'=4] {'heads'}, dimensions={1} | all-to-all | bytes 2097152 | tf_op jit(solution)/shard_map/all_to_all | solution.py:193
  571.7 37.0 %reduce-scatter.29.cloned.1.call-done = f32[128,1024]{1,0:T(8,128)} async-done(((f32[1024,1024]{1,0:T(8,128)}), f32[128,1024]{1,0:T(8,128)}) %reduce-scatter.29.cloned.1.call-update) | async-done | bytes 524304 | tf_op jit(solution)/shard_map/reduce_scatter | solution.py:213
  608.7 90.5 %reduce-scatter.41.cloned.1.call-done = f32[128,2816]{1,0:T(8,128)} async-done(((f32[1024,2816]{1,0:T(8,128)}), f32[128,2816]{1,0:T(8,128)}) %reduce-scatter.41.cloned.1.call-update) | async-done | bytes 1441808 | tf_op jit(solution)/shard_map/reduce_scatter | solution.py:216
  702.2 87.6 %reduce-scatter.43.cloned.1.call-done = f32[128,2816]{1,0:T(8,128)} async-done(((f32[1024,2816]{1,0:T(8,128)}), f32[128,2816]{1,0:T(8,128)}) %reduce-scatter.43.cloned.1.call-update) | async-done | bytes 1441808 | tf_op jit(solution)/shard_map/reduce_scatter | solution.py:217
  797.7 82.6 %reduce-scatter.45.cloned.1.call-done = f32[352,1024]{1,0:T(8,128)} async-done(((f32[2816,1024]{1,0:T(8,128)}), f32[352,1024]{1,0:T(8,128)}) %reduce-scatter.45.cloned.1.call-update) | async-done | bytes 1441808 | tf_op jit(solution)/shard_map/reduce_scatter | solution.py:218
  896.1 8.7 reduce-scatter.39.cloned.1.call-done
  904.8 22.6 %reduce-scatter.35.cloned.1.call-done = f32[128,256]{1,0:T(8,128)} async-done(((f32[128,1024]{1,0:T(8,128)}), f32[128,256]{1,0:T(8,128)}) %reduce-scatter.35.cloned.1.call-update) | async-done | bytes 131088 | tf_op jit(solution)/shard_map/reduce_scatter | solution.py:224
  927.4 22.9 %reduce-scatter.23.cloned.1.call-done = f32[128,256]{1,0:T(8,128)} async-done(((f32[128,1024]{1,0:T(8,128)}), f32[128,256]{1,0:T(8,128)}) %reduce-scatter.23.cloned.1.call-update) | async-done | bytes 131088 | tf_op jit(solution)/shard_map/reduce_scatter | solution.py:221
  950.3 22.7 %reduce-scatter.27.cloned.1.call-done = f32[128,256]{1,0:T(8,128)} async-done(((f32[128,1024]{1,0:T(8,128)}), f32[128,256]{1,0:T(8,128)}) %reduce-scatter.27.cloned.1.call-update) | async-done | bytes 131088 | tf_op jit(solution)/shard_map/reduce_scatter | solution.py:222
  973.0 22.9 %reduce-scatter.31.cloned.1.call-done = f32[128,256]{1,0:T(8,128)} async-done(((f32[128,1024]{1,0:T(8,128)}), f32[128,256]{1,0:T(8,128)}) %reduce-scatter.31.cloned.1.call-update) | async-done | bytes 131088 | tf_op jit(solution)/shard_map/reduce_scatter | solution.py:223
  995.9 34.6 %reduce-scatter.49.cloned.1.call-done = f32[704,128]{1,0:T(8,128)} async-done(((f32[2816,128]{1,0:T(8,128)}), f32[704,128]{1,0:T(8,128)}) %reduce-scatter.49.cloned.1.call-update) | async-done | bytes 360464
  1030.5 35.2 %reduce-scatter.51.cloned.1.call-done = f32[704,128]{1,0:T(8,128)} async-done(((f32[2816,128]{1,0:T(8,128)}), f32[704,128]{1,0:T(8,128)}) %reduce-scatter.51.cloned.1.call-update) | async-done | bytes 360464
  1065.7 35.0 %reduce-scatter.47.cloned.1.call-done = f32[352,256]{1,0:T(8,128)} async-done(((f32[352,1024]{1,0:T(8,128)}), f32[352,256]{1,0:T(8,128)}) %reduce-scatter.47.cloned.1.call-update) | async-done | bytes 360464 | tf_op jit(solution)/shard_map/reduce_scatter | solution.py:228
  (244 shorter events, 233.9 us)
Async XLA Ops:
  7.2 33.4 %all-gather.9.cloned.1.call-start = ((), (), s32[]{:S(2)}) async-start(), calls=%async_computation.24 | async-start | bytes 2359296 | tf_op jit(solution)/shard_map/all_gather | solution.py:114
  7.9 62.4 %all-gather.11.cloned.1.call-start = ((), (), s32[]{:S(2)}) async-start(), calls=%async_computation.25 | async-start | bytes 2359296 | tf_op jit(solution)/shard_map/all_gather | solution.py:115
  8.7 91.5 %all-gather.13.cloned.1.call-start = ((), (), s32[]{:S(2)}) async-start(), calls=%async_computation.26 | async-start | bytes 2359296 | tf_op jit(solution)/shard_map/all_gather | solution.py:116
  9.4 201.2 %all-gather.15.cloned.1.call-start = ((), (), s32[]{:S(2)}) async-start(), calls=%async_computation.27 | async-start | bytes 2359296 | tf_op jit(solution)/shard_map/all_gather | solution.py:117
  10.0 206.3 %all-gather.17.cloned.1.call-start = ((), (), s32[]{:S(2)}) async-start(), calls=%async_computation.28 | async-start | bytes 2359296 | tf_op jit(solution)/shard_map/all_gather | solution.py:118
  10.6 211.8 %all-gather.21.cloned.1.call-start = ((), (), s32[]{:S(2)}) async-start(), calls=%async_computation.30 | async-start | bytes 6488064 | tf_op jit(solution)/shard_map/all_gather | solution.py:120
  11.1 238.7 %all-gather.19.cloned.1.call-start = ((), (), s32[]{:S(2)}) async-start(), calls=%async_computation.29 | async-start | bytes 6488064 | tf_op jit(solution)/shard_map/all_gather | solution.py:119
  46.3 30.8 %all-to-all-start = ((bf16[4,128,1024]{1,0,2:T(4,128)(2,1)}), bf16[4,128,1024]{1,0,2:T(4,128)(2,1)S(1)}, u32[]{:S(2)}, u32[]{:S(2)}) async-start(bf16[4,128,1024]{1,0,2:T(4,128)(2,1)} %copy.192), calls=%async_computation | async-start | bytes 2097152 | tf_op jit(solution)/shard_map/all_to_all | solution.py:135
  77.1 29.9 %all-to-all-start.1 = ((bf16[4,128,1024]{1,0,2:T(4,128)(2,1)}), bf16[4,128,1024]{1,0,2:T(4,128)(2,1)S(1)}, u32[]{:S(2)}, u32[]{:S(2)}) async-start(bf16[4,128,1024]{1,0,2:T(4,128)(2,1)} %copy.196), calls=%async_computation.1 | async-start | bytes 2097152 | tf_op jit(solution)/shard_map/all_to_all | solution.py:136
  80.7 214.3 %all-gather.23.cloned.1.call-start = ((), (), s32[]{:S(2)}) async-start(), calls=%async_computation.31 | async-start | bytes 6488064 | tf_op jit(solution)/shard_map/all_gather | solution.py:121
  106.9 30.4 %all-to-all-start.2 = ((bf16[4,128,1024]{1,0,2:T(4,128)(2,1)}), bf16[4,128,1024]{1,0,2:T(4,128)(2,1)}, u32[]{:S(2)}, u32[]{:S(2)}) async-start(bf16[4,128,1024]{1,0,2:T(4,128)(2,1)} %copy.201), calls=%async_computation.2 | async-start | bytes 2097152 | tf_op jit(solution)/shard_map/all_to_all | solution.py:137
  111.2 458.1 %reduce-scatter.37.cloned.1.call-start = ((), (), s32[]{:S(2)}) async-start(), calls=%async_computation.40 | async-start | bytes 4718592 | tf_op jit(solution)/shard_map/reduce_scatter | solution.py:215
  148.5 9.5 copy-start
  332.6 30.9 %all-to-all-start.4 = ((bf16[4,128,1024]{1,0,2:T(4,128)(2,1)}), bf16[4,128,1024]{1,0,2:T(4,128)(2,1)}, u32[]{:S(2)}, u32[]{:S(2)}) async-start(bf16[4,128,1024]{1,0,2:T(4,128)(2,1)} %copy.206), calls=%async_computation.4 | async-start | bytes 2097152 | tf_op jit(solution)/shard_map/all_to_all | solution.py:184
  337.2 232.6 %reduce-scatter.33.cloned.1.call-start = ((), (), s32[]{:S(2)}) async-start(), calls=%async_computation.38 | async-start | bytes 4718592 | tf_op jit(solution)/shard_map/reduce_scatter | solution.py:214
  342.1 228.3 %reduce-scatter.21.cloned.1.call-start = ((), (), s32[]{:S(2)}) async-start(), calls=%async_computation.32 | async-start | bytes 4718592 | tf_op jit(solution)/shard_map/reduce_scatter | solution.py:211
  372.6 9.7 copy-start.10
  449.4 121.7 %reduce-scatter.25.cloned.1.call-start = ((), (), s32[]{:S(2)}) async-start(), calls=%async_computation.34 | async-start | bytes 4718592 | tf_op jit(solution)/shard_map/reduce_scatter | solution.py:212
  489.6 8.4 copy-start.11
  489.6 119.0 %reduce-scatter.29.cloned.1.call-start = ((), (), s32[]{:S(2)}) async-start(), calls=%async_computation.36 | async-start | bytes 4718592 | tf_op jit(solution)/shard_map/reduce_scatter | solution.py:213
  542.4 156.9 %reduce-scatter.41.cloned.1.call-start = ((), (), s32[]{:S(2)}) async-start(), calls=%async_computation.42 | async-start | bytes 12976128 | tf_op jit(solution)/shard_map/reduce_scatter | solution.py:216
  551.7 238.1 %reduce-scatter.43.cloned.1.call-start = ((), (), s32[]{:S(2)}) async-start(), calls=%async_computation.43 | async-start | bytes 12976128 | tf_op jit(solution)/shard_map/reduce_scatter | solution.py:217
  559.5 320.8 %reduce-scatter.45.cloned.1.call-start = ((), (), s32[]{:S(2)}) async-start(), calls=%async_computation.44 | async-start | bytes 12976128 | tf_op jit(solution)/shard_map/reduce_scatter | solution.py:218
  569.1 335.6 %reduce-scatter.39.cloned.1.call-start = ((), (), s32[]{:S(2)}) async-start(), calls=%async_computation.41 | async-start | bytes 655360 | tf_op jit(solution)/shard_map/reduce_scatter | solution.py:225
  569.7 357.6 %reduce-scatter.35.cloned.1.call-start = ((), (), s32[]{:S(2)}) async-start(), calls=%async_computation.39 | async-start | bytes 655360 | tf_op jit(solution)/shard_map/reduce_scatter | solution.py:224
  570.3 380.0 %reduce-scatter.23.cloned.1.call-start = ((), (), s32[]{:S(2)}) async-start(), calls=%async_computation.33 | async-start | bytes 655360 | tf_op jit(solution)/shard_map/reduce_scatter | solution.py:221
  571.1 401.9 %reduce-scatter.27.cloned.1.call-start = ((), (), s32[]{:S(2)}) async-start(), calls=%async_computation.35 | async-start | bytes 655360 | tf_op jit(solution)/shard_map/reduce_scatter | solution.py:222
  571.7 424.3 %reduce-scatter.31.cloned.1.call-start = ((), (), s32[]{:S(2)}) async-start(), calls=%async_computation.37 | async-start | bytes 655360 | tf_op jit(solution)/shard_map/reduce_scatter | solution.py:223
  608.7 421.8 %reduce-scatter.49.cloned.1.call-start = ((), (), s32[]{:S(2)}) async-start(), calls=%async_computation.46 | async-start | bytes 1802240
  702.2 363.5 %reduce-scatter.51.cloned.1.call-start = ((), (), s32[]{:S(2)}) async-start(), calls=%async_computation.47 | async-start | bytes 1802240
  792.7 87.6 %copy-start.18 = (f32[4,128,1024]{2,1,0:T(8,128)S(1)}, f32[4,128,1024]{2,1,0:T(8,128)}, u32[]{:S(2)}) copy-start(f32[4,128,1024]{2,1,0:T(8,128)} %copy-done.16) | copy-start | bytes 6291460
  792.7 308.0 %reduce-scatter.47.cloned.1.call-start = ((), (), s32[]{:S(2)}) async-start(), calls=%async_computation.45 | async-start | bytes 1802240 | tf_op jit(solution)/shard_map/reduce_scatter | solution.py:228
  (43 other events, 151.1 us)
Sparse Core Ops, SparseCore 0:
  9.9 30.5 all-gather.8
  42.4 27.8 all-gather.10
  72.2 27.8 all-gather.12
  101.9 27.8 all-gather.14
  131.6 27.8 all-gather.16
  161.2 43.3 all-gather.20
  206.5 43.3 all-gather.18
  251.7 43.3 all-gather.22
  322.7 51.3 reduce-scatter.36
  377.7 51.3 reduce-scatter.32
  449.5 49.4 reduce-scatter.20
  502.6 51.3 reduce-scatter.24
  557.3 51.3 reduce-scatter.28
  612.4 86.7 reduce-scatter.40
  703.0 86.7 reduce-scatter.42
  793.5 86.7 reduce-scatter.44
  883.1 21.6 reduce-scatter.38
  907.6 19.7 reduce-scatter.34
  930.3 19.9 reduce-scatter.22
  953.1 19.8 reduce-scatter.26
  976.0 19.9 reduce-scatter.30
  998.9 31.5 reduce-scatter.48
  1033.5 32.1 reduce-scatter.50
  1068.5 32.1 reduce-scatter.46
where the time goes:
time: 1110 us
  waiting for transfers between devices  661 us (60%)
  matrix products  211 us (19%)
  blocking collectives  114 us (10%)
  local copies, waits for them, and re-layouts  65.4 us (6%)
  other arithmetic  22.8 us (2%)
  starting transfers between devices  18.4 us (2%)
  between operations  15.3 us (1%)
    reduce_scatter x1, waiting for transfers between devices, on_device(): lax.psum_scatter(g_left, 'rows', scatter_dimension=0, tiled=True)  90.5 us
    reduce_scatter x1, waiting for transfers between devices, on_device(): lax.psum_scatter(g_right, 'rows', scatter_dimension=0, tiled=True)  87.6 us
    reduce_scatter x1, waiting for transfers between devices, on_device(): lax.psum_scatter(g_down, 'rows', scatter_dimension=0, tiled=True)  82.6 us
    unnamed x26, waiting for transfers between devices  77.2 us
    dot_general x8, matrix products, project(): return jnp.einsum('std,de->ste', a, w, preferred_element_type=jnp.float32)  47 us
    dot_general x8, matrix products, weight_grad(): return jnp.einsum('std,ste->de', a, g, preferred_element_type=jnp.float32)  42.3 us
    reduce_scatter x1, waiting for transfers between devices, on_device(): lax.psum_scatter(g_value, 'rows', scatter_dimension=0, tiled=True)  37 us
    all_gather x1, waiting for transfers between devices, on_device(): lax.all_gather(shards[7], 'rows', axis=0, tiled=True)  36.6 us
  transfers between devices with their start and end apart: 28, of which 21 were waited for; matrix products, arithmetic and copies ran while one was open for 23% of the time, Pallas kernels for 0%

commit v1 on v0

v1 whole, which is shorter than its diff:
```python
import functools
import math
import types

import jax
import jax.numpy as jnp
from jax import lax
from jax.experimental import pallas as pl
from jax.experimental.pallas import tpu as pltpu
from jax.sharding import PartitionSpec as P

HEADS = 8
HEAD_DIM = 128
EPS = 1e-06
F32 = jnp.float32
BF16 = jnp.bfloat16
VMEM_LIMIT = 48 << 20

BITS = (0, 2, 4, 6, 1, 3, 5, 7)
BITS_X = (0, 4, 2, 6, 1, 5, 3, 7)
BITS_Y = (0, 2, 4, 6, 1, 3, 5, 7)


def after(value, *others):
    return lax.optimization_barrier((value,) + others)[0]


def dot(a, b, dims, out=F32):
    return lax.dot_general(a, b, (dims, ((), ())), preferred_element_type=F32).astype(out)


NN = ((1,), (0,))
NT = ((1,), (1,))
TN = ((0,), (0,))


def swap(value, bit, size):
    return lax.ppermute(value, "rows", [(i, i ^ bit) for i in range(size)])


def place_body(rows, splits, order, *refs):
    pieces, outs, sems = refs[:10], refs[10 : 10 + len(splits)], refs[-1]
    half = sum(w for _, _, w in splits) // 2
    copies = []
    for i, (at, to, width) in enumerate(splits):
        for k in range(8):
            core, chip = k // 4, k % 4
            source = pieces[5 * core + chip]
            begin = at
            if chip == 3 and at >= half:
                source, begin = pieces[5 * core + 4], at - half
            copies.append(
                pltpu.make_async_copy(
                    source.at[:, begin : begin + width],
                    outs[i].at[at_block(order, BITS[k], rows), to : to + width],
                    sems.at[i, k],
                )
            )
    for copy in copies:
        copy.start()
    for copy in copies:
        copy.wait()


def pack_body(splits, order, *refs):
    count = len(splits)
    ins, out, sems = refs[:count], refs[count], refs[-1]
    copies = [
        pltpu.make_async_copy(
            ins[i].at[:, to : to + width], out.at[:, at : at + width], sems.at[i]
        )
        for i, (at, to, width) in enumerate(splits)
    ]
    for copy in copies:
        copy.start()
    for copy in copies:
        copy.wait()


def whole_spec(rows, width):
    return pl.BlockSpec((rows, width), lambda i, *_: (0, 0))


ANYWHERE = pl.BlockSpec(memory_space=pltpu.HBM)


def pack(splits, arrays, order):
    rows = arrays[0].shape[0]
    width = sum(w for _, _, w in splits)
    (out,) = call(
        functools.partial(pack_body, splits), (1,), order, [(a, ANYWHERE) for a in arrays],
        [((rows, width), BF16, whole_spec(rows, width))],
        scratch=[pltpu.SemaphoreType.DMA((len(splits),))],
    )
    return out


class Clock:
    def __init__(self, start):
        self.token = start

    def tick(self, *places):
        held = [getattr(o, n) for o, n in places]
        held, self.token = lax.optimization_barrier((held, self.token))
        for (o, n), value in zip(places, held):
            setattr(o, n, value)


class Gather:
    def __init__(self, piece, splits, owners, widths):
        self.piece, self.splits, self.owners, self.widths = piece, splits, owners, widths

    def first(self):
        self.near = [swap(self.piece, 2, 8), swap(self.piece, 4, 8)]

    def second(self):
        half = self.piece.shape[1] // 2
        self.far = [swap(self.near[0][:, :half], 4, 8), swap(self.near[1][:, half:], 2, 8)]

    def cross_first(self):
        self.other = [swap(p, 1, 8) for p in [self.piece] + self.near]

    def cross_second(self):
        self.other_far = [swap(p, 1, 8) for p in self.far]

    def whole(self, order):
        rows, splits, owners = self.piece.shape[0], self.splits, self.owners
        pieces = [self.piece] + self.near + self.far + self.other + self.other_far
        count = len(self.widths)

        def body(order, *refs):
            outs = refs[10 : 10 + count]
            place_body(rows, splits, order, *refs[:10], *[outs[o] for o in owners], refs[-1])

        return call(
            body, (1,), order, [(p, ANYWHERE) for p in pieces],
            [((8 * rows, w), BF16, whole_spec(8 * rows, w)) for w in self.widths],
            scratch=[pltpu.SemaphoreType.DMA((len(splits), 8))],
        )


def add(one, two, out=BF16):
    return (one.astype(F32) + two.astype(F32)).astype(out)


class Reduce:
    def __init__(self, sends, keeps, bits):
        self.sends, self.keeps, self.bits = list(sends), list(keeps), list(bits)

    def core(self):
        self.theirs = [swap(s, 1, 8) for s in self.sends]

    def join(self):
        self.totals = [k(t) for k, t in zip(self.keeps, self.theirs)]

    def first(self):
        self.got = [swap(t[t.shape[0] // 2 :], b, 8) for t, b in zip(self.totals, self.bits)]

    def join_first(self):
        self.parts = [add(t[: t.shape[0] // 2], g) for t, g in zip(self.totals, self.got)]

    def second(self):
        self.got_last = [swap(p[p.shape[0] // 2 :], 6 - b, 8) for p, b in zip(self.parts, self.bits)]

    def join_second(self):
        self.sums = [
            add(p[: p.shape[0] // 2], g, F32) for p, g in zip(self.parts, self.got_last)
        ]


def column_block(s, here, bit):
    width = s.shape[1] // 4
    return lax.dynamic_slice_in_dim(s, (here ^ bit) * width, width, axis=1)


class Settle:
    def __init__(self, sums, here):
        self.widths = [s.shape[1] // 4 for s in sums]
        self.own = [column_block(s, here, 0) for s in sums]
        self.far = [column_block(s, here, 2) for s in sums]
        near = [column_block(s, here, 1) for s in sums] + [column_block(s, here, 3) for s in sums]
        self.out = jnp.concatenate([n.astype(BF16) for n in near], axis=1)

    def pass_on(self, bit):
        self.got = lax.ppermute(self.out, "heads", [(i, i ^ bit) for i in range(4)])

    def split(self, at=0):
        pieces = []
        for w in self.widths:
            pieces.append(self.got[:, at : at + w].astype(F32))
            at += w
        return pieces

    def join(self):
        self.own = [o + g for o, g in zip(self.own, self.split())]
        far = [o + g for o, g in zip(self.far, self.split(sum(self.widths)))]
        self.out = jnp.concatenate([f.astype(BF16) for f in far], axis=1)

    def result(self):
        return [o + g for o, g in zip(self.own, self.split())]


def at_block(order_ref, index, width):
    return pl.ds(pl.multiple_of(order_ref[index] * width, width), width)


def sigmoid(v):
    return 1.0 / (1.0 + jnp.exp(-v))


def swish_slope(v):
    sig = sigmoid(v)
    return sig * (1.0 + v * (1.0 - sig))


def call(body, grid, order, ins, outs, scratch=(), flops=0):
    moved = sum(a.size * a.dtype.itemsize for a, _ in ins) + sum(
        math.prod(s) * jnp.dtype(t).itemsize for s, t, _ in outs
    )
    return pl.pallas_call(
        body,
        grid_spec=pltpu.PrefetchScalarGridSpec(
            num_scalar_prefetch=1,
            grid=grid,
            in_specs=[spec for _, spec in ins],
            out_specs=[spec for _, _, spec in outs],
            scratch_shapes=list(scratch),
        ),
        out_shape=[jax.ShapeDtypeStruct(s, t) for s, t, _ in outs],
        compiler_params=pltpu.CompilerParams(vmem_limit_bytes=VMEM_LIMIT),
        cost_estimate=pl.CostEstimate(flops=0, bytes_accessed=0, transcendentals=0),
    )(order, *[a for a, _ in ins])


def rows_spec(count, width, column=0):
    return pl.BlockSpec((count, width), lambda i, *_: (i, column))


def spread(order, blocks, h, outs):
    outs[0][...] = h
    width = h.shape[1] // blocks
    for out, bits in zip(outs[1:], (BITS_X, BITS_Y)):
        for k in range(blocks):
            source = at_block(order, bits[k], width)
            out[:, k * width : (k + 1) * width] = outs[0][:, source]


def norm_body(blocks, order, x_ref, *outs):
    x = x_ref[...].astype(F32)
    scale = lax.rsqrt(jnp.mean(x * x, axis=-1, keepdims=True) + EPS)
    spread(order, blocks, (x * scale).astype(BF16), outs)


def mid_body(blocks, order, x_ref, b_ref, mid_ref, *outs):
    mid = x_ref[...].astype(F32) + b_ref[...]
    mid_ref[...] = mid
    scale = lax.rsqrt(jnp.mean(mid * mid, axis=-1, keepdims=True) + EPS)
    spread(order, blocks, (mid * scale).astype(BF16), outs)


def norm_back_body(order, v_ref, base_ref, g_ref, *outs):
    v = v_ref[...].astype(F32)
    g = g_ref[...]
    scale = lax.rsqrt(jnp.mean(v * v, axis=-1, keepdims=True) + EPS)
    inner = jnp.mean(g * v, axis=-1, keepdims=True) * (scale * scale * scale)
    total = base_ref[...].astype(F32) + scale * g - v * inner
    outs[0][...] = total
    if len(outs) > 1:
        outs[1][...] = total.astype(BF16)


def ramp(rows, start, sign, slope):
    place = lax.broadcasted_iota(jnp.int32, (rows, HEAD_DIM), 0).astype(F32)
    return jnp.exp(-slope * (start + sign * place))


def decays(ids_col, ids_row, slope):
    rows = ids_col.shape[0]
    gap = (
        lax.broadcasted_iota(jnp.int32, (rows, rows), 0)
        - lax.broadcasted_iota(jnp.int32, (rows, rows), 1)
    ).astype(F32)
    keep = (gap >= 0.0) & (ids_col == ids_row)
    return jnp.where(keep, jnp.exp(-slope * jnp.maximum(gap, 0.0)), 0.0)


def slope_of(head):
    return 2.0 ** (-8.0 * (head + 1) / HEADS)


def columns(head):
    return slice(head * HEAD_DIM, (head + 1) * HEAD_DIM)


def turned(a, cos, sin):
    return jnp.concatenate([a * cos, a * sin], axis=1)


def rounded_swish(v):
    return (v * sigmoid(v)).astype(BF16).astype(F32)


def fresh_body(order, k_ref, v_ref, cos_ref, sin_ref, tail_ref, state_ref):
    rows = k_ref.shape[1]
    cos, sin = cos_ref[...], sin_ref[...]
    tail = tail_ref[0]
    for head in range(HEADS):
        key = rounded_swish(k_ref[0, :, columns(head)])
        key = key * (ramp(rows, rows - 1.0, -1.0, slope_of(head)) * tail)
        value = v_ref[0, :, columns(head)].astype(BF16)
        state_ref[0, head] = dot(turned(key, cos, sin).astype(BF16), value, TN, BF16)


def mix_body(
    order, q_ref, k_ref, v_ref, u_ref, cos_ref, sin_ref, col_ref, row_ref, link_ref, s_ref,
    mix_ref, gated_ref, *ordered_refs,
):
    rows = q_ref.shape[1]
    cos, sin = cos_ref[...], sin_ref[...]
    ids_col, ids_row = col_ref[0], row_ref[0]
    link = link_ref[0]
    power = jnp.zeros((rows, 1), F32)
    for head in range(HEADS):
        cols = columns(head)
        slope = slope_of(head)
        rq = turned(rounded_swish(q_ref[0, :, cols]), cos, sin).astype(BF16)
        rk = turned(rounded_swish(k_ref[0, :, cols]), cos, sin).astype(BF16)
        value = v_ref[0, :, cols].astype(BF16)
        weights = (dot(rq, rk, NT) * decays(ids_col, ids_row, slope)).astype(BF16)
        mixed = dot(weights, value, NN) + dot(rq, s_ref[0, head], NN) * (
            ramp(rows, 1.0, 1.0, slope) * link
        )
        mixed = mixed.astype(BF16)
        mix_ref[0, :, cols] = mixed
        mixed = mixed.astype(F32)
        power += jnp.sum(mixed * mixed, axis=-1, keepdims=True)
    scale = lax.rsqrt(power / (HEADS * HEAD_DIM) + EPS)
    for head in range(HEADS):
        cols = columns(head)
        u = u_ref[0, :, cols]
        gated_ref[0, :, cols] = (
            mix_ref[0, :, cols].astype(F32) * scale * (u * sigmoid(u))
        ).astype(BF16)
    for out in ordered_refs:
        for k in range(HEADS):
            out[0, :, columns(k)] = gated_ref[0, :, at_block(order, BITS_X[k], HEAD_DIM)]


def gate_back_body(
    order, q_ref, u_ref, mix_ref, dg_ref, cos_ref, sin_ref, link_ref, du_ref, dm_ref, state_ref
):
    rows = q_ref.shape[1]
    cos, sin = cos_ref[...], sin_ref[...]
    link = link_ref[0]
    mix = mix_ref[0].astype(F32)
    scale = lax.rsqrt(jnp.mean(mix * mix, axis=-1, keepdims=True) + EPS)
    inner = jnp.zeros((rows, 1), F32)
    for head in range(HEADS):
        cols = columns(head)
        u = u_ref[0, :, cols]
        part = mix_ref[0, :, cols].astype(F32)
        dg = dg_ref[0, :, cols]
        sig = sigmoid(u)
        inner += jnp.sum(dg * (u * sig) * part, axis=-1, keepdims=True)
        du_ref[0, :, cols] = (dg * part * scale * (sig * (1.0 + u * (1.0 - sig)))).astype(BF16)
    inner = inner * (scale * scale * scale) / (HEADS * HEAD_DIM)
    for head in range(HEADS):
        cols = columns(head)
        u = u_ref[0, :, cols]
        part = mix_ref[0, :, cols].astype(F32)
        dg = dg_ref[0, :, cols]
        d_mix = (scale * (dg * (u * sigmoid(u))) - part * inner).astype(BF16)
        dm_ref[0, :, cols] = d_mix
        query = rounded_swish(q_ref[0, :, cols]) * (
            ramp(rows, 1.0, 1.0, slope_of(head)) * link
        )
        state_ref[0, head] = dot(turned(query, cos, sin).astype(BF16), d_mix, TN, BF16)


def mix_back_body(
    order, q_ref, k_ref, v_ref, dm_ref, cos_ref, sin_ref, col_ref, row_ref, link_ref, s_ref,
    dq_ref, dk_ref, dv_ref,
):
    rows = q_ref.shape[1]
    cos, sin = cos_ref[...], sin_ref[...]
    ids_col, ids_row = col_ref[0], row_ref[0]
    link = link_ref[0]
    for head in range(HEADS):
        cols = columns(head)
        slope = slope_of(head)
        q_pre = q_ref[0, :, cols]
        rq = turned(rounded_swish(q_pre), cos, sin).astype(BF16)
        rk = turned(rounded_swish(k_ref[0, :, cols]), cos, sin).astype(BF16)
        value = v_ref[0, :, cols].astype(BF16)
        d_mix = dm_ref[0, :, cols]
        decay = decays(ids_col, ids_row, slope)
        weights = (dot(rq, rk, NT) * decay).astype(BF16)
        d_scores = (dot(d_mix, value, NT) * decay).astype(BF16)
        enter = ramp(rows, 1.0, 1.0, slope) * link
        d_rq = dot(d_scores, rk, NN) + dot(d_mix, s_ref[0, head], NT) * jnp.concatenate(
            [enter, enter], axis=1
        )
        d_query = d_rq[:, :HEAD_DIM] * cos + d_rq[:, HEAD_DIM:] * sin
        dq_ref[0, :, cols] = (
            d_query.astype(BF16).astype(F32) * swish_slope(q_pre)
        ).astype(BF16)
        d_rk = dot(d_scores, rq, TN)
        dk_ref[0, :, cols] = d_rk[:, :HEAD_DIM] * cos + d_rk[:, HEAD_DIM:] * sin
        dv_ref[0, :, cols] = dot(weights, d_mix, TN)


def state_back_body(
    order, k_ref, v_ref, dk_ref, dv_ref, cos_ref, sin_ref, tail_ref, s_ref, dko_ref, dvo_ref
):
    rows = k_ref.shape[1]
    cos, sin = cos_ref[...], sin_ref[...]
    tail = tail_ref[0]
    for head in range(HEADS):
        cols = columns(head)
        k_pre = k_ref[0, :, cols]
        leave = ramp(rows, rows - 1.0, -1.0, slope_of(head)) * tail
        key = rounded_swish(k_pre) * leave
        rk = turned(key, cos, sin).astype(BF16)
        value = v_ref[0, :, cols].astype(BF16)
        state = s_ref[0, head]
        d_rk = dot(value, state, NT) * jnp.concatenate([leave, leave], axis=1)
        d_key = dk_ref[0, :, cols] + d_rk[:, :HEAD_DIM] * cos + d_rk[:, HEAD_DIM:] * sin
        dko_ref[0, :, cols] = (d_key.astype(BF16).astype(F32) * swish_slope(k_pre)).astype(BF16)
        dvo_ref[0, :, cols] = (dv_ref[0, :, cols] + dot(rk, state, NN)).astype(BF16)


class Chain:
    def __init__(self, fresh, factor, forward, parts):
        self.fresh, self.factor, self.forward, self.parts = fresh, factor, forward, parts
        self.seqs = fresh.shape[0]
        self.now = [fresh[s] for s in range(self.seqs)]
        self.got = [[] for _ in range(self.seqs)]
        self.turns = self.seqs + parts - 2

    def pass_on(self, s, hop):
        pair = (hop - 1, hop) if self.forward else (self.parts - hop, self.parts - hop - 1)
        self.got[s].append(lax.ppermute(self.now[s], "heads", [pair]))

    def begin(self):
        for s in range(self.seqs):
            self.pass_on(s, 1)

    def at(self, turn):
        return [(s, turn - s) for s in range(self.seqs) if 1 <= turn - s < self.parts]

    def arrivals(self, turn):
        self.new = [self.got[s][hop - 1] for s, hop in self.at(turn)]
        return self, "new"

    def go_on(self, turn):
        for (s, hop), new in zip(self.at(turn), self.new):
            self.got[s][hop - 1] = new
            if hop + 1 < self.parts:
                arrived = new.astype(F32) * self.factor[s][:, None, None]
                self.now[s] = (self.fresh[s].astype(F32) + arrived).astype(BF16)
                self.pass_on(s, hop + 1)

    def result(self):
        return jnp.stack([functools.reduce(lambda a, b: a + b, g) for g in self.got])


class Layer:
    def __init__(self, tokens, doc_lengths, cotangent, by_hand):
        seqs, length, width = tokens.shape
        self.seqs, self.length, self.width, self.count = seqs, length, width, seqs * length
        self.by_hand = by_hand
        self.here = lax.axis_index("rows")
        self.place = lax.axis_index("heads")
        self.order = jnp.stack([self.here ^ b for b in range(8)]).astype(jnp.int32)
        self.x = tokens.reshape(self.count, width)
        self.dy = cotangent.reshape(self.count, width)

        ends = jnp.cumsum(doc_lengths, axis=-1, dtype=jnp.int32)[:, :-1]

        def ids_at(where):
            return jnp.sum((where[None, :, None] >= ends[:, None, :]).astype(jnp.int32), axis=-1)

        start = self.place * length
        positions = start + jnp.arange(length, dtype=jnp.int32)
        ids = ids_at(positions)
        before = jnp.where(self.place > 0, ids_at(jnp.reshape(start - 1, (1,))), -1)
        final = ids[:, -1:]
        link = (ids == before).astype(F32)[:, :, None]
        tail = (ids == final).astype(F32)[:, :, None]
        slopes = jnp.array([slope_of(h) for h in range(HEADS)], F32)
        self.factor = (final == before).astype(F32) * jnp.exp(-slopes * length)[None, :]
        theta = jnp.exp(-math.log(10000.0) * jnp.arange(HEAD_DIM, dtype=F32) / HEAD_DIM)
        angle = positions.astype(F32)[:, None] * theta[None, :]

        table = pl.BlockSpec((length, HEAD_DIM), lambda s, *_: (0, 0))
        one_col = pl.BlockSpec((1, length, 1), lambda s, *_: (s, 0, 0))
        one_row = pl.BlockSpec((1, 1, length), lambda s, *_: (s, 0, 0))
        self.turn = [(jnp.cos(angle), table), (jnp.sin(angle), table)]
        self.link = link, one_col
        self.tail = tail, one_col
        self.masks = [(ids[:, :, None], one_col), (ids[:, None, :], one_row), self.link]
        self.seq = pl.BlockSpec((1, length, width), lambda s, *_: (s, 0, 0))
        self.state = pl.BlockSpec(
            (1, HEADS, 2 * HEAD_DIM, HEAD_DIM), lambda s, *_: (s, 0, 0, 0)
        )
        self.states = (seqs, HEADS, 2 * HEAD_DIM, HEAD_DIM), BF16, self.state
        step = min(self.count, 256)
        self.grid = (self.count // step,)
        self.wide = rows_spec(step, width)

    def rows(self, body, ins, types, order=None):
        return call(
            body, self.grid, self.order, [(a, self.wide) for a in ins],
            [((self.count, self.width), t, self.wide) for t in types],
        )

    def seqwise(self, body, ins, outs):
        shape = (self.seqs, self.length, self.width)
        ins = [i if isinstance(i, tuple) else (i.reshape(shape), self.seq) for i in ins]
        outs = [o if isinstance(o, tuple) else (shape, o, self.seq) for o in outs]
        got = call(body, (self.seqs,), self.order, ins, outs)
        return [g.reshape(self.count, self.width) if g.shape == shape else g for g in got]

    def copies(self):
        return [BF16] * (3 if self.by_hand else 1)

    def norm(self):
        blocks = 8 if self.by_hand else 1
        return self.rows(functools.partial(norm_body, blocks), [self.x], self.copies())

    def fresh(self, k_pre, v_pre):
        return self.seqwise(fresh_body, [k_pre, v_pre] + self.turn + [self.tail], [self.states])[0]

    def mix(self, q_pre, k_pre, v_pre, u_pre, state_in):
        ins = [q_pre, k_pre, v_pre, u_pre] + self.turn + self.masks + [(state_in, self.state)]
        return self.seqwise(mix_body, ins, [BF16] + self.copies())

    def mid(self, branch):
        blocks = 8 if self.by_hand else 1
        return self.rows(
            functools.partial(mid_body, blocks), [self.x, branch], [F32] + self.copies()
        )

    def mid_back(self, x_mid, grad):
        return self.rows(norm_back_body, [x_mid, self.dy, grad], [F32, BF16])

    def in_back(self, d_mid, grad):
        return self.rows(norm_back_body, [self.x, d_mid, grad], [F32])[0]

    def gate_back(self, q_pre, u_pre, mix, d_gated):
        ins = [q_pre, u_pre, mix, d_gated] + self.turn + [self.link]
        return self.seqwise(gate_back_body, ins, [BF16, BF16, self.states])

    def mix_back(self, q_pre, k_pre, v_pre, d_mix, state_in):
        ins = [q_pre, k_pre, v_pre, d_mix] + self.turn + self.masks + [(state_in, self.state)]
        return self.seqwise(mix_back_body, ins, [BF16, F32, F32])

    def state_back(self, k_pre, v_pre, dk_near, dv_near, d_state):
        ins = [k_pre, v_pre, dk_near, dv_near] + self.turn + [self.tail, (d_state, self.state)]
        return self.seqwise(state_back_body, ins, [BF16, BF16])


def plainly(layer, heads_count, weights):
    w_query, w_key, w_value, w_gate, w_out, w_left, w_right, w_down = (
        lax.all_gather(w, "rows", axis=0, tiled=True) for w in weights
    )

    def carried(fresh, forward):
        chain = Chain(fresh, layer.factor, forward, heads_count)
        chain.begin()
        for turn in range(1, chain.turns + 1):
            chain.arrivals(turn)
            chain.go_on(turn)
        return chain.result()

    def gradient(lhs, d):
        total = lax.psum_scatter(dot(lhs, d, TN, BF16), "rows", scatter_dimension=0, tiled=True)
        return lax.psum_scatter(total, "heads", scatter_dimension=1, tiled=True).astype(F32)

    (h_in,) = layer.norm()
    q_pre, k_pre, v_pre, u_pre = (
        dot(h_in, w, NN) for w in (w_query, w_key, w_value, w_gate)
    )
    state_in = carried(layer.fresh(k_pre, v_pre), True)
    mix, gated = layer.mix(q_pre, k_pre, v_pre, u_pre, state_in)
    x_mid, h_mid = layer.mid(dot(gated, w_out, NN))
    left, right = dot(h_mid, w_left, NN), dot(h_mid, w_right, NN)
    product = (left * right).astype(BF16)
    activations = (x_mid + dot(product, w_down, NN)).astype(BF16)
    grad_product = dot(layer.dy, w_down, NT)
    d_left = (grad_product * right).astype(BF16)
    d_right = (grad_product * left).astype(BF16)
    d_mid, d_branch = layer.mid_back(
        x_mid, dot(d_left, w_left, NT) + dot(d_right, w_right, NT)
    )
    d_u, d_mix, d_fresh = layer.gate_back(q_pre, u_pre, mix, dot(d_branch, w_out, NT))
    d_state = carried(d_fresh, False)
    d_q, dk_near, dv_near = layer.mix_back(q_pre, k_pre, v_pre, d_mix, state_in)
    d_k, d_v = layer.state_back(k_pre, v_pre, dk_near, dv_near, d_state)
    grad_in = (
        dot(d_q, w_query, NT) + dot(d_u, w_gate, NT) + dot(d_k, w_key, NT) + dot(d_v, w_value, NT)
    )
    input_grad = layer.in_back(d_mid, grad_in)
    pairs = (
        (h_in, d_q), (h_in, d_k), (h_in, d_v), (h_in, d_u), (gated, d_branch),
        (h_mid, d_left), (h_mid, d_right), (product, layer.dy),
    )
    return (activations, input_grad) + tuple(gradient(lhs, d) for lhs, d in pairs)


def reducing(terms):
    sends, keeps = [], []
    for lhs, d, _ in terms:
        half = lhs.shape[1] // 2
        sends.append(dot(lhs[:, half:], d, TN, BF16))

        def keep(theirs, lhs=lhs, d=d, half=half):
            return (dot(lhs[:, :half], d, TN) + theirs.astype(F32)).astype(BF16)

        keeps.append(keep)
    return Reduce(sends, keeps, [b for _, _, b in terms])


def reducing_rows(whole, here):
    rows, half = whole.shape[0] // 8, whole.shape[1] // 2

    def block(side, bits):
        cut = whole[:, side * half : (side + 1) * half]
        return jnp.concatenate(
            [lax.dynamic_slice_in_dim(cut, (here ^ b) * rows, rows, axis=0) for b in bits], axis=0
        )

    sends, keeps = [], []
    for side, bits in enumerate((BITS_X, BITS_Y)):
        sends.append(block(side, bits[4:]))

        def keep(theirs, side=side, bits=bits):
            return add(block(side, bits[:4]), theirs)

        keeps.append(keep)
    return Reduce(sends, keeps, [2, 4])


def stepwise(layer, heads_count, weights):
    w_query, w_key, w_value, w_gate, w_out, w_left, w_right, w_down = weights
    width, inner = layer.width, w_left.shape[1]
    half = width // 2
    order, here, place = layer.order, layer.here, layer.place
    v = types.SimpleNamespace()
    clock = Clock(order)
    tick = clock.tick

    pair = [(0, 0, width), (width, 0, width)]
    triple = [
        (0, 0, width), (width, 0, half), (width + half, 0, width), (2 * width + half, half, half),
    ]
    kv = Gather(pack(pair, [w_key, w_value], order), pair, (0, 1), (width, width))
    kv.first()
    v.h = layer.norm()
    v.qu = pack(triple, [w_query, w_out, w_gate, w_out], order)
    ff_pair = [(0, 0, inner), (inner, 0, inner)]
    v.ff = pack(ff_pair, [w_left, w_right], order)
    tick((kv, "near"), (v, "qu"), (v, "ff"), (v, "h"))
    kv.second()
    qu = Gather(v.qu, triple, (0, 2, 1, 2), (width, width, width))
    qu.first()
    ff = Gather(v.ff, ff_pair, (0, 1), (inner, inner))
    ff.first()
    kv.cross_first()
    tick((kv, "far"))
    kv.cross_second()
    full_k, full_v = kv.whole(order)
    h_in = v.h[0]
    k_pre, v_pre = dot(h_in, full_k, NN), dot(h_in, full_v, NN)
    v.fresh = layer.fresh(k_pre, v_pre)
    tick((v, "fresh"))
    forward = Chain(v.fresh, layer.factor, True, heads_count)
    forward.begin()

    tick(forward.arrivals(1), (qu, "near"))
    forward.go_on(1)
    qu.second()
    v.down = w_down
    down = Gather(v.down, [(0, 0, half), (half, half, half)], (0, 0), (width,))
    tick((down, "piece"))
    down.first()
    qu.cross_first()
    tick(forward.arrivals(2))
    forward.go_on(2)
    tick(forward.arrivals(3), (ff, "near"))
    forward.go_on(3)
    ff.second()
    ff.cross_first()
    tick(forward.arrivals(4), (qu, "far"))
    forward.go_on(4)
    qu.cross_second()
    full_q, full_u, full_out = qu.whole(order)
    v.q_pre, v.u_pre = dot(h_in, full_q, NN), dot(h_in, full_u, NN)
    tick(forward.arrivals(5), (down, "near"), (v, "q_pre"), (v, "u_pre"))
    forward.go_on(5)
    down.second()
    down.cross_first()
    tick(forward.arrivals(6))
    forward.go_on(6)
    state_in = forward.result()
    v.mix, *v.gated = layer.mix(v.q_pre, k_pre, v_pre, v.u_pre, state_in)
    tick((v, "mix"), (v, "gated"), (ff, "far"))
    ff.cross_second()
    branch = dot(v.gated[0], full_out, NN)
    v.x_mid, *v.h_mid = layer.mid(branch)
    full_left, full_right = ff.whole(order)
    tick((v, "x_mid"), (v, "h_mid"), (down, "far"))
    down.cross_second()

    h_mid = v.h_mid[0]
    v.left, v.right = dot(h_mid, full_left, NN), dot(h_mid, full_right, NN)
    v.product = (v.left * v.right).astype(BF16)
    tick((v, "left"), (v, "right"), (v, "product"))
    (full_down,) = down.whole(order)
    r_down = reducing_rows(dot(v.product, layer.dy, TN, BF16), here)
    tick((r_down, "sends"))
    r_down.core()
    grad_product = dot(layer.dy, full_down, NT)
    v.d_left = (grad_product * v.right).astype(BF16)
    v.d_right = (grad_product * v.left).astype(BF16)
    tick((v, "d_left"), (v, "d_right"), (r_down, "theirs"))
    r_down.join()
    tick((r_down, "totals"), (v, "d_left"), (v, "d_right"))
    r_down.first()
    v.d_mid, v.d_branch = layer.mid_back(
        v.x_mid, dot(v.d_left, full_left, NT) + dot(v.d_right, full_right, NT)
    )
    v.d_u, v.d_mix, v.d_fresh = layer.gate_back(
        v.q_pre, v.u_pre, v.mix, dot(v.d_branch, full_out, NT)
    )
    tick((v, "d_fresh"), (v, "d_u"), (v, "d_mix"), (v, "d_branch"), (v, "d_mid"), (v, "d_left"), (v, "d_right"))

    backward = Chain(v.d_fresh, layer.factor, False, heads_count)
    backward.begin()
    r_ff = reducing([(v.h_mid[1], v.d_left, 2), (v.h_mid[2], v.d_right, 4)])
    tick((r_ff, "sends"), (r_down, "got"))
    r_ff.core()
    r_down.join_first()
    tick(backward.arrivals(1), (r_down, "parts"), (v, "d_mix"))
    backward.go_on(1)
    r_down.second()
    v.d_q, v.dk_near, v.dv_near = layer.mix_back(v.q_pre, k_pre, v_pre, v.d_mix, state_in)
    tick(backward.arrivals(2), (r_ff, "theirs"), (v, "d_q"), (v, "dk_near"), (v, "dv_near"), (v, "d_u"))
    backward.go_on(2)
    r_ff.join()
    tick((r_ff, "totals"))
    r_ff.first()
    tick(backward.arrivals(3), (v, "d_branch"), (v, "d_u"))
    backward.go_on(3)
    r_out = reducing([(v.gated[1], v.d_branch, 2), (v.h[2], v.d_u, 4)])
    tick((r_out, "sends"), (r_down, "got_last"))
    r_out.core()
    r_down.join_second()
    s_down = Settle([jnp.concatenate(r_down.sums, axis=1)], place)
    tick(backward.arrivals(4), (r_out, "theirs"), (v, "d_q"))
    backward.go_on(4)
    r_out.join()
    r_query = reducing([(v.h[2], v.d_q, 4)])
    tick((r_out, "totals"), (r_query, "sends"))
    r_out.first()
    r_query.core()
    tick(backward.arrivals(5), (r_query, "theirs"), (v, "product"))
    backward.go_on(5)
    r_query.join()
    tick((r_query, "totals"))
    r_query.first()
    v.activations = (v.x_mid + dot(v.product, full_down, NN)).astype(BF16)
    tick(backward.arrivals(6), (v, "activations"), (r_ff, "got"))
    backward.go_on(6)
    d_state = backward.result()
    r_ff.join_first()
    v.d_k, v.d_v = layer.state_back(k_pre, v_pre, v.dk_near, v.dv_near, d_state)
    tick((r_ff, "parts"), (v, "d_k"), (v, "d_v"))
    r_ff.second()
    r_key = reducing([(v.h[1], v.d_k, 2), (v.h[2], v.d_v, 4)])
    tick((r_key, "sends"), (r_out, "got"))
    r_key.core()
    r_out.join_first()
    tick((r_key, "theirs"), (r_out, "parts"))
    r_out.second()
    r_key.join()
    tick((r_key, "totals"), (r_query, "got"), (v, "d_q"))
    r_key.first()
    r_query.join_first()
    tick((r_query, "parts"), (v, "d_q"), (s_down, "out"))
    r_query.second()
    s_down.pass_on(1)
    v.grad_in = (
        dot(v.d_q, full_q, NT) + dot(v.d_u, full_u, NT)
        + dot(v.d_k, full_k, NT) + dot(v.d_v, full_v, NT)
    )
    tick((v, "grad_in"), (r_ff, "got_last"), (s_down, "got"))
    r_ff.join_second()
    s_ff = Settle(r_ff.sums, place)
    s_down.join()
    tick((s_ff, "out"), (s_ff, "own"), (s_down, "out"))
    s_ff.pass_on(1)
    s_down.pass_on(2)
    v.input_grad = layer.in_back(v.d_mid, v.grad_in)
    tick((v, "input_grad"), (r_out, "got_last"), (r_query, "got_last"))
    r_out.join_second()
    r_query.join_second()
    s_out = Settle(r_out.sums + r_query.sums, place)
    tick((s_out, "out"), (r_key, "got"))
    s_out.pass_on(1)
    r_key.join_first()
    tick((r_key, "parts"), (s_ff, "got"))
    r_key.second()
    s_ff.join()
    tick((s_ff, "out"), (s_out, "got"))
    s_ff.pass_on(2)
    s_out.join()
    tick((s_out, "out"), (r_key, "got_last"))
    s_out.pass_on(2)
    r_key.join_second()
    s_key = Settle(r_key.sums, place)
    tick((s_key, "out"))
    s_key.pass_on(1)
    tick((s_key, "got"), (s_down, "got"), (s_ff, "got"))
    s_key.join()
    tick((s_key, "out"), (s_out, "got"))
    s_key.pass_on(2)
    (g_down,) = s_down.result()
    g_left, g_right = s_ff.result()
    g_out, g_gate, g_query = s_out.result()
    g_key, g_value = s_key.result()
    return (
        v.activations, v.input_grad, g_query, g_key, g_value, g_gate, g_out, g_left, g_right, g_down
    )


def on_device(rows_count, heads_count, tokens, doc_lengths, cotangent, *weights):
    by_hand = rows_count == 8 and heads_count == 4
    layer = Layer(tokens, doc_lengths, cotangent, by_hand)
    run = stepwise if by_hand else plainly
    activations, input_grad, *grads = run(layer, heads_count, weights)
    return (activations.reshape(tokens.shape), input_grad.reshape(tokens.shape), *grads)


def solution(mesh):
    sizes = dict(mesh.shape)
    tokens = P("rows", "heads", None)
    weights = P("rows", None)
    grads = P("rows", "heads")
    return jax.shard_map(
        functools.partial(on_device, sizes["rows"], sizes["heads"]),
        mesh=mesh,
        in_specs=(tokens, weights, tokens) + (weights,) * 8,
        out_specs=(tokens, tokens) + (grads,) * 8,
        check_vma=False,
    )
```

time: 1110 us -> 523 us (0.47)
  waiting for transfers between devices: 661 us -> 166 us
  matrix products: 211 us -> 85.5 us
  blocking collectives: 114 us -> 0 us
  Pallas kernels: 0 us -> 74.5 us
  starting transfers between devices: 18.4 us -> 88.1 us
  other arithmetic: 22.8 us -> 46.3 us
  local copies, waits for them, and re-layouts: 65.4 us -> 50.6 us
  between operations: 15.3 us -> 3.32 us
    reduce_scatter x14 -> x0, waiting for transfers between devices: 433 us -> none  [the longest x1 90.5 us: on_device(): lax.psum_scatter(g_left, 'rows', scatter_dimension=0, tiled=True)]
    ppermute x0 -> x95, waiting for transfers between devices: none -> 166 us  [the longest x24 71.9 us: pass_on(): self.got[s].append(lax.ppermute(self.now[s], 'heads', [pair]))]
    dot_general x34 -> x31, matrix products: 211 us -> 85.5 us  [dot(): lax.dot_general(a, b, (dims, ((), ())), preferred_element_type=F32)]
    all_gather x8 -> x0, waiting for transfers between devices: 119 us -> none  [the longest x1 36.6 us: on_device(): lax.all_gather(shards[7], 'rows', axis=0, tiled=True)]
    all_to_all x4 -> x0, blocking collectives: 114 us -> none  [the longest x1 29.2 us: on_device(): lax.all_to_all(mixed_heads.astype(jnp.bfloat16), 'heads', split_axis=1, c...]
    ppermute x0 -> x95, starting transfers between devices: none -> 88.1 us  [the longest x63 48.4 us: swap(): return lax.ppermute(value, 'rows', [(i, i ^ bit) for i in range(size)])]
    unnamed x26 -> x0, waiting for transfers between devices: 77.2 us -> none
    pallas_call x0 -> x16, Pallas kernels: none -> 74.5 us  [call(): pl.pallas_call(body, grid_spec=pltpu.PrefetchScalarGridSpec(num_scalar_pr...]
  transfers between devices with their start and end apart: 28 -> 95, of which waited for: 21 -> 28; matrix products, arithmetic and copies ran while one was open for 23% -> 28% of each run, Pallas kernels for 0% -> 12%
where the time goes in v1:
time: 523 us; the launch traced here: 514 us
  waiting for transfers between devices  166 us (32%)
  starting transfers between devices  88.1 us (17%)
  matrix products  85.5 us (16%)
  Pallas kernels  74.5 us (14%)
  local copies, waits for them, and re-layouts  50.6 us (10%)
  other arithmetic  46.3 us (9%)
    dot_general x31, matrix products, dot(): lax.dot_general(a, b, (dims, ((), ())), preferred_element_type=F32)  85.5 us
    pallas_call x16, Pallas kernels, call(): pl.pallas_call(body, grid_spec=pltpu.PrefetchScalarGridSpec(num_scalar_pr...  74.5 us
    ppermute x24, waiting for transfers between devices, pass_on(): self.got[s].append(lax.ppermute(self.now[s], 'heads', [pair]))  71.9 us
    ppermute x63, waiting for transfers between devices, swap(): return lax.ppermute(value, 'rows', [(i, i ^ bit) for i in range(size)])  57.9 us
    ppermute x63, starting transfers between devices, swap(): return lax.ppermute(value, 'rows', [(i, i ^ bit) for i in range(size)])  48.4 us
    ppermute x8, waiting for transfers between devices, pass_on(): self.got = lax.ppermute(self.out, 'heads', [(i, i ^ bit) for i in range(4)])  36 us
    ppermute x24, starting transfers between devices, pass_on(): self.got[s].append(lax.ppermute(self.now[s], 'heads', [pair]))  34.2 us
    unnamed x253, local copies, waits for them, and re-layouts  28.8 us
  transfers between devices with their start and end apart: 95, of which 28 were waited for; matrix products, arithmetic and copies ran while one was open for 28% of the time, Pallas kernels for 12%

profile of v1, /device:TPU:0, one launch (start us, length us, event | category | flops | bytes accessed | tf_op | source)
XLA Modules:
  0.0 514.1 jit_solution(17268363187106771254)
XLA Ops:
  23.1 5.7 %collective-permute-done.2.refs_3_ = bf16[128,1024]{1,0:T(8,128)(2,1)} collective-permute-done((bf16[128,1024]{1,0:T(8,128)(2,1)S(1)}, bf16[128,1024]{1,0:T(8,128)(2,1)}, u32[]{:S(2)}, u32[]{:S(2)}) %collective-permute-start.2) | collective-permute-done | bytes 262176 | tf_op jit(solution)/shard_map/ppermute | solution.py:38
  43.3 4.4 shard_map.200
  56.2 7.6 %collective-permute-done.9 = bf16[8,256,128]{2,1,0:T(8,128)(2,1)S(1)} collective-permute-done((bf16[8,256,128]{2,1,0:T(8,128)(2,1)S(1)}, bf16[8,256,128]{2,1,0:T(8,128)(2,1)S(1)}, u32[]{:S(2)}, u32[]{:S(2)}) %collective-permute-start.9) | collective-permute-done | bytes 524320 | tf_op jit(solution)/shard_map/ppermute | solution.py:442
  64.8 5.0 collective-permute-start.16
  69.8 5.2 %collective-permute-done.13 = bf16[8,256,128]{2,1,0:T(8,128)(2,1)S(1)} collective-permute-done((bf16[8,256,128]{2,1,0:T(8,128)(2,1)S(1)}, bf16[8,256,128]{2,1,0:T(8,128)(2,1)S(1)}, u32[]{:S(2)}, u32[]{:S(2)}) %collective-permute-start.13) | collective-permute-done | bytes 524320 | tf_op jit(solution)/shard_map/ppermute | solution.py:442
  76.9 7.8 %collective-permute-done.16 = bf16[8,256,128]{2,1,0:T(8,128)(2,1)S(1)} collective-permute-done((bf16[8,256,128]{2,1,0:T(8,128)(2,1)S(1)}, bf16[8,256,128]{2,1,0:T(8,128)(2,1)S(1)}, u32[]{:S(2)}, u32[]{:S(2)}) %collective-permute-start.16) | collective-permute-done | bytes 524320 | tf_op jit(solution)/shard_map/ppermute | solution.py:442
  84.7 4.4 collective-permute-start.21
  94.2 4.8 collective-permute-done.21
  110.5 5.1 shard_map.201
  129.8 12.5 %collective-permute-done.34.refs_3_ = bf16[128,2816]{1,0:T(8,128)(2,1)} collective-permute-done((bf16[128,2816]{1,0:T(8,128)(2,1)S(1)}, bf16[128,2816]{1,0:T(8,128)(2,1)}, u32[]{:S(2)}, u32[]{:S(2)}) %collective-permute-start.34) | collective-permute-done | bytes 720928 | tf_op jit(solution)/shard_map/ppermute | solution.py:38
  146.7 8.7 %shard_map.202 = (bf16[4,128,1024]{2,1,0:T(8,128)(2,1)S(1)}, bf16[4,128,1024]{2,1,0:T(8,128)(2,1)S(1)}, bf16[4,128,1024]{2,1,0:T(8,128)(2,1)S(1)}, bf16[4,128,1024]{2,1,0:T(8,128)(2,1)}) custom-call(s32[8]{0:T(128)S(1)} %stack.65.order, f32[4,128,1024]{2,1,0:T(8,128)} %bitcast.196, f32[4,128,1024]{2,1,0:T(8,128)} %bitcast.163, f32[4,128,1024]{2,1,0:T(8,128)} %bitcast.193, ...), custom_call_target="tpu_custom_call" | custom-call | tf_op jit(solution)/shard_map/pallas_call | solution.py:220
  158.9 4.6 fusion.54.b_ref
  169.1 8.9 %shard_map.204 = (bf16[1024,2816]{1,0:T(8,128)(2,1)}, bf16[1024,2816]{1,0:T(8,128)(2,1)}) custom-call(s32[8]{0:T(128)S(1)} %stack.65.order, bf16[128,5632]{1,0:T(8,128)(2,1)} %shard_map.197.refs_0_, bf16[128,5632]{1,0:T(8,128)(2,1)S(1)} %collective-permute-done.17.refs_1_, bf16[128,5632]{1,0:T(8,128)(2,1)} %collective-permute-done.18.refs_2_, ...), custom_call_target="tpu_custom_call" | custom-call | tf_op jit(solution)/shard_map/pallas_call | solution.py:220
  178.0 5.9 %fusion.55 = f32[512,2816]{1,0:T(8,128)S(1)} fusion(bf16[512,1024]{1,0:T(8,128)(2,1)S(1)} %get-tuple-element.281, bf16[1024,2816]{1,0:T(8,128)(2,1)} %get-tuple-element.285), kind=kOutput, calls=%fused_computation.207 | convolution fusion | flops 2952790016 | bytes 12582912 | tf_op jit(solution)/shard_map/dot_general | solution.py:29
  184.0 5.2 %multiply_convert_fusion = (bf16[512,2816]{1,0:T(8,128)(2,1)S(1)}, f32[512,2816]{1,0:T(8,128)}) fusion(f32[512,2816]{1,0:T(8,128)S(1)} %fusion.55, bf16[512,1024]{1,0:T(8,128)(2,1)S(1)} %get-tuple-element.281, bf16[1024,2816]{1,0:T(8,128)(2,1)S(1)} %copy-done.57), kind=kOutput, calls=%fused_computation.6 | convolution fusion | flops 2955673600 | bytes 21233664 | tf_op jit(solution)/shard_map/dot_general | solution.py:29
  190.8 5.1 convolution_convert_fusion
  208.7 4.5 shard_map.205
  213.2 7.8 %fusion.1 = (bf16[512,2816]{1,0:T(8,128)(2,1)S(1)}, bf16[512,2816]{1,0:T(8,128)(2,1)S(1)}) fusion(f32[512,2816]{1,0:T(8,128)} %get-tuple-element.291, f32[512,2816]{1,0:T(8,128)S(1)} %fusion.55, bf16[2816,1024]{1,0:T(8,128)(2,1)} %shard_map.205, bf16[512,1024]{1,0:T(8,128)(2,1)S(1)} %bitcast.170), kind=kOutput, calls=%fused_computation.3 | convolution fusion | flops 2958557184 | bytes 24117248 | tf_op jit(solution)/shard_map/dot_general | solution.py:29
  226.7 5.3 %fusion.56 = f32[512,1024]{1,0:T(8,128)S(1)} fusion(bf16[512,2816]{1,0:T(8,128)(2,1)S(1)} %get-tuple-element.314, bf16[1024,2816]{1,0:T(8,128)(2,1)} %get-tuple-element.285), kind=kOutput, calls=%fused_computation.208 | convolution fusion | flops 2952790016 | bytes 10747904 | tf_op jit(solution)/shard_map/dot_general | solution.py:29
  232.1 4.6 convolution_add_fusion.g_ref
  242.6 7.2 %shard_map.207 = (bf16[4,128,1024]{2,1,0:T(8,128)(2,1)S(1)}, bf16[4,128,1024]{2,1,0:T(8,128)(2,1)S(1)}, bf16[4,8,256,128]{3,2,1,0:T(8,128)(2,1)S(1)}) custom-call(s32[8]{0:T(128)S(1)} %stack.65.order, f32[4,128,1024]{2,1,0:T(8,128)} %bitcast.197, f32[4,128,1024]{2,1,0:T(8,128)} %bitcast.200, bf16[4,128,1024]{2,1,0:T(8,128)(2,1)S(1)} %copy-done.17, ...), custom_call_target="tpu_custom_call" | custom-call | tf_op jit(solution)/shard_map/pallas_call | solution.py:220
  258.3 10.0 %collective-permute-done.51 = bf16[704,512]{1,0:T(8,128)(2,1)S(1)} collective-permute-done((bf16[704,512]{1,0:T(8,128)(2,1)S(1)}, bf16[704,512]{1,0:T(8,128)(2,1)S(1)}, u32[]{:S(2)}, u32[]{:S(2)}) %collective-permute-start.51) | collective-permute-done | bytes 720928 | tf_op jit(solution)/shard_map/ppermute | solution.py:38
  281.1 11.3 %shard_map.208 = (bf16[4,128,1024]{2,1,0:T(8,128)(2,1)S(1)}, f32[4,128,1024]{2,1,0:T(8,128)S(1)}, f32[4,128,1024]{2,1,0:T(8,128)}) custom-call(s32[8]{0:T(128)S(1)} %stack.65.order, f32[4,128,1024]{2,1,0:T(8,128)} %bitcast.198, f32[4,128,1024]{2,1,0:T(8,128)} %bitcast.164, f32[4,128,1024]{2,1,0:T(8,128)} %bitcast.194, bf16[4,128,1024]{2,1,0:T(8,128)(2,1)S(1)} %copy-done.20, ...), custom_call_target="tpu_custom_call" | custom-call | tf_op jit(solution)/shard_map/pallas_call | solution.py:220
  307.4 12.8 %collective-permute-done.57 = bf16[8,256,128]{2,1,0:T(8,128)(2,1)S(1)} collective-permute-done((bf16[8,256,128]{2,1,0:T(8,128)(2,1)S(1)}, bf16[8,256,128]{2,1,0:T(8,128)(2,1)S(1)}, u32[]{:S(2)}, u32[]{:S(2)}) %collective-permute-start.57) | collective-permute-done | bytes 524320 | tf_op jit(solution)/shard_map/ppermute | solution.py:442
  329.3 15.5 %collective-permute-done.60 = bf16[8,256,128]{2,1,0:T(8,128)(2,1)S(1)} collective-permute-done((bf16[8,256,128]{2,1,0:T(8,128)(2,1)S(1)}, bf16[8,256,128]{2,1,0:T(8,128)(2,1)S(1)}, u32[]{:S(2)}, u32[]{:S(2)}) %collective-permute-start.60) | collective-permute-done | bytes 524320 | tf_op jit(solution)/shard_map/ppermute | solution.py:442
  356.3 11.0 %collective-permute-done.67 = bf16[8,256,128]{2,1,0:T(8,128)(2,1)S(1)} collective-permute-done((bf16[8,256,128]{2,1,0:T(8,128)(2,1)S(1)}, bf16[8,256,128]{2,1,0:T(8,128)(2,1)S(1)}, u32[]{:S(2)}, u32[]{:S(2)}) %collective-permute-start.67) | collective-permute-done | bytes 524320 | tf_op jit(solution)/shard_map/ppermute | solution.py:442
  379.3 7.0 %collective-permute-done.70 = bf16[8,256,128]{2,1,0:T(8,128)(2,1)S(1)} collective-permute-done((bf16[8,256,128]{2,1,0:T(8,128)(2,1)S(1)}, bf16[8,256,128]{2,1,0:T(8,128)(2,1)S(1)}, u32[]{:S(2)}, u32[]{:S(2)}) %collective-permute-start.70) | collective-permute-done | bytes 524320 | tf_op jit(solution)/shard_map/ppermute | solution.py:442
  389.4 6.2 %shard_map.209 = (bf16[4,128,1024]{2,1,0:T(8,128)(2,1)S(1)}, bf16[4,128,1024]{2,1,0:T(8,128)(2,1)S(1)}) custom-call(s32[8]{0:T(128)S(1)} %stack.65.order, f32[4,128,1024]{2,1,0:T(8,128)S(1)} %bitcast.165, f32[4,128,1024]{2,1,0:T(8,128)} %bitcast.195, f32[4,128,1024]{2,1,0:T(8,128)} %copy-done.11, f32[4,128,1024]{2,1,0:T(8,128)} %get-tuple-element.327, ...), custom_call_target="tpu_custom_call" | custom-call | tf_op jit(solution)/shard_map/pallas_call | solution.py:220
  408.2 5.7 %collective-permute-done.77 = bf16[256,1024]{1,0:T(8,128)(2,1)S(1)} collective-permute-done((bf16[256,1024]{1,0:T(8,128)(2,1)S(1)}, bf16[256,1024]{1,0:T(8,128)(2,1)S(1)}, u32[]{:S(2)}, u32[]{:S(2)}) %collective-permute-start.77) | collective-permute-done | bytes 524320 | tf_op jit(solution)/shard_map/ppermute | solution.py:38
  420.7 8.6 %collective-permute-done.78 = bf16[128,2816]{1,0:T(8,128)(2,1)S(1)} collective-permute-done((bf16[128,2816]{1,0:T(8,128)(2,1)S(1)}, bf16[128,2816]{1,0:T(8,128)(2,1)S(1)}, u32[]{:S(2)}, u32[]{:S(2)}) %collective-permute-start.78) | collective-permute-done | bytes 720928 | tf_op jit(solution)/shard_map/ppermute | solution.py:38
  452.0 11.4 %collective-permute-done.86 = bf16[128,2816]{1,0:T(8,128)(2,1)S(1)} collective-permute-done((bf16[128,2816]{1,0:T(8,128)(2,1)}, bf16[128,2816]{1,0:T(8,128)(2,1)S(1)}, u32[]{:S(2)}, u32[]{:S(2)}) %collective-permute-start.86) | collective-permute-done | bytes 720928 | tf_op jit(solution)/shard_map/ppermute | solution.py:185
  479.7 19.7 %collective-permute-done.91 = bf16[352,256]{1,0:T(8,128)(2,1)S(1)} collective-permute-done((bf16[352,256]{1,0:T(8,128)(2,1)}, bf16[352,256]{1,0:T(8,128)(2,1)S(1)}, u32[]{:S(2)}, u32[]{:S(2)}) %collective-permute-start.91) | collective-permute-done | bytes 180256 | tf_op jit(solution)/shard_map/ppermute | solution.py:185
  (572 shorter events, 261.4 us)
Async XLA Ops:
  7.8 24.5 %collective-permute-start.4 = (bf16[128,2048]{1,0:T(8,128)(2,1)S(1)}, bf16[128,2048]{1,0:T(8,128)(2,1)}, u32[]{:S(2)}, u32[]{:S(2)}) collective-permute-start(bf16[128,2048]{1,0:T(8,128)(2,1)S(1)} %shard_map.195.refs_0_), channel_id=1, source_target_pairs={{0,4},{4,0},{8,12},{12,8},{16,20},{20,16},{24,28},{28,24},{1,5},{5... | collective-permute-start | bytes 1572872 | tf_op jit(solution)/shard_map/ppermute | solution.py:38
  32.3 22.5 %collective-permute-start.10 = (bf16[128,3072]{1,0:T(8,128)(2,1)S(1)}, bf16[128,3072]{1,0:T(8,128)(2,1)S(1)}, u32[]{:S(2)}, u32[]{:S(2)}) collective-permute-start(bf16[128,3072]{1,0:T(8,128)(2,1)S(1)} %shard_map.196.refs_0_), channel_id=1, source_target_pairs={{0,8},{4,12},{8,0},{12,4},{16,24},{20,28},{24,16},{28,20},{1,9},{5... | collective-permute-start | bytes 2359304 | tf_op jit(solution)/shard_map/ppermute | solution.py:38
  32.9 23.2 %collective-permute-start.11 = (bf16[128,3072]{1,0:T(8,128)(2,1)S(1)}, bf16[128,3072]{1,0:T(8,128)(2,1)S(1)}, u32[]{:S(2)}, u32[]{:S(2)}) collective-permute-start(bf16[128,3072]{1,0:T(8,128)(2,1)S(1)} %shard_map.196.refs_0_), channel_id=1, source_target_pairs={{0,16},{4,20},{8,24},{12,28},{16,0},{20,4},{24,8},{28,12},{1,17},{... | collective-permute-start | bytes 2359304 | tf_op jit(solution)/shard_map/ppermute | solution.py:38
  51.8 37.4 %collective-permute-start.17 = (bf16[128,5632]{1,0:T(8,128)(2,1)}, bf16[128,5632]{1,0:T(8,128)(2,1)S(1)}, u32[]{:S(2)}, u32[]{:S(2)}) collective-permute-start(bf16[128,5632]{1,0:T(8,128)(2,1)} %shard_map.197.refs_0_), channel_id=1, source_target_pairs={{0,8},{4,12},{8,0},{12,4},{16,24},{20,28},{24,16},{28,20},{1,9},{5... | collective-permute-start | bytes 4325384 | tf_op jit(solution)/shard_map/ppermute | solution.py:38
  53.3 37.5 %collective-permute-start.18 = (bf16[128,5632]{1,0:T(8,128)(2,1)}, bf16[128,5632]{1,0:T(8,128)(2,1)}, u32[]{:S(2)}, u32[]{:S(2)}) collective-permute-start(bf16[128,5632]{1,0:T(8,128)(2,1)} %shard_map.197.refs_0_), channel_id=1, source_target_pairs={{0,16},{4,20},{8,24},{12,28},{16,0},{20,4},{24,8},{28,12},{1,17},{... | collective-permute-start | bytes 4325384 | tf_op jit(solution)/shard_map/ppermute | solution.py:38
  104.9 63.5 %collective-permute-start.38 = (bf16[128,5632]{1,0:T(8,128)(2,1)}, bf16[128,5632]{1,0:T(8,128)(2,1)}, u32[]{:S(2)}, u32[]{:S(2)}) collective-permute-start(bf16[128,5632]{1,0:T(8,128)(2,1)} %shard_map.197.refs_0_), channel_id=1, source_target_pairs={{0,4},{4,0},{8,12},{12,8},{16,20},{20,16},{24,28},{28,24},{1,5},{5... | collective-permute-start | bytes 4325384 | tf_op jit(solution)/shard_map/ppermute | solution.py:38
  123.6 45.0 %collective-permute-start.39 = (bf16[128,5632]{1,0:T(8,128)(2,1)S(1)}, bf16[128,5632]{1,0:T(8,128)(2,1)}, u32[]{:S(2)}, u32[]{:S(2)}) collective-permute-start(bf16[128,5632]{1,0:T(8,128)(2,1)S(1)} %collective-permute-done.17.refs_1_), channel_id=1, source_target_pairs={{0,4},{4,0},{8,12},{12,8},{16,20},{20,16},{24,28},{28,24},{1,5},{5... | collective-permute-start | bytes 4325384 | tf_op jit(solution)/shard_map/ppermute | solution.py:38
  127.8 41.2 %collective-permute-start.40 = (bf16[128,5632]{1,0:T(8,128)(2,1)}, bf16[128,5632]{1,0:T(8,128)(2,1)}, u32[]{:S(2)}, u32[]{:S(2)}) collective-permute-start(bf16[128,5632]{1,0:T(8,128)(2,1)} %collective-permute-done.18.refs_2_), channel_id=1, source_target_pairs={{0,4},{4,0},{8,12},{12,8},{16,20},{20,16},{24,28},{28,24},{1,5},{5... | collective-permute-start | bytes 4325384 | tf_op jit(solution)/shard_map/ppermute | solution.py:38
  168.4 35.7 %collective-permute-start.43 = (bf16[352,1024]{1,0:T(8,128)(2,1)S(1)}, bf16[352,1024]{1,0:T(8,128)(2,1)S(1)}, u32[]{:S(2)}, u32[]{:S(2)}) collective-permute-start(bf16[352,1024]{1,0:T(8,128)(2,1)S(1)} %copy-done.24), channel_id=1, source_target_pairs={{0,4},{4,0},{8,12},{12,8},{16,20},{20,16},{24,28},{28,24},{1,5},{5... | collective-permute-start | bytes 2162696 | tf_op jit(solution)/shard_map/ppermute | solution.py:38
  168.6 36.0 %collective-permute-start.44 = (bf16[352,1024]{1,0:T(8,128)(2,1)S(1)}, bf16[352,1024]{1,0:T(8,128)(2,1)S(1)}, u32[]{:S(2)}, u32[]{:S(2)}) collective-permute-start(bf16[352,1024]{1,0:T(8,128)(2,1)S(1)} %copy-done.13), channel_id=1, source_target_pairs={{0,4},{4,0},{8,12},{12,8},{16,20},{20,16},{24,28},{28,24},{1,5},{5... | collective-permute-start | bytes 2162696 | tf_op jit(solution)/shard_map/ppermute | solution.py:38
  169.0 35.7 %collective-permute-start.45 = (bf16[352,1024]{1,0:T(8,128)(2,1)S(1)}, bf16[352,1024]{1,0:T(8,128)(2,1)S(1)}, u32[]{:S(2)}, u32[]{:S(2)}) collective-permute-start(bf16[352,1024]{1,0:T(8,128)(2,1)S(1)} %copy-done.15), channel_id=1, source_target_pairs={{0,4},{4,0},{8,12},{12,8},{16,20},{20,16},{24,28},{28,24},{1,5},{5... | collective-permute-start | bytes 2162696 | tf_op jit(solution)/shard_map/ppermute | solution.py:38
  268.7 25.5 %collective-permute-start.55 = (bf16[512,2816]{1,0:T(8,128)(2,1)}, bf16[512,2816]{1,0:T(8,128)(2,1)}, u32[]{:S(2)}, u32[]{:S(2)}) collective-permute-start(bf16[512,2816]{1,0:T(8,128)(2,1)} %convolution_convert_fusion.2), channel_id=1, source_target_pairs={{0,4},{4,0},{8,12},{12,8},{16,20},{20,16},{24,28},{28,24},{1,5},{5... | collective-permute-start | bytes 8650760 | tf_op jit(solution)/shard_map/ppermute | solution.py:38
  268.7 25.5 %collective-permute-start.56 = (bf16[512,2816]{1,0:T(8,128)(2,1)}, bf16[512,2816]{1,0:T(8,128)(2,1)}, u32[]{:S(2)}, u32[]{:S(2)}) collective-permute-start(bf16[512,2816]{1,0:T(8,128)(2,1)} %convolution_convert_fusion.1), channel_id=1, source_target_pairs={{0,4},{4,0},{8,12},{12,8},{16,20},{20,16},{24,28},{28,24},{1,5},{5... | collective-permute-start | bytes 8650760 | tf_op jit(solution)/shard_map/ppermute | solution.py:38
  278.2 27.7 %collective-permute-start.59 = (bf16[8,256,128]{2,1,0:T(8,128)(2,1)}, bf16[8,256,128]{2,1,0:T(8,128)(2,1)S(1)}, u32[]{:S(2)}, u32[]{:S(2)}) collective-permute-start(bf16[8,256,128]{2,1,0:T(8,128)(2,1)} %get-tuple-element.497), channel_id=1, source_target_pairs={{3,2},{7,6},{11,10},{15,14},{19,18},{23,22},{27,26},{31,30}} | collective-permute-start | bytes 1572872 | tf_op jit(solution)/shard_map/ppermute | solution.py:442
  292.5 35.5 %collective-permute-start.62 = (bf16[8,256,128]{2,1,0:T(8,128)(2,1)}, bf16[8,256,128]{2,1,0:T(8,128)(2,1)S(1)}, u32[]{:S(2)}, u32[]{:S(2)}) collective-permute-start(bf16[8,256,128]{2,1,0:T(8,128)(2,1)} %get-tuple-element.494), channel_id=1, source_target_pairs={{3,2},{7,6},{11,10},{15,14},{19,18},{23,22},{27,26},{31,30}} | collective-permute-start | bytes 1572872 | tf_op jit(solution)/shard_map/ppermute | solution.py:442
  293.4 28.4 %collective-permute-start.63 = (bf16[352,512]{1,0:T(8,128)(2,1)S(1)}, bf16[352,512]{1,0:T(8,128)(2,1)S(1)}, u32[]{:S(2)}, u32[]{:S(2)}) collective-permute-start(bf16[352,512]{1,0:T(8,128)(2,1)S(1)} %slice.347), channel_id=1, source_target_pairs={{0,16},{4,20},{8,24},{12,28},{16,0},{20,4},{24,8},{28,12},{1,17},{... | collective-permute-start | bytes 1081352 | tf_op jit(solution)/shard_map/ppermute | solution.py:38
  296.0 24.2 %collective-permute-start.57 = (bf16[8,256,128]{2,1,0:T(8,128)(2,1)S(1)}, bf16[8,256,128]{2,1,0:T(8,128)(2,1)S(1)}, u32[]{:S(2)}, u32[]{:S(2)}) collective-permute-start(bf16[8,256,128]{2,1,0:T(8,128)(2,1)S(1)} %get-tuple-element.501), channel_id=1, source_target_pairs={{1,0},{5,4},{9,8},{13,12},{17,16},{21,20},{25,24},{29,28}} | collective-permute-start | bytes 1572872 | tf_op jit(solution)/shard_map/ppermute | solution.py:442
  297.4 22.9 %collective-permute-start.58 = (bf16[8,256,128]{2,1,0:T(8,128)(2,1)S(1)}, bf16[8,256,128]{2,1,0:T(8,128)(2,1)S(1)}, u32[]{:S(2)}, u32[]{:S(2)}) collective-permute-start(bf16[8,256,128]{2,1,0:T(8,128)(2,1)S(1)} %get-tuple-element.500), channel_id=1, source_target_pairs={{2,1},{6,5},{10,9},{14,13},{18,17},{22,21},{26,25},{30,29}} | collective-permute-start | bytes 1572872 | tf_op jit(solution)/shard_map/ppermute | solution.py:442
  321.8 24.3 %collective-permute-start.65 = (bf16[512,1024]{1,0:T(8,128)(2,1)S(1)}, bf16[512,1024]{1,0:T(8,128)(2,1)S(1)}, u32[]{:S(2)}, u32[]{:S(2)}) collective-permute-start(bf16[512,1024]{1,0:T(8,128)(2,1)S(1)} %convolution_convert_fusion.7), channel_id=1, source_target_pairs={{0,4},{4,0},{8,12},{12,8},{16,20},{20,16},{24,28},{28,24},{1,5},{5... | collective-permute-start | bytes 3145736 | tf_op jit(solution)/shard_map/ppermute | solution.py:38
  321.9 24.2 %collective-permute-start.66 = (bf16[512,1024]{1,0:T(8,128)(2,1)S(1)}, bf16[512,1024]{1,0:T(8,128)(2,1)S(1)}, u32[]{:S(2)}, u32[]{:S(2)}) collective-permute-start(bf16[512,1024]{1,0:T(8,128)(2,1)S(1)} %convolution_convert_fusion.6), channel_id=1, source_target_pairs={{0,4},{4,0},{8,12},{12,8},{16,20},{20,16},{24,28},{28,24},{1,5},{5... | collective-permute-start | bytes 3145736 | tf_op jit(solution)/shard_map/ppermute | solution.py:38
  328.0 48.7 %collective-permute-start.71 = (bf16[256,2816]{1,0:T(8,128)(2,1)S(1)}, bf16[256,2816]{1,0:T(8,128)(2,1)S(1)}, u32[]{:S(2)}, u32[]{:S(2)}) collective-permute-start(bf16[256,2816]{1,0:T(8,128)(2,1)S(1)} %slice.351), channel_id=1, source_target_pairs={{0,8},{4,12},{8,0},{12,4},{16,24},{20,28},{24,16},{28,20},{1,9},{5... | collective-permute-start | bytes 4325384 | tf_op jit(solution)/shard_map/ppermute | solution.py:38
  344.8 34.5 %collective-permute-start.72 = (bf16[256,2816]{1,0:T(8,128)(2,1)S(1)}, bf16[256,2816]{1,0:T(8,128)(2,1)S(1)}, u32[]{:S(2)}, u32[]{:S(2)}) collective-permute-start(bf16[256,2816]{1,0:T(8,128)(2,1)S(1)} %slice.352), channel_id=1, source_target_pairs={{0,16},{4,20},{8,24},{12,28},{16,0},{20,4},{24,8},{28,12},{1,17},{... | collective-permute-start | bytes 4325384 | tf_op jit(solution)/shard_map/ppermute | solution.py:38
  367.3 30.3 %collective-permute-start.73 = (bf16[256,1024]{1,0:T(8,128)(2,1)}, bf16[256,1024]{1,0:T(8,128)(2,1)}, u32[]{:S(2)}, u32[]{:S(2)}) collective-permute-start(bf16[256,1024]{1,0:T(8,128)(2,1)} %slice.358), channel_id=1, source_target_pairs={{0,8},{4,12},{8,0},{12,4},{16,24},{20,28},{24,16},{28,20},{1,9},{5... | collective-permute-start | bytes 1572872 | tf_op jit(solution)/shard_map/ppermute | solution.py:38
  368.6 29.0 %collective-permute-start.74 = (bf16[256,1024]{1,0:T(8,128)(2,1)}, bf16[256,1024]{1,0:T(8,128)(2,1)}, u32[]{:S(2)}, u32[]{:S(2)}) collective-permute-start(bf16[256,1024]{1,0:T(8,128)(2,1)} %slice.359), channel_id=1, source_target_pairs={{0,16},{4,20},{8,24},{12,28},{16,0},{20,4},{24,8},{28,12},{1,17},{... | collective-permute-start | bytes 1572872 | tf_op jit(solution)/shard_map/ppermute | solution.py:38
  399.9 29.4 %collective-permute-start.78 = (bf16[128,2816]{1,0:T(8,128)(2,1)S(1)}, bf16[128,2816]{1,0:T(8,128)(2,1)S(1)}, u32[]{:S(2)}, u32[]{:S(2)}) collective-permute-start(bf16[128,2816]{1,0:T(8,128)(2,1)S(1)} %slice.365), channel_id=1, source_target_pairs={{0,16},{4,20},{8,24},{12,28},{16,0},{20,4},{24,8},{28,12},{1,17},{... | collective-permute-start | bytes 2162696 | tf_op jit(solution)/shard_map/ppermute | solution.py:38
  401.3 29.5 %collective-permute-start.79 = (bf16[128,2816]{1,0:T(8,128)(2,1)S(1)}, bf16[128,2816]{1,0:T(8,128)(2,1)S(1)}, u32[]{:S(2)}, u32[]{:S(2)}) collective-permute-start(bf16[128,2816]{1,0:T(8,128)(2,1)S(1)} %slice.366), channel_id=1, source_target_pairs={{0,8},{4,12},{8,0},{12,4},{16,24},{20,28},{24,16},{28,20},{1,9},{5... | collective-permute-start | bytes 2162696 | tf_op jit(solution)/shard_map/ppermute | solution.py:38
  415.5 23.2 %collective-permute-start.81 = (bf16[128,1024]{1,0:T(8,128)(2,1)S(1)}, bf16[128,1024]{1,0:T(8,128)(2,1)S(1)}, u32[]{:S(2)}, u32[]{:S(2)}) collective-permute-start(bf16[128,1024]{1,0:T(8,128)(2,1)S(1)} %slice.367), channel_id=1, source_target_pairs={{0,16},{4,20},{8,24},{12,28},{16,0},{20,4},{24,8},{28,12},{1,17},{... | collective-permute-start | bytes 786440 | tf_op jit(solution)/shard_map/ppermute | solution.py:38
  416.3 22.4 %collective-permute-start.82 = (bf16[128,1024]{1,0:T(8,128)(2,1)S(1)}, bf16[128,1024]{1,0:T(8,128)(2,1)S(1)}, u32[]{:S(2)}, u32[]{:S(2)}) collective-permute-start(bf16[128,1024]{1,0:T(8,128)(2,1)S(1)} %slice.368), channel_id=1, source_target_pairs={{0,8},{4,12},{8,0},{12,4},{16,24},{20,28},{24,16},{28,20},{1,9},{5... | collective-permute-start | bytes 786440 | tf_op jit(solution)/shard_map/ppermute | solution.py:38
  471.3 28.2 %collective-permute-start.92 = (bf16[128,1408]{1,0:T(8,128)(2,1)}, bf16[128,1408]{1,0:T(8,128)(2,1)S(1)}, u32[]{:S(2)}, u32[]{:S(2)}) collective-permute-start(bf16[128,1408]{1,0:T(8,128)(2,1)} %pad_maximum_fusion.5), channel_id=1, source_target_pairs={{0,2},{1,3},{2,0},{3,1},{4,6},{5,7},{6,4},{7,5},{8,10},{9,11},{10,... | collective-permute-start | bytes 1081352 | tf_op jit(solution)/shard_map/ppermute | solution.py:185
  476.4 23.0 %collective-permute-start.90 = (bf16[128,1024]{1,0:T(8,128)(2,1)S(1)}, bf16[128,1024]{1,0:T(8,128)(2,1)S(1)}, u32[]{:S(2)}, u32[]{:S(2)}) collective-permute-start(bf16[128,1024]{1,0:T(8,128)(2,1)S(1)} %pad_maximum_fusion.6), channel_id=1, source_target_pairs={{0,1},{1,0},{2,3},{3,2},{4,5},{5,4},{6,7},{7,6},{8,9},{9,8},{10,11... | collective-permute-start | bytes 786440 | tf_op jit(solution)/shard_map/ppermute | solution.py:185
  476.8 22.7 %collective-permute-start.91 = (bf16[352,256]{1,0:T(8,128)(2,1)}, bf16[352,256]{1,0:T(8,128)(2,1)S(1)}, u32[]{:S(2)}, u32[]{:S(2)}) collective-permute-start(bf16[352,256]{1,0:T(8,128)(2,1)} %fusion.41), channel_id=1, source_target_pairs={{0,2},{1,3},{2,0},{3,1},{4,6},{5,7},{6,4},{7,5},{8,10},{9,11},{10,... | collective-permute-start | bytes 540680 | tf_op jit(solution)/shard_map/ppermute | solution.py:185
  476.8 26.0 %collective-permute-start.93 = (bf16[128,768]{1,0:T(8,128)(2,1)}, bf16[128,768]{1,0:T(8,128)(2,1)}, u32[]{:S(2)}, u32[]{:S(2)}) collective-permute-start(bf16[128,768]{1,0:T(8,128)(2,1)} %pad_maximum_fusion.7), channel_id=1, source_target_pairs={{0,2},{1,3},{2,0},{3,1},{4,6},{5,7},{6,4},{7,5},{8,10},{9,11},{10,... | collective-permute-start | bytes 589832 | tf_op jit(solution)/shard_map/ppermute | solution.py:185
  (186 other events, 2055.6 us)

commit v2 on v1

--- a/solution.py
+++ b/solution.py
@@ -14,7 +14,7 @@
 EPS = 1e-06
 F32 = jnp.float32
 BF16 = jnp.bfloat16
-VMEM_LIMIT = 48 << 20
+VMEM_LIMIT = 60 << 20
 
 BITS = (0, 2, 4, 6, 1, 3, 5, 7)
 BITS_X = (0, 4, 2, 6, 1, 5, 3, 7)
@@ -38,61 +38,50 @@
     return lax.ppermute(value, "rows", [(i, i ^ bit) for i in range(size)])
 
 
-def place_body(rows, splits, order, *refs):
-    pieces, outs, sems = refs[:10], refs[10 : 10 + len(splits)], refs[-1]
-    half = sum(w for _, _, w in splits) // 2
-    copies = []
-    for i, (at, to, width) in enumerate(splits):
-        for k in range(8):
-            core, chip = k // 4, k % 4
-            source = pieces[5 * core + chip]
-            begin = at
-            if chip == 3 and at >= half:
-                source, begin = pieces[5 * core + 4], at - half
-            copies.append(
-                pltpu.make_async_copy(
-                    source.at[:, begin : begin + width],
-                    outs[i].at[at_block(order, BITS[k], rows), to : to + width],
-                    sems.at[i, k],
-                )
-            )
+def swap_heads(value, bit):
+    return lax.ppermute(value, "heads", [(i, i ^ bit) for i in range(4)])
+
+
+HBM = pl.BlockSpec(memory_space=pltpu.HBM)
+
+
+def whole_spec(rows, width):
+    return pl.BlockSpec((rows, width), lambda i, *_: (0, 0))
+
+
+def run_copies(copies):
     for copy in copies:
         copy.start()
     for copy in copies:
         copy.wait()
 
 
-def pack_body(splits, order, *refs):
-    count = len(splits)
-    ins, out, sems = refs[:count], refs[count], refs[-1]
-    copies = [
-        pltpu.make_async_copy(
-            ins[i].at[:, to : to + width], out.at[:, at : at + width], sems.at[i]
-        )
-        for i, (at, to, width) in enumerate(splits)
-    ]
-    for copy in copies:
-        copy.start()
-    for copy in copies:
-        copy.wait()
-
-
-def whole_spec(rows, width):
-    return pl.BlockSpec((rows, width), lambda i, *_: (0, 0))
-
-
-ANYWHERE = pl.BlockSpec(memory_space=pltpu.HBM)
-
-
-def pack(splits, arrays, order):
+def pack(order, arrays, lists):
     rows = arrays[0].shape[0]
-    width = sum(w for _, _, w in splits)
-    (out,) = call(
-        functools.partial(pack_body, splits), (1,), order, [(a, ANYWHERE) for a in arrays],
-        [((rows, width), BF16, whole_spec(rows, width))],
-        scratch=[pltpu.SemaphoreType.DMA((len(splits),))],
-    )
-    return out
+    widths = [sum(w for _, _, w in parts) for parts in lists]
+    most = max(len(parts) for parts in lists)
+
+    def body(order, *refs):
+        ins, outs, sems = refs[: len(arrays)], refs[len(arrays) : -1], refs[-1]
+        copies = []
+        for j, parts in enumerate(lists):
+            at = 0
+            for i, (which, begin, width) in enumerate(parts):
+                copies.append(
+                    pltpu.make_async_copy(
+                        ins[which].at[:, begin : begin + width],
+                        outs[j].at[:, at : at + width],
+                        sems.at[j, i],
+                    )
+                )
+                at += width
+        run_copies(copies)
+
+    return call(
+        body, (1,), order, [(a, HBM) for a in arrays],
+        [((rows, w), BF16, whole_spec(rows, w)) for w in widths],
+        scratch=[pltpu.SemaphoreType.DMA((len(lists), most))],
+    )
 
 
 class Clock:
@@ -106,66 +95,87 @@
             setattr(o, n, value)
 
 
+def places(here, head):
+    return jnp.stack([here ^ b for b in range(8)] + [head ^ b for b in range(4)]).astype(jnp.int32)
+
+
 class Gather:
-    def __init__(self, piece, splits, owners, widths):
-        self.piece, self.splits, self.owners, self.widths = piece, splits, owners, widths
+    def __init__(self, pieces):
+        self.pieces = list(pieces)
 
     def first(self):
-        self.near = [swap(self.piece, 2, 8), swap(self.piece, 4, 8)]
+        self.near_x = [swap(p, 2, 8) for p in self.pieces]
+        self.near_y = [swap(p, 4, 8) for p in self.pieces]
 
     def second(self):
-        half = self.piece.shape[1] // 2
-        self.far = [swap(self.near[0][:, :half], 4, 8), swap(self.near[1][:, half:], 2, 8)]
-
-    def cross_first(self):
-        self.other = [swap(p, 1, 8) for p in [self.piece] + self.near]
-
-    def cross_second(self):
-        self.other_far = [swap(p, 1, 8) for p in self.far]
-
-    def whole(self, order):
-        rows, splits, owners = self.piece.shape[0], self.splits, self.owners
-        pieces = [self.piece] + self.near + self.far + self.other + self.other_far
-        count = len(self.widths)
-
-        def body(order, *refs):
-            outs = refs[10 : 10 + count]
-            place_body(rows, splits, order, *refs[:10], *[outs[o] for o in owners], refs[-1])
-
-        return call(
-            body, (1,), order, [(p, ANYWHERE) for p in pieces],
-            [((8 * rows, w), BF16, whole_spec(8 * rows, w)) for w in self.widths],
-            scratch=[pltpu.SemaphoreType.DMA((len(splits), 8))],
-        )
+        self.far = [swap(self.near_x[0], 4, 8), swap(self.near_y[1], 2, 8)]
+
+    def cross(self, *names):
+        for name in names:
+            setattr(self, name + "_other", [swap(p, 1, 8) for p in getattr(self, name)])
+
+    def all(self, half):
+        names = ("pieces", "near_x", "near_y", "far")
+        return [getattr(self, n + core)[half] for core in ("", "_other") for n in names]
 
 
 def add(one, two, out=BF16):
     return (one.astype(F32) + two.astype(F32)).astype(out)
 
 
+def added(order, outs):
+    steps = 2
+    ins, results, counts = [], [], []
+    for terms, rows, dtype in outs:
+        size = rows // steps
+        width = terms[0][0].shape[1]
+        for array, first in terms:
+            ins.append((array, pl.BlockSpec((size, width), lambda i, *_, f=first // size: (f + i, 0))))
+        results.append(((rows, width), dtype, pl.BlockSpec((size, width), lambda i, *_: (i, 0))))
+        counts.append(len(terms))
+
+    def body(order, *refs):
+        at = 0
+        for out, count in zip(refs[len(ins) :], counts):
+            total = refs[at][...].astype(F32)
+            for ref in refs[at + 1 : at + count]:
+                total += ref[...].astype(F32)
+            out[...] = total.astype(out.dtype)
+            at += count
+
+    return call(body, (steps,), order, ins, results)
+
+
 class Reduce:
-    def __init__(self, sends, keeps, bits):
-        self.sends, self.keeps, self.bits = list(sends), list(keeps), list(bits)
+    def __init__(self, order, sends, keeps, bits):
+        self.order, self.sends, self.keeps, self.bits = order, list(sends), list(keeps), list(bits)
 
     def core(self):
         self.theirs = [swap(s, 1, 8) for s in self.sends]
 
     def join(self):
-        self.totals = [k(t) for k, t in zip(self.keeps, self.theirs)]
+        half = self.keeps[0].shape[0] // 2
+        pairs = zip(self.keeps, self.theirs)
+        self.totals = added(self.order, [([(k, half), (t, half)], half, BF16) for k, t in pairs])
 
     def first(self):
-        self.got = [swap(t[t.shape[0] // 2 :], b, 8) for t, b in zip(self.totals, self.bits)]
+        self.got = [swap(t, b, 8) for t, b in zip(self.totals, self.bits)]
 
     def join_first(self):
-        self.parts = [add(t[: t.shape[0] // 2], g) for t, g in zip(self.totals, self.got)]
+        rows = self.keeps[0].shape[0] // 4
+        outs = []
+        for at in (0, rows):
+            for k, t, g in zip(self.keeps, self.theirs, self.got):
+                outs.append(([(k, at), (t, at), (g, at)], rows, BF16))
+        parts = added(self.order, outs)
+        count = len(self.keeps)
+        self.own, self.parts = parts[:count], parts[count:]
 
     def second(self):
-        self.got_last = [swap(p[p.shape[0] // 2 :], 6 - b, 8) for p, b in zip(self.parts, self.bits)]
+        self.got_last = [swap(p, 6 - b, 8) for p, b in zip(self.parts, self.bits)]
 
     def join_second(self):
-        self.sums = [
-            add(p[: p.shape[0] // 2], g, F32) for p, g in zip(self.parts, self.got_last)
-        ]
+        self.sums = [add(p, g, F32) for p, g in zip(self.own, self.got_last)]
 
 
 def column_block(s, here, bit):
@@ -198,6 +208,66 @@
 
     def result(self):
         return [o + g for o, g in zip(self.own, self.split())]
+
+
+class SettleWide:
+    def __init__(self, order, parts, got):
+        self.order, self.count = order, len(parts)
+        rows, width = parts[0].shape
+        self.rows, self.block = rows, width // 4
+        count, block = self.count, self.block
+
+        def body(order, *refs):
+            own, out, held = refs[2 * count], refs[2 * count + 1], refs[2 * count + 2]
+            for i in range(count):
+                held[...] = refs[2 * i][...].astype(F32) + refs[2 * i + 1][...].astype(F32)
+                for j, bit in enumerate((0, 2)):
+                    at = (2 * i + j) * block
+                    own[:, at : at + block] = held[:, at_block(order, 8 + bit, block)]
+                    out[:, at : at + block] = held[:, at_block(order, 9 + bit, block)].astype(BF16)
+
+        spec = whole_spec(rows, width)
+        wide = whole_spec(rows, 2 * count * block)
+        shape = rows, 2 * count * block
+        ins = [(a, spec) for pair in zip(parts, got) for a in pair]
+        self.own, self.out = call(
+            body, (1,), order, ins, [(shape, F32, wide), (shape, BF16, wide)],
+            scratch=[pltpu.VMEM((rows, width), F32)],
+        )
+
+    def pass_on(self, bit):
+        self.got = lax.ppermute(self.out, "heads", [(i, i ^ bit) for i in range(4)])
+
+    def join(self):
+        rows, count, block = self.rows, self.count, self.block
+
+        def body(order, own_ref, got_ref, mine, out):
+            for i in range(count):
+                at = 2 * i * block
+                both = own_ref[:, at : at + 2 * block] + got_ref[:, at : at + 2 * block].astype(F32)
+                mine[:, i * block : (i + 1) * block] = both[:, :block]
+                out[:, i * block : (i + 1) * block] = both[:, block:].astype(BF16)
+
+        wide, narrow = whole_spec(rows, 2 * count * block), whole_spec(rows, count * block)
+        shape = rows, count * block
+        self.own, self.out = call(
+            body, (1,), self.order, [(self.own, wide), (self.got, wide)],
+            [(shape, F32, narrow), (shape, BF16, narrow)],
+        )
+
+    def result(self):
+        rows, count, block = self.rows, self.count, self.block
+
+        def body(order, own_ref, got_ref, *outs):
+            for i, out in enumerate(outs):
+                cols = slice(i * block, (i + 1) * block)
+                out[...] = own_ref[:, cols] + got_ref[:, cols].astype(F32)
+
+        narrow = whole_spec(rows, count * block)
+        return call(
+            body, (1,), self.order, [(self.own, narrow), (self.got, narrow)],
+            [((rows, block), F32, whole_spec(rows, block))] * count,
+        )
 
 
 def at_block(order_ref, index, width):
@@ -228,7 +298,7 @@
         ),
         out_shape=[jax.ShapeDtypeStruct(s, t) for s, t, _ in outs],
         compiler_params=pltpu.CompilerParams(vmem_limit_bytes=VMEM_LIMIT),
-        cost_estimate=pl.CostEstimate(flops=0, bytes_accessed=0, transcendentals=0),
+        cost_estimate=pl.CostEstimate(flops=flops // 32, bytes_accessed=moved // 32, transcendentals=0),
     )(order, *[a for a, _ in ins])
 
 
@@ -236,26 +306,17 @@
     return pl.BlockSpec((count, width), lambda i, *_: (i, column))
 
 
-def spread(order, blocks, h, outs):
-    outs[0][...] = h
-    width = h.shape[1] // blocks
-    for out, bits in zip(outs[1:], (BITS_X, BITS_Y)):
-        for k in range(blocks):
-            source = at_block(order, bits[k], width)
-            out[:, k * width : (k + 1) * width] = outs[0][:, source]
-
-
-def norm_body(blocks, order, x_ref, *outs):
+def norm_body(order, x_ref, h_ref):
     x = x_ref[...].astype(F32)
     scale = lax.rsqrt(jnp.mean(x * x, axis=-1, keepdims=True) + EPS)
-    spread(order, blocks, (x * scale).astype(BF16), outs)
-
-
-def mid_body(blocks, order, x_ref, b_ref, mid_ref, *outs):
+    h_ref[...] = (x * scale).astype(BF16)
+
+
+def mid_body(order, x_ref, b_ref, mid_ref, h_ref):
     mid = x_ref[...].astype(F32) + b_ref[...]
     mid_ref[...] = mid
     scale = lax.rsqrt(jnp.mean(mid * mid, axis=-1, keepdims=True) + EPS)
-    spread(order, blocks, (mid * scale).astype(BF16), outs)
+    h_ref[...] = (mid * scale).astype(BF16)
 
 
 def norm_back_body(order, v_ref, base_ref, g_ref, *outs):
@@ -313,7 +374,7 @@
 
 def mix_body(
     order, q_ref, k_ref, v_ref, u_ref, cos_ref, sin_ref, col_ref, row_ref, link_ref, s_ref,
-    mix_ref, gated_ref, *ordered_refs,
+    mix_ref, gated_ref,
 ):
     rows = q_ref.shape[1]
     cos, sin = cos_ref[...], sin_ref[...]
@@ -341,9 +402,6 @@
         gated_ref[0, :, cols] = (
             mix_ref[0, :, cols].astype(F32) * scale * (u * sigmoid(u))
         ).astype(BF16)
-    for out in ordered_refs:
-        for k in range(HEADS):
-            out[0, :, columns(k)] = gated_ref[0, :, at_block(order, BITS_X[k], HEAD_DIM)]
 
 
 def gate_back_body(
@@ -429,6 +487,282 @@
         dvo_ref[0, :, cols] = (dv_ref[0, :, cols] + dot(rk, state, NN)).astype(BF16)
 
 
+ORDERS = (BITS_Y, BITS_X)
+
+
+def spread(order, h_ref, outs):
+    width = h_ref.shape[1] // 8
+    for out, bits in zip(outs, ORDERS):
+        for k in range(8):
+            out[:, k * width : (k + 1) * width] = h_ref[:, at_block(order, bits[k], width)]
+
+
+def row_norm_body(order, x_ref, *refs):
+    x = x_ref[...].astype(F32)
+    scale = lax.rsqrt(jnp.mean(x * x, axis=-1, keepdims=True) + EPS)
+    refs[-1][...] = (x * scale).astype(BF16)
+    spread(order, refs[-1], refs[:-1])
+
+
+def head_slope(head):
+    return jnp.exp2(-8.0 * (head.astype(F32) + 1.0) / HEADS)
+
+
+def block_decay(ids_col, ids_row, i, j, size, slope):
+    gap = (
+        (i - j) * size
+        + lax.broadcasted_iota(jnp.int32, (size, size), 0)
+        - lax.broadcasted_iota(jnp.int32, (size, size), 1)
+    ).astype(F32)
+    same = ids_col[i * size : (i + 1) * size] == ids_row[:, j * size : (j + 1) * size]
+    keep = same if i > j else same & (gap >= 0.0)
+    return jnp.where(keep, jnp.exp(-slope * jnp.maximum(gap, 0.0)), 0.0)
+
+
+def row_mix_body(size, order, q_ref, k_ref, v_ref, cos_ref, sin_ref, col_ref, row_ref, mix_ref):
+    cos, sin = cos_ref[...], sin_ref[...]
+    col, row = col_ref[...], row_ref[...]
+    each = q_ref.shape[1] // HEAD_DIM
+    for part in range(each):
+        cols = columns(part)
+        slope = head_slope(pl.program_id(0) * each + part)
+        rq = turned(rounded_swish(q_ref[:, cols]), cos, sin).astype(BF16)
+        rk = turned(rounded_swish(k_ref[:, cols]), cos, sin).astype(BF16)
+        value = v_ref[:, cols].astype(BF16)
+        for i in range(rq.shape[0] // size):
+            here = slice(i * size, (i + 1) * size)
+            mixed = jnp.zeros((size, HEAD_DIM), F32)
+            for j in range(i + 1):
+                there = slice(j * size, (j + 1) * size)
+                scores = dot(rq[here], rk[there], NT) * block_decay(col, row, i, j, size, slope)
+                mixed += dot(scores.astype(BF16), value[there], NN)
+            mix_ref[here, cols] = mixed.astype(BF16)
+
+
+def row_mix_back_body(
+    size, order, q_ref, k_ref, v_ref, dm_ref, cos_ref, sin_ref, col_ref, row_ref,
+    dq_ref, dk_ref, dv_ref,
+):
+    cos, sin = cos_ref[...], sin_ref[...]
+    col, row = col_ref[...], row_ref[...]
+    each = q_ref.shape[1] // HEAD_DIM
+    count = q_ref.shape[0] // size
+    cut = [slice(i * size, (i + 1) * size) for i in range(count)]
+
+    def back(d_turned, pre, at):
+        d = d_turned[:, :HEAD_DIM] * cos[at] + d_turned[:, HEAD_DIM:] * sin[at]
+        return (d.astype(BF16).astype(F32) * swish_slope(pre[at])).astype(BF16)
+
+    for part in range(each):
+        cols = columns(part)
+        slope = head_slope(pl.program_id(0) * each + part)
+        q_pre, k_pre = q_ref[:, cols], k_ref[:, cols]
+        rq = turned(rounded_swish(q_pre), cos, sin).astype(BF16)
+        rk = turned(rounded_swish(k_pre), cos, sin).astype(BF16)
+        value = v_ref[:, cols].astype(BF16)
+        d_mix = dm_ref[:, cols]
+        d_rq = [0.0] * count
+        d_rk = [0.0] * count
+        d_value = [0.0] * count
+        for i in range(count):
+            for j in range(i + 1):
+                decay = block_decay(col, row, i, j, size, slope)
+                scores = (dot(rq[cut[i]], rk[cut[j]], NT) * decay).astype(BF16)
+                d_scores = (dot(d_mix[cut[i]], value[cut[j]], NT) * decay).astype(BF16)
+                d_value[j] += dot(scores, d_mix[cut[i]], TN)
+                d_rq[i] += dot(d_scores, rk[cut[j]], NN)
+                d_rk[j] += dot(d_scores, rq[cut[i]], TN)
+        for i in range(count):
+            dq_ref[cut[i], cols] = back(d_rq[i], q_pre, cut[i])
+            dk_ref[cut[i], cols] = back(d_rk[i], k_pre, cut[i])
+            dv_ref[cut[i], cols] = d_value[i].astype(BF16)
+
+
+def stacked(refs):
+    return jnp.concatenate([r[...] for r in refs], axis=0)
+
+
+def restored(order, value, out):
+    width = value.shape[1] // 8
+    for k, at in enumerate(BITS_Y):
+        out[:, at_block(order, at, width)] = value[:, k * width : (k + 1) * width]
+
+
+def project_body(order, h_ref, *refs):
+    h = h_ref[...]
+    refs[16][...] = dot(h, stacked(refs[:8]), NN)
+    refs[17][...] = dot(h, stacked(refs[8:16]), NN)
+
+
+def out_mid_body(order, mix_ref, u_ref, x_ref, *refs):
+    gated_ref, mid_ref, plain = refs[16], refs[17], refs[-1]
+    mix = mix_ref[...].astype(F32)
+    u = u_ref[...]
+    scale = lax.rsqrt(jnp.mean(mix * mix, axis=-1, keepdims=True) + EPS)
+    plain[...] = (mix * scale * (u * sigmoid(u))).astype(BF16)
+    spread(order, plain, (refs[-2], gated_ref))
+    gated = refs[-2][...]
+    half = x_ref.shape[1] // 2
+    low = x_ref[:, :half].astype(F32) + dot(gated, stacked(refs[:8]), NN)
+    high = x_ref[:, half:].astype(F32) + dot(gated, stacked(refs[8:16]), NN)
+    mid_ref[:, :half] = low
+    mid_ref[:, half:] = high
+    power = jnp.sum(low * low, axis=-1, keepdims=True) + jnp.sum(high * high, axis=-1, keepdims=True)
+    scale = lax.rsqrt(power / x_ref.shape[1] + EPS)
+    plain[:, :half] = (low * scale).astype(BF16)
+    plain[:, half:] = (high * scale).astype(BF16)
+    spread(order, plain, refs[18:20])
+
+
+def left_right_body(order, h_ref, *refs):
+    left_ref, right_ref, product_ref = refs[16:19]
+    h = h_ref[...]
+    left = dot(h, stacked(refs[:8]), NN)
+    right = dot(h, stacked(refs[8:16]), NN)
+    left_ref[...] = left.astype(BF16)
+    right_ref[...] = right.astype(BF16)
+    product_ref[...] = (left * right).astype(BF16)
+
+
+def down_grad_body(rows, order, product_ref, c_ref, *refs):
+    outs, held, sems = refs[:4], refs[4], refs[5]
+    step = pl.program_id(0)
+    size = product_ref.shape[1]
+    held[pl.ds(pl.multiple_of(step * size, size), size), :] = dot(
+        product_ref[...], c_ref[...], TN, BF16
+    )
+
+    @pl.when(step == pl.num_programs(0) - 1)
+    def _():
+        half = held.shape[1] // 2
+        copies = []
+        for side, bits in enumerate((BITS_X, BITS_Y)):
+            for k, bit in enumerate(bits):
+                copies.append(
+                    pltpu.make_async_copy(
+                        held.at[at_block(order, bit, rows), side * half : (side + 1) * half],
+                        outs[2 * (k // 4) + side].at[(k % 4) * rows : (k % 4 + 1) * rows, :],
+                        sems.at[side, k],
+                    )
+                )
+        run_copies(copies)
+
+
+def feed_back_body(
+    rows, order, left_ref, right_ref, product_ref, hx_ref, hy_ref, c_ref, mid_ref, *refs
+):
+    weights, downs = refs[:16], refs[16:32]
+    keep_l, send_l, keep_r, send_r, d_mid_ref, d_branch_ref, act_ref = refs[32:39]
+    down, grad, total, held_l, held_r, sems = refs[39:]
+    step = pl.program_id(0)
+
+    @pl.when(step == 0)
+    def _():
+        half = down.shape[1] // 2
+        run_copies(
+            [
+                pltpu.make_async_copy(
+                    downs[8 * side + k],
+                    down.at[at_block(order, at, rows), side * half : (side + 1) * half],
+                    sems.at[side, k],
+                )
+                for side in range(2)
+                for k, at in enumerate(BITS_Y)
+            ]
+        )
+        held_l[...] = jnp.zeros_like(held_l)
+        held_r[...] = jnp.zeros_like(held_r)
+
+    size = left_ref.shape[1]
+    last = pl.num_programs(0) - 2
+
+    def down_rows(block):
+        return down[pl.ds(pl.multiple_of(block * size, size), size), :]
+
+    d_left, d_right = held_l[...], held_r[...]
+    half = hx_ref.shape[1] // 2
+    g_left = dot(hx_ref[...], d_left, TN, BF16)
+    keep_l[...] = g_left[:half]
+    send_l[...] = g_left[half:]
+    g_right = dot(hy_ref[...], d_right, TN, BF16)
+    keep_r[...] = g_right[:half]
+    send_r[...] = g_right[half:]
+    total[...] += dot(product_ref[...], down_rows(jnp.maximum(step - 1, 0)), NN)
+    grad[...] += dot(d_left, stacked(weights[:8]), NT) + dot(d_right, stacked(weights[8:]), NT)
+
+    grad_product = dot(c_ref[...], down_rows(jnp.minimum(step, last)), NT)
+    held_l[...] = (grad_product * right_ref[...].astype(F32)).astype(BF16)
+    held_r[...] = (grad_product * left_ref[...].astype(F32)).astype(BF16)
+
+    @pl.when(step == 0)
+    def _():
+        grad[...] = jnp.zeros_like(grad)
+        total[...] = jnp.zeros_like(total)
+
+    @pl.when(step == pl.num_programs(0) - 1)
+    def _():
+        mid = mid_ref[...]
+        act_ref[...] = (mid + total[...]).astype(BF16)
+        restored(order, grad[...], total)
+        g = total[...]
+        scale = lax.rsqrt(jnp.mean(mid * mid, axis=-1, keepdims=True) + EPS)
+        inner = jnp.mean(g * mid, axis=-1, keepdims=True) * (scale * scale * scale)
+        d_mid = c_ref[...].astype(F32) + scale * g - mid * inner
+        d_mid_ref[...] = d_mid
+        d_branch_ref[...] = d_mid.astype(BF16)
+
+
+def gate_out_back_body(order, d_ref, mix_ref, u_ref, *refs):
+    du_ref, dm_ref, held = refs[16:]
+    half = d_ref.shape[1] // 2
+    d = d_ref[...]
+    restored(
+        order, dot(d[:, :half], stacked(refs[:8]), NT) + dot(d[:, half:], stacked(refs[8:16]), NT), held
+    )
+    dg = held[...]
+    mix = mix_ref[...].astype(F32)
+    u = u_ref[...]
+    sig = sigmoid(u)
+    scale = lax.rsqrt(jnp.mean(mix * mix, axis=-1, keepdims=True) + EPS)
+    du_ref[...] = (dg * mix * scale * (sig * (1.0 + u * (1.0 - sig)))).astype(BF16)
+    dn = dg * (u * sig)
+    inner = jnp.mean(dn * mix, axis=-1, keepdims=True) * (scale * scale * scale)
+    dm_ref[...] = (scale * dn - mix * inner).astype(BF16)
+
+
+def in_back_body(order, x_ref, d_mid_ref, *refs):
+    ds, weights, out, grad, held = refs[:4], refs[4:36], refs[36], refs[37], refs[38]
+    step = pl.program_id(0)
+    value = dot(ds[0][...], stacked(weights[:8]), NT)
+    for i in (1, 2, 3):
+        value += dot(ds[i][...], stacked(weights[8 * i : 8 * i + 8]), NT)
+
+    @pl.when(step == 0)
+    def _():
+        grad[...] = value
+
+    @pl.when(step > 0)
+    def _():
+        grad[...] += value
+
+    @pl.when(step == pl.num_programs(0) - 1)
+    def _():
+        restored(order, grad[...], held)
+        g = held[...]
+        x = x_ref[...].astype(F32)
+        scale = lax.rsqrt(jnp.mean(x * x, axis=-1, keepdims=True) + EPS)
+        inner = jnp.mean(g * x, axis=-1, keepdims=True) * (scale * scale * scale)
+        out[...] = d_mid_ref[...] + scale * g - x * inner
+
+
+def weight_grads_body(count, order, *refs):
+    for i in range(count):
+        g = dot(refs[2 * i][...], refs[2 * i + 1][...], TN, BF16)
+        half = g.shape[0] // 2
+        refs[2 * count + 2 * i][...] = g[:half]
+        refs[2 * count + 2 * i + 1][...] = g[half:]
+
+
 class Chain:
     def __init__(self, fresh, factor, forward, parts):
         self.fresh, self.factor, self.forward, self.parts = fresh, factor, forward, parts
@@ -465,13 +799,12 @@
 
 
 class Layer:
-    def __init__(self, tokens, doc_lengths, cotangent, by_hand):
+    def __init__(self, tokens, doc_lengths, cotangent):
         seqs, length, width = tokens.shape
         self.seqs, self.length, self.width, self.count = seqs, length, width, seqs * length
-        self.by_hand = by_hand
         self.here = lax.axis_index("rows")
         self.place = lax.axis_index("heads")
-        self.order = jnp.stack([self.here ^ b for b in range(8)]).astype(jnp.int32)
+        self.order = places(self.here, self.place)
         self.x = tokens.reshape(self.count, width)
         self.dy = cotangent.reshape(self.count, width)
 
@@ -521,25 +854,18 @@
         got = call(body, (self.seqs,), self.order, ins, outs)
         return [g.reshape(self.count, self.width) if g.shape == shape else g for g in got]
 
-    def copies(self):
-        return [BF16] * (3 if self.by_hand else 1)
-
     def norm(self):
-        blocks = 8 if self.by_hand else 1
-        return self.rows(functools.partial(norm_body, blocks), [self.x], self.copies())
+        return self.rows(norm_body, [self.x], [BF16])
 
     def fresh(self, k_pre, v_pre):
         return self.seqwise(fresh_body, [k_pre, v_pre] + self.turn + [self.tail], [self.states])[0]
 
     def mix(self, q_pre, k_pre, v_pre, u_pre, state_in):
         ins = [q_pre, k_pre, v_pre, u_pre] + self.turn + self.masks + [(state_in, self.state)]
-        return self.seqwise(mix_body, ins, [BF16] + self.copies())
+        return self.seqwise(mix_body, ins, [BF16, BF16])
 
     def mid(self, branch):
-        blocks = 8 if self.by_hand else 1
-        return self.rows(
-            functools.partial(mid_body, blocks), [self.x, branch], [F32] + self.copies()
-        )
+        return self.rows(mid_body, [self.x, branch], [F32, BF16])
 
     def mid_back(self, x_mid, grad):
         return self.rows(norm_back_body, [x_mid, self.dy, grad], [F32, BF16])
@@ -608,237 +934,305 @@
     return (activations, input_grad) + tuple(gradient(lhs, d) for lhs, d in pairs)
 
 
-def reducing(terms):
-    sends, keeps = [], []
-    for lhs, d, _ in terms:
-        half = lhs.shape[1] // 2
-        sends.append(dot(lhs[:, half:], d, TN, BF16))
-
-        def keep(theirs, lhs=lhs, d=d, half=half):
-            return (dot(lhs[:, :half], d, TN) + theirs.astype(F32)).astype(BF16)
-
-        keeps.append(keep)
-    return Reduce(sends, keeps, [b for _, _, b in terms])
-
-
-def reducing_rows(whole, here):
-    rows, half = whole.shape[0] // 8, whole.shape[1] // 2
-
-    def block(side, bits):
-        cut = whole[:, side * half : (side + 1) * half]
-        return jnp.concatenate(
-            [lax.dynamic_slice_in_dim(cut, (here ^ b) * rows, rows, axis=0) for b in bits], axis=0
-        )
-
-    sends, keeps = [], []
-    for side, bits in enumerate((BITS_X, BITS_Y)):
-        sends.append(block(side, bits[4:]))
-
-        def keep(theirs, side=side, bits=bits):
-            return add(block(side, bits[:4]), theirs)
-
-        keeps.append(keep)
-    return Reduce(sends, keeps, [2, 4])
-
-
-def stepwise(layer, heads_count, weights):
+class Row:
+    def __init__(self, doc_lengths, length, width, here, head):
+        self.length, self.width = length, width
+        self.order = places(here, head)
+        lengths = lax.dynamic_index_in_dim(doc_lengths, head, 0, keepdims=False)
+        ends = jnp.cumsum(lengths, dtype=jnp.int32)[:-1]
+        positions = jnp.arange(length, dtype=jnp.int32)
+        ids = jnp.sum((positions[:, None] >= ends[None, :]).astype(jnp.int32), axis=-1)
+        theta = jnp.exp(-math.log(10000.0) * jnp.arange(HEAD_DIM, dtype=F32) / HEAD_DIM)
+        angle = positions.astype(F32)[:, None] * theta[None, :]
+
+        def whole(rows, cols):
+            return pl.BlockSpec((rows, cols), lambda *_: (0, 0))
+
+        table = whole(length, HEAD_DIM)
+        self.extra = [
+            (jnp.cos(angle), table), (jnp.sin(angle), table),
+            (ids[:, None], whole(length, 1)), (ids[None, :], whole(1, length)),
+        ]
+        self.heads = pl.BlockSpec((length, 2 * HEAD_DIM), lambda h, *_: (0, h))
+        self.wide = rows_spec(min(length, 256), width)
+        self.all = whole(length, width)
+        self.block = math.gcd(length, 256)
+        self.flops = 2 * length * width * width
+
+    def norm(self, x):
+        return self.by_rows(row_norm_body, [(x, self.wide)], [], [BF16, BF16], [BF16])
+
+    def pieces(self, group, half, width, column=None, offset=0):
+        rows = group.pieces[0].shape[0]
+        if column is None:
+            spec = pl.BlockSpec((rows, width), lambda i, *_: (0, offset + i))
+        else:
+            spec = pl.BlockSpec((rows, width), lambda *_: (0, column))
+        return [(a, spec) for a in group.all(half)]
+
+    def project(self, h, att):
+        half = self.width // 2
+        out = (self.length, 2 * self.width), F32, pl.BlockSpec((self.length, half), lambda i, *_: (0, i))
+        return call(
+            project_body, (4,), self.order,
+            [(h, self.all)] + self.pieces(att, 0, half) + self.pieces(att, 1, half), [out, out],
+            flops=4 * self.flops,
+        )
+
+    def column(self, block, offset=0):
+        return pl.BlockSpec((self.length, block), lambda i, *_: (0, offset + i))
+
+    def mix(self, qk, vu):
+        ins = [(qk, self.heads), (qk, self.column(2 * HEAD_DIM, HEADS // 2)), (vu, self.heads)]
+        return call(
+            functools.partial(row_mix_body, self.block), (HEADS // 2,), self.order, ins + self.extra,
+            [((self.length, self.width), BF16, self.heads)], flops=self.flops * 3 // 8,
+        )[0]
+
+    def mix_back(self, qk, vu, d_mix):
+        ins = [(qk, self.heads), (qk, self.column(2 * HEAD_DIM, HEADS // 2)), (vu, self.heads)]
+        return call(
+            functools.partial(row_mix_back_body, self.block), (HEADS // 2,), self.order,
+            ins + [(d_mix, self.heads)] + self.extra,
+            [((self.length, self.width), BF16, self.heads)] * 3, flops=self.flops,
+        )
+
+    def out_weights(self, att):
+        half = self.width // 2
+        return self.pieces(att, 0, half, 4) + self.pieces(att, 1, half, 4)
+
+    def by_rows(self, body, ins, weights, types, scratch):
+        step = self.wide.block_shape[0]
+        return call(
+            body, (self.length // step,), self.order, ins + weights,
+            [((self.length, self.width), t, self.wide) for t in types],
+            scratch=[pltpu.VMEM((step, self.width), t) for t in scratch], flops=self.flops,
+        )
+
+    def gate_spec(self):
+        return pl.BlockSpec(self.wide.block_shape, lambda i, *_: (i, 1))
+
+    def out_mid(self, mix, vu, x, att):
+        return self.by_rows(
+            out_mid_body, [(mix, self.wide), (vu, self.gate_spec()), (x, self.wide)],
+            self.out_weights(att), [BF16, F32, BF16, BF16], [BF16, BF16],
+        )
+
+    def gate_out_back(self, d_branch, mix, vu, att):
+        return self.by_rows(
+            gate_out_back_body, [(d_branch, self.wide), (mix, self.wide), (vu, self.gate_spec())],
+            self.out_weights(att), [BF16, BF16], [F32],
+        )
+
+    def left_right(self, h, ff):
+        inner = ff.pieces[0].shape[1]
+        block = math.gcd(inner, 1408)
+        return call(
+            left_right_body, (inner // block,), self.order,
+            [(h, self.all)] + self.pieces(ff, 0, block) + self.pieces(ff, 1, block),
+            [((self.length, inner), BF16, self.column(block))] * 3,
+            flops=2 * self.flops * inner // self.width,
+        )
+
+    def down_grad(self, product, c):
+        inner, half = product.shape[1], self.width // 2
+        block = math.gcd(inner, 1408)
+        rows = inner // 8
+        got = call(
+            functools.partial(down_grad_body, rows), (inner // block,), self.order,
+            [(product, self.column(block)), (c, self.all)], [((4 * rows, half), BF16, HBM)] * 4,
+            scratch=[pltpu.VMEM((inner, self.width), BF16), pltpu.SemaphoreType.DMA((2, 8))],
+            flops=self.flops * inner // self.width,
+        )
+        return Reduce(self.order, got[2:], got[:2], [2, 4])
+
+    def feed_back(self, left, right, product, h_x, h_y, c, x_mid, ff, down):
+        inner, rows = ff.pieces[0].shape[1], down.pieces[0].shape[0]
+        block = math.gcd(inner, 256)
+        steps = inner // block
+
+        def now(rows):
+            return pl.BlockSpec((rows, block), lambda i, *_: (0, jnp.minimum(i, steps - 1)))
+
+        def before(rows):
+            return pl.BlockSpec((rows, block), lambda i, *_: (0, jnp.maximum(i - 1, 0)))
+
+        full = (self.length, self.width)
+        weights = [
+            (a, before(ff.pieces[0].shape[0])) for a in ff.all(0) + ff.all(1)
+        ]
+        return call(
+            functools.partial(feed_back_body, rows), (steps + 1,), self.order,
+            [(left, now(self.length)), (right, now(self.length)), (product, before(self.length))]
+            + [(a, self.all) for a in (h_x, h_y, c, x_mid)]
+            + weights + [(a, HBM) for a in down.all(0) + down.all(1)],
+            [((self.width // 2, inner), BF16, before(self.width // 2))] * 4
+            + [(full, F32, self.all), (full, BF16, self.all), (full, BF16, self.all)],
+            scratch=[pltpu.VMEM((inner, self.width), BF16)] + [pltpu.VMEM(full, F32)] * 2
+            + [pltpu.VMEM((self.length, block), BF16)] * 2 + [pltpu.SemaphoreType.DMA((2, 8))],
+            flops=6 * self.flops * inner // self.width,
+        )
+
+    def in_back(self, x, d_mid, ds, att):
+        half = self.width // 2
+        weights = []
+        for which, offset in ((0, 0), (0, 2), (1, 0), (1, 2)):
+            weights += self.pieces(att, which, half, offset=offset)
+        full = (self.length, self.width)
+        return call(
+            in_back_body, (2,), self.order,
+            [(x, self.all), (d_mid, self.all)] + [(d, self.column(half)) for d in ds] + weights,
+            [(full, F32, self.all)], scratch=[pltpu.VMEM(full, F32)] * 2, flops=4 * self.flops,
+        )[0]
+
+    def weight_grads(self, pairs, bits):
+        half = self.width // 2
+        tall = pl.BlockSpec((half, half), lambda i, *_: (0, i))
+        ins = []
+        for lhs, d in pairs:
+            ins += [(lhs, self.all), (d, self.column(half))]
+        got = call(
+            functools.partial(weight_grads_body, len(pairs)), (2,), self.order, ins,
+            [((half, self.width), BF16, tall)] * (2 * len(pairs)), flops=len(pairs) * self.flops,
+        )
+        return Reduce(self.order, got[1::2], got[::2], bits)
+
+
+def stepwise(tokens, doc_lengths, cotangent, weights):
     w_query, w_key, w_value, w_gate, w_out, w_left, w_right, w_down = weights
-    width, inner = layer.width, w_left.shape[1]
-    half = width // 2
-    order, here, place = layer.order, layer.here, layer.place
+    size, width = tokens.shape[1:]
+    length, half = 4 * size, width // 2
+    here, head = lax.axis_index("rows"), lax.axis_index("heads")
+    row = Row(doc_lengths, length, width, here, head)
+    order = row.order
     v = types.SimpleNamespace()
     clock = Clock(order)
     tick = clock.tick
 
-    pair = [(0, 0, width), (width, 0, width)]
-    triple = [
-        (0, 0, width), (width, 0, half), (width + half, 0, width), (2 * width + half, half, half),
-    ]
-    kv = Gather(pack(pair, [w_key, w_value], order), pair, (0, 1), (width, width))
-    kv.first()
-    v.h = layer.norm()
-    v.qu = pack(triple, [w_query, w_out, w_gate, w_out], order)
-    ff_pair = [(0, 0, inner), (inner, 0, inner)]
-    v.ff = pack(ff_pair, [w_left, w_right], order)
-    tick((kv, "near"), (v, "qu"), (v, "ff"), (v, "h"))
-    kv.second()
-    qu = Gather(v.qu, triple, (0, 2, 1, 2), (width, width, width))
-    qu.first()
-    ff = Gather(v.ff, ff_pair, (0, 1), (inner, inner))
+    def exchanged(a):
+        return lax.all_to_all(a.reshape(4, size, width), "heads", 0, 0, tiled=True)
+
+    def whole_row(a):
+        return exchanged(a).reshape(length, width)
+
+    att = Gather(
+        pack(
+            order, [w_query, w_key, w_value, w_gate, w_out],
+            [[(0, 0, width), (1, 0, width), (4, 0, half)], [(2, 0, width), (3, 0, width), (4, half, half)]],
+        )
+    )
+    att.first()
+    v.x = whole_row(tokens)
+    v.down = pack(order, [w_down], [[(0, 0, half)], [(0, half, half)]])
+    v.ff = [w_left, w_right]
+    att.cross("pieces")
+    tick((v, "x"), (v, "down"), (att, "pieces_other"))
+    v.h = row.norm(v.x)
+    tick((att, "near_x"), (att, "near_y"), (v, "ff"), (v, "down"), (v, "h"))
+    att.second()
+    ff = Gather(v.ff)
     ff.first()
-    kv.cross_first()
-    tick((kv, "far"))
-    kv.cross_second()
-    full_k, full_v = kv.whole(order)
-    h_in = v.h[0]
-    k_pre, v_pre = dot(h_in, full_k, NN), dot(h_in, full_v, NN)
-    v.fresh = layer.fresh(k_pre, v_pre)
-    tick((v, "fresh"))
-    forward = Chain(v.fresh, layer.factor, True, heads_count)
-    forward.begin()
-
-    tick(forward.arrivals(1), (qu, "near"))
-    forward.go_on(1)
-    qu.second()
-    v.down = w_down
-    down = Gather(v.down, [(0, 0, half), (half, half, half)], (0, 0), (width,))
-    tick((down, "piece"))
+    att.cross("near_x", "near_y")
+    tick((att, "far"), (att, "near_x_other"), (att, "near_y_other"))
+    att.cross("far")
+    tick((att, "far_other"), (v, "h"))
+    v.qk, v.vu = row.project(v.h[0], att)
+    tick((v, "qk"), (v, "vu"))
+    v.c = cotangent
+    tick((v, "c"))
+    v.c = whole_row(v.c)
+    v.mix = row.mix(v.qk, v.vu)
+    tick((v, "mix"), (ff, "near_x"), (ff, "near_y"), (ff, "pieces"), (v, "down"))
+    ff.second()
+    ff.cross("pieces", "near_x", "near_y")
+    down = Gather(v.down)
     down.first()
-    qu.cross_first()
-    tick(forward.arrivals(2))
-    forward.go_on(2)
-    tick(forward.arrivals(3), (ff, "near"))
-    forward.go_on(3)
-    ff.second()
-    ff.cross_first()
-    tick(forward.arrivals(4), (qu, "far"))
-    forward.go_on(4)
-    qu.cross_second()
-    full_q, full_u, full_out = qu.whole(order)
-    v.q_pre, v.u_pre = dot(h_in, full_q, NN), dot(h_in, full_u, NN)
-    tick(forward.arrivals(5), (down, "near"), (v, "q_pre"), (v, "u_pre"))
-    forward.go_on(5)
+    gated, v.x_mid, *v.h_mid = row.out_mid(v.mix, v.vu, v.x, att)
+    tick((v, "x_mid"), (v, "h_mid"), (v, "c"), (ff, "far"))
+    ff.cross("far")
+    tick((v, "c"), (ff, "far_other"), (v, "h_mid"))
+
+    v.left, v.right, v.product = row.left_right(v.h_mid[0], ff)
+    tick((v, "left"), (v, "right"), (v, "product"), (down, "near_x"), (down, "near_y"), (down, "pieces"))
     down.second()
-    down.cross_first()
-    tick(forward.arrivals(6))
-    forward.go_on(6)
-    state_in = forward.result()
-    v.mix, *v.gated = layer.mix(v.q_pre, k_pre, v_pre, v.u_pre, state_in)
-    tick((v, "mix"), (v, "gated"), (ff, "far"))
-    ff.cross_second()
-    branch = dot(v.gated[0], full_out, NN)
-    v.x_mid, *v.h_mid = layer.mid(branch)
-    full_left, full_right = ff.whole(order)
-    tick((v, "x_mid"), (v, "h_mid"), (down, "far"))
-    down.cross_second()
-
-    h_mid = v.h_mid[0]
-    v.left, v.right = dot(h_mid, full_left, NN), dot(h_mid, full_right, NN)
-    v.product = (v.left * v.right).astype(BF16)
-    tick((v, "left"), (v, "right"), (v, "product"))
-    (full_down,) = down.whole(order)
-    r_down = reducing_rows(dot(v.product, layer.dy, TN, BF16), here)
-    tick((r_down, "sends"))
+    down.cross("pieces", "near_x", "near_y")
+    r_down = row.down_grad(v.product, v.c)
+    tick((r_down, "sends"), (down, "far"), (v, "left"))
     r_down.core()
-    grad_product = dot(layer.dy, full_down, NT)
-    v.d_left = (grad_product * v.right).astype(BF16)
-    v.d_right = (grad_product * v.left).astype(BF16)
-    tick((v, "d_left"), (v, "d_right"), (r_down, "theirs"))
+    down.cross("far")
+    tick((r_down, "theirs"), (down, "far_other"), (v, "left"))
     r_down.join()
-    tick((r_down, "totals"), (v, "d_left"), (v, "d_right"))
+    tick((r_down, "totals"), (v, "left"))
     r_down.first()
-    v.d_mid, v.d_branch = layer.mid_back(
-        v.x_mid, dot(v.d_left, full_left, NT) + dot(v.d_right, full_right, NT)
-    )
-    v.d_u, v.d_mix, v.d_fresh = layer.gate_back(
-        v.q_pre, v.u_pre, v.mix, dot(v.d_branch, full_out, NT)
-    )
-    tick((v, "d_fresh"), (v, "d_u"), (v, "d_mix"), (v, "d_branch"), (v, "d_mid"), (v, "d_left"), (v, "d_right"))
-
-    backward = Chain(v.d_fresh, layer.factor, False, heads_count)
-    backward.begin()
-    r_ff = reducing([(v.h_mid[1], v.d_left, 2), (v.h_mid[2], v.d_right, 4)])
-    tick((r_ff, "sends"), (r_down, "got"))
+    keep_l, send_l, keep_r, send_r, v.d_mid, v.d_branch, v.act = row.feed_back(
+        v.left, v.right, v.product, v.h_mid[1], v.h_mid[0], v.c, v.x_mid, ff, down
+    )
+    r_ff = Reduce(order, [send_l, send_r], [keep_l, keep_r], [2, 4])
+    tick((r_ff, "sends"), (v, "d_mid"), (v, "d_branch"), (v, "act"), (r_down, "got"))
     r_ff.core()
     r_down.join_first()
-    tick(backward.arrivals(1), (r_down, "parts"), (v, "d_mix"))
-    backward.go_on(1)
+    tick((r_down, "parts"), (v, "d_branch"), (v, "act"))
     r_down.second()
-    v.d_q, v.dk_near, v.dv_near = layer.mix_back(v.q_pre, k_pre, v_pre, v.d_mix, state_in)
-    tick(backward.arrivals(2), (r_ff, "theirs"), (v, "d_q"), (v, "dk_near"), (v, "dv_near"), (v, "d_u"))
-    backward.go_on(2)
+    v.act = exchanged(v.act)
+    v.d_u, v.d_mix = row.gate_out_back(v.d_branch, v.mix, v.vu, att)
+    tick((r_ff, "theirs"), (v, "d_u"), (v, "d_mix"), (r_down, "got_last"))
     r_ff.join()
-    tick((r_ff, "totals"))
+    tick((r_ff, "totals"), (v, "d_mix"))
     r_ff.first()
-    tick(backward.arrivals(3), (v, "d_branch"), (v, "d_u"))
-    backward.go_on(3)
-    r_out = reducing([(v.gated[1], v.d_branch, 2), (v.h[2], v.d_u, 4)])
-    tick((r_out, "sends"), (r_down, "got_last"))
-    r_out.core()
-    r_down.join_second()
-    s_down = Settle([jnp.concatenate(r_down.sums, axis=1)], place)
-    tick(backward.arrivals(4), (r_out, "theirs"), (v, "d_q"))
-    backward.go_on(4)
-    r_out.join()
-    r_query = reducing([(v.h[2], v.d_q, 4)])
-    tick((r_out, "totals"), (r_query, "sends"))
-    r_out.first()
-    r_query.core()
-    tick(backward.arrivals(5), (r_query, "theirs"), (v, "product"))
-    backward.go_on(5)
-    r_query.join()
-    tick((r_query, "totals"))
-    r_query.first()
-    v.activations = (v.x_mid + dot(v.product, full_down, NN)).astype(BF16)
-    tick(backward.arrivals(6), (v, "activations"), (r_ff, "got"))
-    backward.go_on(6)
-    d_state = backward.result()
+    v.d_q, v.d_k, v.d_v = row.mix_back(v.qk, v.vu, v.d_mix)
+    tick((v, "d_q"), (v, "d_k"), (v, "d_v"), (v, "act"), (r_down, "own"), (r_down, "got_last"))
+    s_down = SettleWide(order, [jnp.concatenate(r_down.own, axis=1)], [jnp.concatenate(r_down.got_last, axis=1)])
+    tick((s_down, "out"), (s_down, "own"), (v, "d_q"))
+    s_down.pass_on(1)
+    r_att = row.weight_grads(
+        [(v.h[1], v.d_q), (v.h[0], v.d_k), (v.h[1], v.d_v), (v.h[0], v.d_u), (gated, v.d_branch)],
+        [2, 4, 2, 4, 2],
+    )
+    tick((r_att, "sends"), (r_ff, "got"), (s_down, "got"))
+    r_att.core()
     r_ff.join_first()
-    v.d_k, v.d_v = layer.state_back(k_pre, v_pre, v.dk_near, v.dv_near, d_state)
-    tick((r_ff, "parts"), (v, "d_k"), (v, "d_v"))
+    tick((r_ff, "parts"), (r_att, "theirs"), (s_down, "got"))
     r_ff.second()
-    r_key = reducing([(v.h[1], v.d_k, 2), (v.h[2], v.d_v, 4)])
-    tick((r_key, "sends"), (r_out, "got"))
-    r_key.core()
-    r_out.join_first()
-    tick((r_key, "theirs"), (r_out, "parts"))
-    r_out.second()
-    r_key.join()
-    tick((r_key, "totals"), (r_query, "got"), (v, "d_q"))
-    r_key.first()
-    r_query.join_first()
-    tick((r_query, "parts"), (v, "d_q"), (s_down, "out"))
-    r_query.second()
-    s_down.pass_on(1)
-    v.grad_in = (
-        dot(v.d_q, full_q, NT) + dot(v.d_u, full_u, NT)
-        + dot(v.d_k, full_k, NT) + dot(v.d_v, full_v, NT)
-    )
-    tick((v, "grad_in"), (r_ff, "got_last"), (s_down, "got"))
+    r_att.join()
+    s_down.join()
+    tick((r_att, "totals"), (s_down, "out"), (v, "d_q"))
+    r_att.first()
+    s_down.pass_on(2)
+    v.input_grad = row.in_back(v.x, v.d_mid, [v.d_q, v.d_k, v.d_v, v.d_u], att)
+    tick((v, "input_grad"), (r_ff, "got_last"), (s_down, "got"))
     r_ff.join_second()
-    s_ff = Settle(r_ff.sums, place)
-    s_down.join()
-    tick((s_ff, "out"), (s_ff, "own"), (s_down, "out"))
+    s_ff = Settle(r_ff.sums, head)
+    tick((s_ff, "out"), (s_ff, "own"), (v, "input_grad"))
     s_ff.pass_on(1)
-    s_down.pass_on(2)
-    v.input_grad = layer.in_back(v.d_mid, v.grad_in)
-    tick((v, "input_grad"), (r_out, "got_last"), (r_query, "got_last"))
-    r_out.join_second()
-    r_query.join_second()
-    s_out = Settle(r_out.sums + r_query.sums, place)
-    tick((s_out, "out"), (r_key, "got"))
-    s_out.pass_on(1)
-    r_key.join_first()
-    tick((r_key, "parts"), (s_ff, "got"))
-    r_key.second()
+    tick((r_att, "got"), (v, "input_grad"))
+    r_att.join_first()
+    tick((r_att, "parts"), (s_ff, "got"), (v, "input_grad"))
+    r_att.second()
     s_ff.join()
-    tick((s_ff, "out"), (s_out, "got"))
+    (g_down,) = s_down.result()
+    tick((s_ff, "out"), (v, "input_grad"))
     s_ff.pass_on(2)
-    s_out.join()
-    tick((s_out, "out"), (r_key, "got_last"))
-    s_out.pass_on(2)
-    r_key.join_second()
-    s_key = Settle(r_key.sums, place)
-    tick((s_key, "out"))
-    s_key.pass_on(1)
-    tick((s_key, "got"), (s_down, "got"), (s_ff, "got"))
-    s_key.join()
-    tick((s_key, "out"), (s_out, "got"))
-    s_key.pass_on(2)
-    (g_down,) = s_down.result()
+    back = exchanged(v.input_grad.astype(BF16))
+    tick((r_att, "got_last"), (r_att, "own"))
+    s_att = SettleWide(order, r_att.own, r_att.got_last)
+    tick((s_att, "out"), (s_att, "own"))
+    s_att.pass_on(1)
+    tick((s_att, "got"), (s_ff, "got"))
+    s_att.join()
+    tick((s_att, "out"))
+    s_att.pass_on(2)
     g_left, g_right = s_ff.result()
-    g_out, g_gate, g_query = s_out.result()
-    g_key, g_value = s_key.result()
+    g_query, g_key, g_value, g_gate, g_out = s_att.result()
     return (
-        v.activations, v.input_grad, g_query, g_key, g_value, g_gate, g_out, g_left, g_right, g_down
+        v.act, back.astype(F32), g_query, g_key, g_value, g_gate, g_out, g_left, g_right, g_down
     )
 
 
 def on_device(rows_count, heads_count, tokens, doc_lengths, cotangent, *weights):
-    by_hand = rows_count == 8 and heads_count == 4
-    layer = Layer(tokens, doc_lengths, cotangent, by_hand)
-    run = stepwise if by_hand else plainly
-    activations, input_grad, *grads = run(layer, heads_count, weights)
+    if rows_count == 8 and heads_count == 4 and tokens.shape[0] == 4:
+        return stepwise(tokens, doc_lengths, cotangent, weights)
+    layer = Layer(tokens, doc_lengths, cotangent)
+    activations, input_grad, *grads = plainly(layer, heads_count, weights)
     return (activations.reshape(tokens.shape), input_grad.reshape(tokens.shape), *grads)
 
 

time: 523 us -> 428 us (0.82); the launches traced: 514 us -> 426 us
  Pallas kernels: 74.5 us -> 179 us
  matrix products: 85.5 us -> 0 us
  other arithmetic: 46.3 us -> 11.6 us
  waiting for transfers between devices: 166 us -> 133 us
  local copies, waits for them, and re-layouts: 50.6 us -> 27.1 us
  starting transfers between devices: 88.1 us -> 74.8 us
    pallas_call x16 -> x25, Pallas kernels: 74.5 us -> 179 us  [call(): pl.pallas_call(body, grid_spec=pltpu.PrefetchScalarGridSpec(num_scalar_pr...]
    dot_general x31 -> x0, matrix products: 85.5 us -> none  [dot(): lax.dot_general(a, b, (dims, ((), ())), preferred_element_type=F32)]
    ppermute x24 -> x0, waiting for transfers between devices: 71.9 us -> none  [pass_on(): self.got[s].append(lax.ppermute(self.now[s], 'heads', [pair]))]
    ppermute x24 -> x0, starting transfers between devices: 34.2 us -> none  [pass_on(): self.got[s].append(lax.ppermute(self.now[s], 'heads', [pair]))]
    ppermute x63 -> x69, waiting for transfers between devices: 57.9 us -> 87.5 us  [swap(): return lax.ppermute(value, 'rows', [(i, i ^ bit) for i in range(size)])]
    all_to_all x0 -> x4, starting transfers between devices: none -> 19.6 us  [exchanged(): return lax.all_to_all(a.reshape(4, size, width), 'heads', 0, 0, tiled=True)]
    convert_element_type x23 -> x3, other arithmetic: 20.6 us -> 2.69 us  [the longest x1 1.57 us: stepwise(): back.astype(F32)]
    all_to_all x0 -> x4, waiting for transfers between devices: none -> 14.8 us  [exchanged(): return lax.all_to_all(a.reshape(4, size, width), 'heads', 0, 0, tiled=True)]
  transfers between devices with their start and end apart: 95 -> 79, of which waited for: 28 -> 34; matrix products, arithmetic and copies ran while one was open for 28% -> 4% of each run, Pallas kernels for 12% -> 42%
where the time goes in v2:
time: 428 us; the launch traced here: 426 us
  Pallas kernels  179 us (42%)
  waiting for transfers between devices  133 us (31%)
  starting transfers between devices  74.8 us (17%)
  local copies, waits for them, and re-layouts  27.1 us (6%)
  other arithmetic  11.6 us (3%)
    pallas_call x25, Pallas kernels, call(): pl.pallas_call(body, grid_spec=pltpu.PrefetchScalarGridSpec(num_scalar_pr...  179 us
    ppermute x69, waiting for transfers between devices, swap(): return lax.ppermute(value, 'rows', [(i, i ^ bit) for i in range(size)])  87.5 us
    ppermute x69, starting transfers between devices, swap(): return lax.ppermute(value, 'rows', [(i, i ^ bit) for i in range(size)])  45.6 us
    ppermute x6, waiting for transfers between devices, pass_on(): self.got = lax.ppermute(self.out, 'heads', [(i, i ^ bit) for i in range(4)])  30.3 us
    unnamed x121, local copies, waits for them, and re-layouts  19.8 us
    all_to_all x4, starting transfers between devices, exchanged(): return lax.all_to_all(a.reshape(4, size, width), 'heads', 0, 0, tiled=True)  19.6 us
    all_to_all x4, waiting for transfers between devices, exchanged(): return lax.all_to_all(a.reshape(4, size, width), 'heads', 0, 0, tiled=True)  14.8 us
    ppermute x6, starting transfers between devices, pass_on(): self.got = lax.ppermute(self.out, 'heads', [(i, i ^ bit) for i in range(4)])  9.59 us
  transfers between devices with their start and end apart: 79, of which 34 were waited for; matrix products, arithmetic and copies ran while one was open for 4% of the time, Pallas kernels for 42%

profile of v2, /device:TPU:0, one launch (start us, length us, event | category | flops | bytes accessed | tf_op | source)
XLA Modules:
  0.0 426.5 jit_solution(8134143772007348850)
XLA Ops:
  0.7 6.3 %all-to-all-start = ((bf16[4,128,1024]{2,1,0:T(8,128)(2,1)}), bf16[4,128,1024]{2,1,0:T(8,128)(2,1)S(1)}, u32[]{:S(2)}, u32[]{:S(2)}) async-start(bf16[4,128,1024]{2,1,0:T(8,128)(2,1)} %param.11), calls=%async_computation | async-start | bytes 2097152 | tf_op jit(solution)/shard_map/all_to_all | solution.py:1113
  17.9 14.8 %all-to-all-done = bf16[4,128,1024]{2,1,0:T(8,128)(2,1)S(1)} async-done(((bf16[4,128,1024]{2,1,0:T(8,128)(2,1)}), bf16[4,128,1024]{2,1,0:T(8,128)(2,1)S(1)}, u32[]{:S(2)}, u32[]{:S(2)}) %all-to-all-start) | async-done | bytes 1048608 | tf_op jit(solution)/shard_map/all_to_all | solution.py:1113
  37.2 5.1 %collective-permute-done.3.refs_10_.refs_22_.refs_30_ = bf16[128,2560]{1,0:T(8,128)(2,1)} collective-permute-done((bf16[128,2560]{1,0:T(8,128)(2,1)}, bf16[128,2560]{1,0:T(8,128)(2,1)}, u32[]{:S(2)}, u32[]{:S(2)}) %collective-permute-start.3) | collective-permute-done | bytes 655392 | tf_op jit(solution)/shard_map/ppermute | solution.py:38
  49.3 11.7 %collective-permute-done.6.refs_3_.refs_7_.refs_15_ = bf16[128,2560]{1,0:T(8,128)(2,1)} collective-permute-done((bf16[128,2560]{1,0:T(8,128)(2,1)}, bf16[128,2560]{1,0:T(8,128)(2,1)}, u32[]{:S(2)}, u32[]{:S(2)}) %collective-permute-start.6) | collective-permute-done | bytes 655392 | tf_op jit(solution)/shard_map/ppermute | solution.py:38
  63.9 5.1 %all-to-all-start.1 = ((bf16[4,128,1024]{2,1,0:T(8,128)(2,1)}), bf16[4,128,1024]{2,1,0:T(8,128)(2,1)}, u32[]{:S(2)}, u32[]{:S(2)}) async-start(bf16[4,128,1024]{2,1,0:T(8,128)(2,1)} %param.13), calls=%async_computation.1 | async-start | bytes 2097152 | tf_op jit(solution)/shard_map/all_to_all | solution.py:1113
  76.9 10.3 %shard_map.189 = (f32[512,2048]{1,0:T(8,128)}, f32[512,2048]{1,0:T(8,128)}) custom-call(s32[12]{0:T(128)} %stack.51.order, bf16[512,1024]{1,0:T(8,128)(2,1)} %get-tuple-element.288.h_ref.refs_2_.refs_6_, bf16[128,2560]{1,0:T(8,128)(2,1)} %get-tuple-element.268.refs_0_.refs_4_.refs_12_, bf16[128,2560]{1,0:T(8,128)(2,1)} %collective-permute-done.refs_1_.refs_5_.refs_13_, ...), custom_call_target="tpu_custom_call" | custom-call | flops 134217728 | bytes 622592 | tf_op jit(solution)/shard_map/pallas_call | solution.py:290
  87.2 8.4 %shard_map.190.mix_ref = bf16[512,1024]{1,0:T(8,128)(2,1)} custom-call(s32[12]{0:T(128)} %stack.51.order, f32[512,2048]{1,0:T(8,128)} %get-tuple-element.300.q_ref.k_ref, f32[512,2048]{1,0:T(8,128)} %get-tuple-element.300.q_ref.k_ref, f32[512,2048]{1,0:T(8,128)} %get-tuple-element.301.v_ref.u_ref, f32[512,128]{1,0:T(8,128)} %get-tuple-element.565.cos_ref, ...), custom_call_target="tpu_custom_call" | custom-call | flops 12582912 | bytes 442496 | tf_op jit(solution)/shard_map/pallas_call | solution.py:290
  95.6 7.5 %collective-permute-done.17.refs_10_ = bf16[128,2816]{1,0:T(8,128)(2,1)} collective-permute-done((bf16[128,2816]{1,0:T(8,128)(2,1)}, bf16[128,2816]{1,0:T(8,128)(2,1)}, u32[]{:S(2)}, u32[]{:S(2)}) %collective-permute-start.17) | collective-permute-done | bytes 720928 | tf_op jit(solution)/shard_map/ppermute | solution.py:38
  106.9 7.5 %shard_map.191 = (bf16[512,1024]{1,0:T(8,128)(2,1)}, f32[512,1024]{1,0:T(8,128)}, bf16[512,1024]{1,0:T(8,128)(2,1)}, bf16[512,1024]{1,0:T(8,128)(2,1)}) custom-call(s32[12]{0:T(128)} %stack.51.order, bf16[512,1024]{1,0:T(8,128)(2,1)} %shard_map.190.mix_ref, f32[512,2048]{1,0:T(8,128)} %get-tuple-element.301.v_ref.u_ref, bf16[512,1024]{1,0:T(8,128)(2,1)} %bitcast.23, ...), custom_call_target="tpu_custom_call" | custom-call | flops 33554432 | bytes 688128 | tf_op jit(solution)/shard_map/pallas_call | solution.py:290
  114.5 6.4 %collective-permute-done.18.refs_3_ = bf16[128,2816]{1,0:T(8,128)(2,1)S(1)} collective-permute-done((bf16[128,2816]{1,0:T(8,128)(2,1)}, bf16[128,2816]{1,0:T(8,128)(2,1)S(1)}, u32[]{:S(2)}, u32[]{:S(2)}) %collective-permute-start.18) | collective-permute-done | bytes 720928 | tf_op jit(solution)/shard_map/ppermute | solution.py:38
  130.8 12.3 %shard_map.192 = (bf16[512,2816]{1,0:T(8,128)(2,1)}, bf16[512,2816]{1,0:T(8,128)(2,1)}, bf16[512,2816]{1,0:T(8,128)(2,1)}) custom-call(s32[12]{0:T(128)} %stack.51.order, bf16[512,1024]{1,0:T(8,128)(2,1)} %get-tuple-element.322.h_ref.hy_ref, bf16[128,2816]{1,0:T(8,128)(2,1)} %refs_0_.5, bf16[128,2816]{1,0:T(8,128)(2,1)} %collective-permute-done.14.refs_1_, ...), custom_call_target="tpu_custom_call" | custom-call | flops 184549376 | bytes 663552 | tf_op jit(solution)/shard_map/pallas_call | solution.py:290
  146.9 8.4 %shard_map.193 = (bf16[1408,512]{1,0:T(8,128)(2,1)}, bf16[1408,512]{1,0:T(8,128)(2,1)}, bf16[1408,512]{1,0:T(8,128)(2,1)}, bf16[1408,512]{1,0:T(8,128)(2,1)}) custom-call(s32[12]{0:T(128)} %stack.51.order, bf16[512,2816]{1,0:T(8,128)(2,1)} %get-tuple-element.335.product_ref, bf16[512,1024]{1,0:T(8,128)(2,1)} %bitcast.17.c_ref), custom_call_target="tpu_custom_call" | custom-call | flops 92274688 | bytes 303104 | tf_op jit(solution)/shard_map/pallas_call | solution.py:290
  157.1 3.7 collective-permute-done.36.refs_23_
  175.0 34.8 %shard_map.195 = (bf16[512,2816]{1,0:T(8,128)(2,1)}, bf16[512,2816]{1,0:T(8,128)(2,1)}, bf16[512,2816]{1,0:T(8,128)(2,1)}, bf16[512,2816]{1,0:T(8,128)(2,1)}, f3...) custom-call(s32[12]{0:T(128)} %stack.51.order, ...), custom_call_target="tpu_custom_call" | custom-call | flops 553648128 | bytes 1466368 | tf_op jit(solution)/shard_map/pallas_call | solution.py:290
  211.6 4.0 shard_map.196
  215.6 4.5 %all-to-all-start.2 = ((bf16[4,128,1024]{2,1,0:T(8,128)(2,1)}), bf16[4,128,1024]{2,1,0:T(8,128)(2,1)}, u32[]{:S(2)}, u32[]{:S(2)}) async-start(bf16[4,128,1024]{2,1,0:T(8,128)(2,1)} %bitcast.25), calls=%async_computation.2 | async-start | bytes 2097152 | tf_op jit(solution)/shard_map/all_to_all | solution.py:1113
  221.8 6.9 %shard_map.197 = (bf16[512,1024]{1,0:T(8,128)(2,1)}, bf16[512,1024]{1,0:T(8,128)(2,1)}) custom-call(s32[12]{0:T(128)} %stack.51.order, bf16[512,1024]{1,0:T(8,128)(2,1)} %get-tuple-element.385.d_ref.refs_9_, bf16[512,1024]{1,0:T(8,128)(2,1)} %shard_map.190.mix_ref, f32[512,2048]{1,0:T(8,128)} %get-tuple-element.301.v_ref.u_ref, ...), custom_call_target="tpu_custom_call" | custom-call | flops 33554432 | bytes 589824 | tf_op jit(solution)/shard_map/pallas_call | solution.py:290
  232.5 4.7 %shard_map.198 = (bf16[256,2816]{1,0:T(8,128)(2,1)}, bf16[256,2816]{1,0:T(8,128)(2,1)}) custom-call(s32[12]{0:T(128)} %stack.51.order, bf16[512,2816]{1,0:T(8,128)(2,1)} %get-tuple-element.367.refs_0_.refs_6_, bf16[512,2816]{1,0:T(8,128)(2,1)} %copy-done.2, bf16[512,2816]{1,0:T(8,128)(2,1)} %get-tuple-element.392.refs_2_.refs_3_.refs_9_, ...), custom_call_target="tpu_custom_call" | custom-call | bytes 450560 | tf_op jit(solution)/shard_map/pallas_call | solution.py:290
  240.2 11.0 %shard_map.199 = (bf16[512,1024]{1,0:T(8,128)(2,1)}, bf16[512,1024]{1,0:T(8,128)(2,1)}, bf16[512,1024]{1,0:T(8,128)(2,1)}) custom-call(s32[12]{0:T(128)} %stack.51.order, f32[512,2048]{1,0:T(8,128)} %get-tuple-element.300.q_ref.k_ref, f32[512,2048]{1,0:T(8,128)} %get-tuple-element.300.q_ref.k_ref, f32[512,2048]{1,0:T(8,128)} %get-tuple-element.301.v_ref.u_ref, ...), custom_call_target="tpu_custom_call" | custom-call | flops 33554432 | bytes 540800 | tf_op jit(solution)/shard_map/pallas_call | solution.py:290
  258.6 11.9 %shard_map.201 = (bf16[512,1024]{1,0:T(8,128)(2,1)}, bf16[512,1024]{1,0:T(8,128)(2,1)}, bf16[512,1024]{1,0:T(8,128)(2,1)}, bf16[512,1024]{1,0:T(8,128)(2,1)}, bf...) custom-call(s32[12]{0:T(128)} %stack.51.order, ...), custom_call_target="tpu_custom_call" | custom-call | flops 167772160 | bytes 655360 | tf_op jit(solution)/shard_map/pallas_call | solution.py:290
  273.2 5.8 %shard_map.202 = (bf16[128,2816]{1,0:T(8,128)(2,1)}, bf16[128,2816]{1,0:T(8,128)(2,1)}, bf16[128,2816]{1,0:T(8,128)(2,1)}, bf16[128,2816]{1,0:T(8,128)(2,1)}) custom-call(s32[12]{0:T(128)} %stack.51.order, bf16[512,2816]{1,0:T(8,128)(2,1)} %get-tuple-element.367.refs_0_.refs_6_, bf16[512,2816]{1,0:T(8,128)(2,1)} %copy-done.2, bf16[256,2816]{1,0:T(8,128)(2,1)} %copy-done.16, ...), custom_call_target="tpu_custom_call" | custom-call | bytes 991232 | tf_op jit(solution)/shard_map/pallas_call | solution.py:290
  286.1 4.5 %shard_map.203 = (bf16[256,1024]{1,0:T(8,128)(2,1)}, bf16[256,1024]{1,0:T(8,128)(2,1)}, bf16[256,1024]{1,0:T(8,128)(2,1)}, bf16[256,1024]{1,0:T(8,128)(2,1)}, bf16[256,1024]{1,0:T(8,128)(2,1)}) custom-call(s32[12]{0:T(128)} %stack.51.order, bf16[512,1024]{1,0:T(8,128)(2,1)} %get-tuple-element.433.refs_0_.refs_15_, bf16[512,1024]{1,0:T(8,128)(2,1)} %copy-done.12, ...), custom_call_target="tpu_custom_call" | custom-call | bytes 409600 | tf_op jit(solution)/shard_map/pallas_call | solution.py:290
  294.0 12.0 %shard_map.205 = f32[512,1024]{1,0:T(8,128)} custom-call(s32[12]{0:T(128)} %stack.51.order, bf16[512,1024]{1,0:T(8,128)(2,1)} %bitcast.24, f32[512,1024]{1,0:T(8,128)} %get-tuple-element.432.d_mid_ref, bf16[512,1024]{1,0:T(8,128)(2,1)} %get-tuple-element.459.refs_1_.refs_0_, bf16[512,1024]{1,0:T(8,128)(2,1)} %get-tuple-element.417.refs_3_.refs_1_, ...), custom_call_target="tpu_custom_call" | custom-call | flops 134217728 | bytes 950272 | tf_op jit(solution)/shard_map/pallas_call | solution.py:290
  320.4 11.1 %collective-permute-done.62.refs_5_.refs_20_ = bf16[256,1024]{1,0:T(8,128)(2,1)} collective-permute-done((bf16[256,1024]{1,0:T(8,128)(2,1)}, bf16[256,1024]{1,0:T(8,128)(2,1)}, u32[]{:S(2)}, u32[]{:S(2)}) %collective-permute-start.62) | collective-permute-done | bytes 524320 | tf_op jit(solution)/shard_map/ppermute | solution.py:38
  332.1 8.3 %collective-permute-done.64.refs_11_.refs_26_ = bf16[256,1024]{1,0:T(8,128)(2,1)} collective-permute-done((bf16[256,1024]{1,0:T(8,128)(2,1)}, bf16[256,1024]{1,0:T(8,128)(2,1)}, u32[]{:S(2)}, u32[]{:S(2)}) %collective-permute-start.64) | collective-permute-done | bytes 524320 | tf_op jit(solution)/shard_map/ppermute | solution.py:38
  340.8 5.4 %shard_map.206 = (bf16[128,1024]{1,0:T(8,128)(2,1)}, bf16[128,1024]{1,0:T(8,128)(2,1)}, bf16[128,1024]{1,0:T(8,128)(2,1)}, bf16[128,1024]{1,0:T(8,128)(2,1)}, bf...) custom-call(s32[12]{0:T(128)} %stack.51.order, ...), custom_call_target="tpu_custom_call" | custom-call | bytes 901120 | tf_op jit(solution)/shard_map/pallas_call | solution.py:290
  349.2 3.7 all-to-all-start.3
  358.4 4.0 collective-permute-done.67.refs_1_
  362.6 4.8 %collective-permute-done.69.refs_5_ = bf16[128,1024]{1,0:T(8,128)(2,1)S(1)} collective-permute-done((bf16[128,1024]{1,0:T(8,128)(2,1)S(1)}, bf16[128,1024]{1,0:T(8,128)(2,1)S(1)}, u32[]{:S(2)}, u32[]{:S(2)}) %collective-permute-start.69) | collective-permute-done | bytes 262176 | tf_op jit(solution)/shard_map/ppermute | solution.py:38
  370.8 4.2 shard_map.207
  379.1 16.1 %collective-permute-done.73 = bf16[128,1408]{1,0:T(8,128)(2,1)S(1)} collective-permute-done((bf16[128,1408]{1,0:T(8,128)(2,1)S(1)}, bf16[128,1408]{1,0:T(8,128)(2,1)S(1)}, u32[]{:S(2)}, u32[]{:S(2)}) %collective-permute-start.73) | collective-permute-done | bytes 360480 | tf_op jit(solution)/shard_map/ppermute | solution.py:195
  408.1 11.1 %collective-permute-done.74.got_ref = bf16[128,1280]{1,0:T(8,128)(2,1)S(1)} collective-permute-done((bf16[128,1280]{1,0:T(8,128)(2,1)}, bf16[128,1280]{1,0:T(8,128)(2,1)S(1)}, u32[]{:S(2)}, u32[]{:S(2)}) %collective-permute-start.74) | collective-permute-done | bytes 327712 | tf_op jit(solution)/shard_map/ppermute | solution.py:239
  (294 shorter events, 148.9 us)
Async XLA Ops:
  0.7 32.1 %all-to-all-start = ((bf16[4,128,1024]{2,1,0:T(8,128)(2,1)}), bf16[4,128,1024]{2,1,0:T(8,128)(2,1)S(1)}, u32[]{:S(2)}, u32[]{:S(2)}) async-start(bf16[4,128,1024]{2,1,0:T(8,128)(2,1)} %param.11), calls=%async_computation | async-start | bytes 2097152 | tf_op jit(solution)/shard_map/all_to_all | solution.py:1113
  11.2 25.9 %collective-permute-start.2 = (bf16[128,2560]{1,0:T(8,128)(2,1)}, bf16[128,2560]{1,0:T(8,128)(2,1)S(1)}, u32[]{:S(2)}, u32[]{:S(2)}) collective-permute-start(bf16[128,2560]{1,0:T(8,128)(2,1)} %get-tuple-element.268.refs_0_.refs_4_.refs_12_), channel_id=1, source_target_pairs={{0,16},{4,20},{8,24},{12,28},{16,0},{20,4},{24,8},{28,12},{1,17},{... | collective-permute-start | bytes 1966088 | tf_op jit(solution)/shard_map/ppermute | solution.py:38
  12.8 24.4 %collective-permute-start = (bf16[128,2560]{1,0:T(8,128)(2,1)}, bf16[128,2560]{1,0:T(8,128)(2,1)}, u32[]{:S(2)}, u32[]{:S(2)}) collective-permute-start(bf16[128,2560]{1,0:T(8,128)(2,1)} %get-tuple-element.268.refs_0_.refs_4_.refs_12_), channel_id=1, source_target_pairs={{0,8},{4,12},{8,0},{12,4},{16,24},{20,28},{24,16},{28,20},{1,9},{5... | collective-permute-start | bytes 1966088 | tf_op jit(solution)/shard_map/ppermute | solution.py:38
  14.2 28.1 %collective-permute-start.3 = (bf16[128,2560]{1,0:T(8,128)(2,1)}, bf16[128,2560]{1,0:T(8,128)(2,1)}, u32[]{:S(2)}, u32[]{:S(2)}) collective-permute-start(bf16[128,2560]{1,0:T(8,128)(2,1)} %get-tuple-element.269.refs_8_.refs_20_.refs_28_), channel_id=1, source_target_pairs={{0,16},{4,20},{8,24},{12,28},{16,0},{20,4},{24,8},{28,12},{1,17},{... | collective-permute-start | bytes 1966088 | tf_op jit(solution)/shard_map/ppermute | solution.py:38
  14.8 28.8 %collective-permute-start.1 = (bf16[128,2560]{1,0:T(8,128)(2,1)}, bf16[128,2560]{1,0:T(8,128)(2,1)}, u32[]{:S(2)}, u32[]{:S(2)}) collective-permute-start(bf16[128,2560]{1,0:T(8,128)(2,1)} %get-tuple-element.269.refs_8_.refs_20_.refs_28_), channel_id=1, source_target_pairs={{0,8},{4,12},{8,0},{12,4},{16,24},{20,28},{24,16},{28,20},{1,9},{5... | collective-permute-start | bytes 1966088 | tf_op jit(solution)/shard_map/ppermute | solution.py:38
  44.1 17.0 %collective-permute-start.6 = (bf16[128,2560]{1,0:T(8,128)(2,1)}, bf16[128,2560]{1,0:T(8,128)(2,1)}, u32[]{:S(2)}, u32[]{:S(2)}) collective-permute-start(bf16[128,2560]{1,0:T(8,128)(2,1)} %collective-permute-done.refs_1_.refs_5_.refs_13_), channel_id=1, source_target_pairs={{0,16},{4,20},{8,24},{12,28},{16,0},{20,4},{24,8},{28,12},{1,17},{... | collective-permute-start | bytes 1966088 | tf_op jit(solution)/shard_map/ppermute | solution.py:38
  46.8 17.1 %collective-permute-start.7 = (bf16[128,2560]{1,0:T(8,128)(2,1)}, bf16[128,2560]{1,0:T(8,128)(2,1)}, u32[]{:S(2)}, u32[]{:S(2)}) collective-permute-start(bf16[128,2560]{1,0:T(8,128)(2,1)} %collective-permute-done.3.refs_10_.refs_22_.refs_30_), channel_id=1, source_target_pairs={{0,8},{4,12},{8,0},{12,4},{16,24},{20,28},{24,16},{28,20},{1,9},{5... | collective-permute-start | bytes 1966088 | tf_op jit(solution)/shard_map/ppermute | solution.py:38
  63.9 58.1 %all-to-all-start.1 = ((bf16[4,128,1024]{2,1,0:T(8,128)(2,1)}), bf16[4,128,1024]{2,1,0:T(8,128)(2,1)}, u32[]{:S(2)}, u32[]{:S(2)}) async-start(bf16[4,128,1024]{2,1,0:T(8,128)(2,1)} %param.13), calls=%async_computation.1 | async-start | bytes 2097152 | tf_op jit(solution)/shard_map/all_to_all | solution.py:1113
  69.1 26.5 %collective-permute-start.16 = (bf16[128,2816]{1,0:T(8,128)(2,1)}, bf16[128,2816]{1,0:T(8,128)(2,1)}, u32[]{:S(2)}, u32[]{:S(2)}) collective-permute-start(bf16[128,2816]{1,0:T(8,128)(2,1)} %refs_0_.5), channel_id=1, source_target_pairs={{0,16},{4,20},{8,24},{12,28},{16,0},{20,4},{24,8},{28,12},{1,17},{... | collective-permute-start | bytes 2162696 | tf_op jit(solution)/shard_map/ppermute | solution.py:38
  69.6 26.0 %collective-permute-start.14 = (bf16[128,2816]{1,0:T(8,128)(2,1)}, bf16[128,2816]{1,0:T(8,128)(2,1)}, u32[]{:S(2)}, u32[]{:S(2)}) collective-permute-start(bf16[128,2816]{1,0:T(8,128)(2,1)} %refs_0_.5), channel_id=1, source_target_pairs={{0,8},{4,12},{8,0},{12,4},{16,24},{20,28},{24,16},{28,20},{1,9},{5... | collective-permute-start | bytes 2162696 | tf_op jit(solution)/shard_map/ppermute | solution.py:38
  71.1 32.0 %collective-permute-start.17 = (bf16[128,2816]{1,0:T(8,128)(2,1)}, bf16[128,2816]{1,0:T(8,128)(2,1)}, u32[]{:S(2)}, u32[]{:S(2)}) collective-permute-start(bf16[128,2816]{1,0:T(8,128)(2,1)} %refs_8_.1), channel_id=1, source_target_pairs={{0,16},{4,20},{8,24},{12,28},{16,0},{20,4},{24,8},{28,12},{1,17},{... | collective-permute-start | bytes 2162696 | tf_op jit(solution)/shard_map/ppermute | solution.py:38
  72.7 30.7 %collective-permute-start.15 = (bf16[128,2816]{1,0:T(8,128)(2,1)}, bf16[128,2816]{1,0:T(8,128)(2,1)}, u32[]{:S(2)}, u32[]{:S(2)}) collective-permute-start(bf16[128,2816]{1,0:T(8,128)(2,1)} %refs_8_.1), channel_id=1, source_target_pairs={{0,8},{4,12},{8,0},{12,4},{16,24},{20,28},{24,16},{28,20},{1,9},{5... | collective-permute-start | bytes 2162696 | tf_op jit(solution)/shard_map/ppermute | solution.py:38
  103.4 17.4 %collective-permute-start.18 = (bf16[128,2816]{1,0:T(8,128)(2,1)}, bf16[128,2816]{1,0:T(8,128)(2,1)S(1)}, u32[]{:S(2)}, u32[]{:S(2)}) collective-permute-start(bf16[128,2816]{1,0:T(8,128)(2,1)} %collective-permute-done.14.refs_1_), channel_id=1, source_target_pairs={{0,16},{4,20},{8,24},{12,28},{16,0},{20,4},{24,8},{28,12},{1,17},{... | collective-permute-start | bytes 2162696 | tf_op jit(solution)/shard_map/ppermute | solution.py:38
  104.9 17.1 %collective-permute-start.19 = (bf16[128,2816]{1,0:T(8,128)(2,1)}, bf16[128,2816]{1,0:T(8,128)(2,1)S(1)}, u32[]{:S(2)}, u32[]{:S(2)}) collective-permute-start(bf16[128,2816]{1,0:T(8,128)(2,1)} %collective-permute-done.17.refs_10_), channel_id=1, source_target_pairs={{0,8},{4,12},{8,0},{12,4},{16,24},{20,28},{24,16},{28,20},{1,9},{5... | collective-permute-start | bytes 2162696 | tf_op jit(solution)/shard_map/ppermute | solution.py:38
  124.7 18.4 %collective-permute-start.31 = (bf16[352,512]{1,0:T(8,128)(2,1)}, bf16[352,512]{1,0:T(8,128)(2,1)S(1)}, u32[]{:S(2)}, u32[]{:S(2)}) collective-permute-start(bf16[352,512]{1,0:T(8,128)(2,1)} %get-tuple-element.364.refs_24_), channel_id=1, source_target_pairs={{0,16},{4,20},{8,24},{12,28},{16,0},{20,4},{24,8},{28,12},{1,17},{... | collective-permute-start | bytes 1081352 | tf_op jit(solution)/shard_map/ppermute | solution.py:38
  168.9 41.0 %collective-permute-start.44 = (bf16[704,512]{1,0:T(8,128)(2,1)}, bf16[704,512]{1,0:T(8,128)(2,1)S(1)}, u32[]{:S(2)}, u32[]{:S(2)}) collective-permute-start(bf16[704,512]{1,0:T(8,128)(2,1)} %get-tuple-element.373), channel_id=1, source_target_pairs={{0,8},{4,12},{8,0},{12,4},{16,24},{20,28},{24,16},{28,20},{1,9},{5... | collective-permute-start | bytes 2162696 | tf_op jit(solution)/shard_map/ppermute | solution.py:38
  169.8 40.1 %collective-permute-start.45 = (bf16[704,512]{1,0:T(8,128)(2,1)}, bf16[704,512]{1,0:T(8,128)(2,1)S(1)}, u32[]{:S(2)}, u32[]{:S(2)}) collective-permute-start(bf16[704,512]{1,0:T(8,128)(2,1)} %get-tuple-element.374), channel_id=1, source_target_pairs={{0,16},{4,20},{8,24},{12,28},{16,0},{20,4},{24,8},{28,12},{1,17},{... | collective-permute-start | bytes 2162696 | tf_op jit(solution)/shard_map/ppermute | solution.py:38
  211.1 19.9 %collective-permute-start.46 = (bf16[512,2816]{1,0:T(8,128)(2,1)}, bf16[512,2816]{1,0:T(8,128)(2,1)S(1)}, u32[]{:S(2)}, u32[]{:S(2)}) collective-permute-start(bf16[512,2816]{1,0:T(8,128)(2,1)} %get-tuple-element.376), channel_id=1, source_target_pairs={{0,4},{4,0},{8,12},{12,8},{16,20},{20,16},{24,28},{28,24},{1,5},{5... | collective-permute-start | bytes 8650760 | tf_op jit(solution)/shard_map/ppermute | solution.py:38
  211.2 19.8 %collective-permute-start.47 = (bf16[512,2816]{1,0:T(8,128)(2,1)}, bf16[512,2816]{1,0:T(8,128)(2,1)}, u32[]{:S(2)}, u32[]{:S(2)}) collective-permute-start(bf16[512,2816]{1,0:T(8,128)(2,1)} %get-tuple-element.377), channel_id=1, source_target_pairs={{0,4},{4,0},{8,12},{12,8},{16,20},{20,16},{24,28},{28,24},{1,5},{5... | collective-permute-start | bytes 8650760 | tf_op jit(solution)/shard_map/ppermute | solution.py:38
  215.6 35.6 %all-to-all-start.2 = ((bf16[4,128,1024]{2,1,0:T(8,128)(2,1)}), bf16[4,128,1024]{2,1,0:T(8,128)(2,1)}, u32[]{:S(2)}, u32[]{:S(2)}) async-start(bf16[4,128,1024]{2,1,0:T(8,128)(2,1)} %bitcast.25), calls=%async_computation.2 | async-start | bytes 2097152 | tf_op jit(solution)/shard_map/all_to_all | solution.py:1113
  237.3 33.2 %collective-permute-start.50 = (bf16[256,2816]{1,0:T(8,128)(2,1)}, bf16[256,2816]{1,0:T(8,128)(2,1)S(1)}, u32[]{:S(2)}, u32[]{:S(2)}) collective-permute-start(bf16[256,2816]{1,0:T(8,128)(2,1)} %get-tuple-element.426), channel_id=1, source_target_pairs={{0,8},{4,12},{8,0},{12,4},{16,24},{20,28},{24,16},{28,20},{1,9},{5... | collective-permute-start | bytes 4325384 | tf_op jit(solution)/shard_map/ppermute | solution.py:38
  238.6 32.5 %collective-permute-start.51 = (bf16[256,2816]{1,0:T(8,128)(2,1)}, bf16[256,2816]{1,0:T(8,128)(2,1)S(1)}, u32[]{:S(2)}, u32[]{:S(2)}) collective-permute-start(bf16[256,2816]{1,0:T(8,128)(2,1)} %get-tuple-element.427), channel_id=1, source_target_pairs={{0,16},{4,20},{8,24},{12,28},{16,0},{20,4},{24,8},{28,12},{1,17},{... | collective-permute-start | bytes 4325384 | tf_op jit(solution)/shard_map/ppermute | solution.py:38
  281.2 24.8 %collective-permute-start.58 = (bf16[128,2816]{1,0:T(8,128)(2,1)}, bf16[128,2816]{1,0:T(8,128)(2,1)S(1)}, u32[]{:S(2)}, u32[]{:S(2)}) collective-permute-start(bf16[128,2816]{1,0:T(8,128)(2,1)} %get-tuple-element.460), channel_id=1, source_target_pairs={{0,16},{4,20},{8,24},{12,28},{16,0},{20,4},{24,8},{28,12},{1,17},{... | collective-permute-start | bytes 2162696 | tf_op jit(solution)/shard_map/ppermute | solution.py:38
  282.6 23.4 %collective-permute-start.59 = (bf16[128,2816]{1,0:T(8,128)(2,1)}, bf16[128,2816]{1,0:T(8,128)(2,1)}, u32[]{:S(2)}, u32[]{:S(2)}) collective-permute-start(bf16[128,2816]{1,0:T(8,128)(2,1)} %get-tuple-element.461), channel_id=1, source_target_pairs={{0,8},{4,12},{8,0},{12,4},{16,24},{20,28},{24,16},{28,20},{1,9},{5... | collective-permute-start | bytes 2162696 | tf_op jit(solution)/shard_map/ppermute | solution.py:38
  292.7 26.4 %collective-permute-start.61 = (bf16[256,1024]{1,0:T(8,128)(2,1)}, bf16[256,1024]{1,0:T(8,128)(2,1)S(1)}, u32[]{:S(2)}, u32[]{:S(2)}) collective-permute-start(bf16[256,1024]{1,0:T(8,128)(2,1)} %get-tuple-element.464), channel_id=1, source_target_pairs={{0,8},{4,12},{8,0},{12,4},{16,24},{20,28},{24,16},{28,20},{1,9},{5... | collective-permute-start | bytes 1572872 | tf_op jit(solution)/shard_map/ppermute | solution.py:38
  314.9 31.4 %collective-permute-start.66 = (bf16[128,2816]{1,0:T(8,128)(2,1)}, bf16[128,2816]{1,0:T(8,128)(2,1)}, u32[]{:S(2)}, u32[]{:S(2)}) collective-permute-start(bf16[128,2816]{1,0:T(8,128)(2,1)} %concatenate.14), channel_id=1, source_target_pairs={{0,1},{1,0},{2,3},{3,2},{4,5},{5,4},{6,7},{7,6},{8,9},{9,8},{10,11... | collective-permute-start | bytes 2162696 | tf_op jit(solution)/shard_map/ppermute | solution.py:195
  317.7 22.7 %collective-permute-start.64 = (bf16[256,1024]{1,0:T(8,128)(2,1)}, bf16[256,1024]{1,0:T(8,128)(2,1)}, u32[]{:S(2)}, u32[]{:S(2)}) collective-permute-start(bf16[256,1024]{1,0:T(8,128)(2,1)} %get-tuple-element.467), channel_id=1, source_target_pairs={{0,16},{4,20},{8,24},{12,28},{16,0},{20,4},{24,8},{28,12},{1,17},{... | collective-permute-start | bytes 1572872 | tf_op jit(solution)/shard_map/ppermute | solution.py:38
  319.1 21.7 %collective-permute-start.65 = (bf16[256,1024]{1,0:T(8,128)(2,1)}, bf16[256,1024]{1,0:T(8,128)(2,1)}, u32[]{:S(2)}, u32[]{:S(2)}) collective-permute-start(bf16[256,1024]{1,0:T(8,128)(2,1)} %get-tuple-element.468), channel_id=1, source_target_pairs={{0,8},{4,12},{8,0},{12,4},{16,24},{20,28},{24,16},{28,20},{1,9},{5... | collective-permute-start | bytes 1572872 | tf_op jit(solution)/shard_map/ppermute | solution.py:38
  349.2 73.5 %all-to-all-start.3 = ((bf16[4,128,1024]{2,1,0:T(8,128)(2,1)}), bf16[4,128,1024]{2,1,0:T(8,128)(2,1)S(1)}, u32[]{:S(2)}, u32[]{:S(2)}) async-start(bf16[4,128,1024]{2,1,0:T(8,128)(2,1)} %bitcast.19), calls=%async_computation.3 | async-start | bytes 2097152 | tf_op jit(solution)/shard_map/all_to_all | solution.py:1113
  375.0 23.3 %collective-permute-start.72 = (bf16[128,2560]{1,0:T(8,128)(2,1)}, bf16[128,2560]{1,0:T(8,128)(2,1)S(1)}, u32[]{:S(2)}, u32[]{:S(2)}) collective-permute-start(bf16[128,2560]{1,0:T(8,128)(2,1)} %get-tuple-element.511), channel_id=1, source_target_pairs={{0,1},{1,0},{2,3},{3,2},{4,5},{5,4},{6,7},{7,6},{8,9},{9,8},{10,11... | collective-permute-start | bytes 1966088 | tf_op jit(solution)/shard_map/ppermute | solution.py:239
  376.7 18.5 %collective-permute-start.73 = (bf16[128,1408]{1,0:T(8,128)(2,1)S(1)}, bf16[128,1408]{1,0:T(8,128)(2,1)S(1)}, u32[]{:S(2)}, u32[]{:S(2)}) collective-permute-start(bf16[128,1408]{1,0:T(8,128)(2,1)S(1)} %pad_maximum_fusion.2), channel_id=1, source_target_pairs={{0,2},{1,3},{2,0},{3,1},{4,6},{5,7},{6,4},{7,5},{8,10},{9,11},{10,... | collective-permute-start | bytes 1081352 | tf_op jit(solution)/shard_map/ppermute | solution.py:195
  402.4 16.9 %collective-permute-start.74 = (bf16[128,1280]{1,0:T(8,128)(2,1)}, bf16[128,1280]{1,0:T(8,128)(2,1)S(1)}, u32[]{:S(2)}, u32[]{:S(2)}) collective-permute-start(bf16[128,1280]{1,0:T(8,128)(2,1)} %get-tuple-element.515), channel_id=1, source_target_pairs={{0,2},{1,3},{2,0},{3,1},{4,6},{5,7},{6,4},{7,5},{8,10},{9,11},{10,... | collective-permute-start | bytes 983048 | tf_op jit(solution)/shard_map/ppermute | solution.py:239
  (106 other events, 1028.0 us)

commit v3 on v2

--- a/solution.py
+++ b/solution.py
@@ -102,10 +102,12 @@
 class Gather:
     def __init__(self, pieces):
         self.pieces = list(pieces)
-
-    def first(self):
-        self.near_x = [swap(p, 2, 8) for p in self.pieces]
-        self.near_y = [swap(p, 4, 8) for p in self.pieces]
+        self.near_x, self.near_y = [None, None], [None, None]
+
+    def first(self, *halves):
+        for half in halves or (0, 1):
+            self.near_x[half] = swap(self.pieces[half], 2, 8)
+            self.near_y[half] = swap(self.pieces[half], 4, 8)
 
     def second(self):
         self.far = [swap(self.near_x[0], 4, 8), swap(self.near_y[1], 2, 8)]
@@ -119,31 +121,8 @@
         return [getattr(self, n + core)[half] for core in ("", "_other") for n in names]
 
 
-def add(one, two, out=BF16):
-    return (one.astype(F32) + two.astype(F32)).astype(out)
-
-
-def added(order, outs):
-    steps = 2
-    ins, results, counts = [], [], []
-    for terms, rows, dtype in outs:
-        size = rows // steps
-        width = terms[0][0].shape[1]
-        for array, first in terms:
-            ins.append((array, pl.BlockSpec((size, width), lambda i, *_, f=first // size: (f + i, 0))))
-        results.append(((rows, width), dtype, pl.BlockSpec((size, width), lambda i, *_: (i, 0))))
-        counts.append(len(terms))
-
-    def body(order, *refs):
-        at = 0
-        for out, count in zip(refs[len(ins) :], counts):
-            total = refs[at][...].astype(F32)
-            for ref in refs[at + 1 : at + count]:
-                total += ref[...].astype(F32)
-            out[...] = total.astype(out.dtype)
-            at += count
-
-    return call(body, (steps,), order, ins, results)
+def added(*terms):
+    return functools.reduce(lambda a, b: a + b, [t.astype(F32) for t in terms]).astype(BF16)
 
 
 class Reduce:
@@ -155,118 +134,91 @@
 
     def join(self):
         half = self.keeps[0].shape[0] // 2
-        pairs = zip(self.keeps, self.theirs)
-        self.totals = added(self.order, [([(k, half), (t, half)], half, BF16) for k, t in pairs])
+        self.totals = [added(k[half:], t[half:]) for k, t in zip(self.keeps, self.theirs)]
 
     def first(self):
         self.got = [swap(t, b, 8) for t, b in zip(self.totals, self.bits)]
 
     def join_first(self):
         rows = self.keeps[0].shape[0] // 4
-        outs = []
-        for at in (0, rows):
-            for k, t, g in zip(self.keeps, self.theirs, self.got):
-                outs.append(([(k, at), (t, at), (g, at)], rows, BF16))
-        parts = added(self.order, outs)
-        count = len(self.keeps)
-        self.own, self.parts = parts[:count], parts[count:]
+        self.own, self.parts = (
+            [
+                added(k[at : at + rows], t[at : at + rows], g[at : at + rows])
+                for k, t, g in zip(self.keeps, self.theirs, self.got)
+            ]
+            for at in (0, rows)
+        )
 
     def second(self):
         self.got_last = [swap(p, 6 - b, 8) for p, b in zip(self.parts, self.bits)]
 
-    def join_second(self):
-        self.sums = [add(p, g, F32) for p, g in zip(self.own, self.got_last)]
-
-
-def column_block(s, here, bit):
-    width = s.shape[1] // 4
-    return lax.dynamic_slice_in_dim(s, (here ^ bit) * width, width, axis=1)
+    def settle(self, block, starts):
+        return Settle(self.order, self.own, self.got_last, block, starts)
 
 
 class Settle:
-    def __init__(self, sums, here):
-        self.widths = [s.shape[1] // 4 for s in sums]
-        self.own = [column_block(s, here, 0) for s in sums]
-        self.far = [column_block(s, here, 2) for s in sums]
-        near = [column_block(s, here, 1) for s in sums] + [column_block(s, here, 3) for s in sums]
-        self.out = jnp.concatenate([n.astype(BF16) for n in near], axis=1)
+    def __init__(self, order, parts, got, block, starts):
+        self.order, self.block, self.count = order, block, len(starts)
+        rows = self.rows = parts[0].shape[0]
+        widths = [p.shape[1] for p in parts]
+        each = 2 if got else 1
+
+        def body(order, *refs):
+            own, out, held = refs[each * len(parts) :]
+            at = 0
+            for i, width in enumerate(widths):
+                total = refs[each * i][...].astype(F32)
+                if got:
+                    total += refs[each * i + 1][...].astype(F32)
+                held[:, at : at + width] = total
+                at += width
+            for z in range(4):
+
+                @pl.when(order[8] == z)
+                def _(z=z):
+                    for i, start in enumerate(starts):
+                        for j in range(2):
+                            mine, theirs = start(z ^ (2 * j)), start(z ^ (2 * j + 1))
+                            own[2 * i + j] = held[:, mine : mine + block]
+                            out[2 * i + j] = held[:, theirs : theirs + block].astype(BF16)
+
+        self.own, self.out = call(
+            body, (1,), order,
+            [(a, whole_spec(*a.shape)) for terms in zip(parts, *([got] if got else [])) for a in terms],
+            [self.entry(2 * self.count, F32), self.entry(2 * self.count, BF16)],
+            scratch=[pltpu.VMEM((rows, sum(widths)), F32)],
+        )
+
+    def entry(self, count, dtype):
+        shape = (count, self.rows, self.block)
+        return shape, dtype, pl.BlockSpec(shape, lambda *_: (0, 0, 0))
+
+    def given(self):
+        return [(a, pl.BlockSpec(a.shape, lambda *_: (0, 0, 0))) for a in (self.own, self.got)]
 
     def pass_on(self, bit):
         self.got = lax.ppermute(self.out, "heads", [(i, i ^ bit) for i in range(4)])
 
-    def split(self, at=0):
-        pieces = []
-        for w in self.widths:
-            pieces.append(self.got[:, at : at + w].astype(F32))
-            at += w
-        return pieces
-
     def join(self):
-        self.own = [o + g for o, g in zip(self.own, self.split())]
-        far = [o + g for o, g in zip(self.far, self.split(sum(self.widths)))]
-        self.out = jnp.concatenate([f.astype(BF16) for f in far], axis=1)
-
-    def result(self):
-        return [o + g for o, g in zip(self.own, self.split())]
-
-
-class SettleWide:
-    def __init__(self, order, parts, got):
-        self.order, self.count = order, len(parts)
-        rows, width = parts[0].shape
-        self.rows, self.block = rows, width // 4
-        count, block = self.count, self.block
-
-        def body(order, *refs):
-            own, out, held = refs[2 * count], refs[2 * count + 1], refs[2 * count + 2]
-            for i in range(count):
-                held[...] = refs[2 * i][...].astype(F32) + refs[2 * i + 1][...].astype(F32)
-                for j, bit in enumerate((0, 2)):
-                    at = (2 * i + j) * block
-                    own[:, at : at + block] = held[:, at_block(order, 8 + bit, block)]
-                    out[:, at : at + block] = held[:, at_block(order, 9 + bit, block)].astype(BF16)
-
-        spec = whole_spec(rows, width)
-        wide = whole_spec(rows, 2 * count * block)
-        shape = rows, 2 * count * block
-        ins = [(a, spec) for pair in zip(parts, got) for a in pair]
-        self.own, self.out = call(
-            body, (1,), order, ins, [(shape, F32, wide), (shape, BF16, wide)],
-            scratch=[pltpu.VMEM((rows, width), F32)],
-        )
-
-    def pass_on(self, bit):
-        self.got = lax.ppermute(self.out, "heads", [(i, i ^ bit) for i in range(4)])
-
-    def join(self):
-        rows, count, block = self.rows, self.count, self.block
+        count = self.count
 
         def body(order, own_ref, got_ref, mine, out):
             for i in range(count):
-                at = 2 * i * block
-                both = own_ref[:, at : at + 2 * block] + got_ref[:, at : at + 2 * block].astype(F32)
-                mine[:, i * block : (i + 1) * block] = both[:, :block]
-                out[:, i * block : (i + 1) * block] = both[:, block:].astype(BF16)
-
-        wide, narrow = whole_spec(rows, 2 * count * block), whole_spec(rows, count * block)
-        shape = rows, count * block
+                mine[i] = own_ref[2 * i] + got_ref[2 * i].astype(F32)
+                out[i] = (own_ref[2 * i + 1] + got_ref[2 * i + 1].astype(F32)).astype(BF16)
+
         self.own, self.out = call(
-            body, (1,), self.order, [(self.own, wide), (self.got, wide)],
-            [(shape, F32, narrow), (shape, BF16, narrow)],
+            body, (1,), self.order, self.given(), [self.entry(count, F32), self.entry(count, BF16)]
         )
 
     def result(self):
-        rows, count, block = self.rows, self.count, self.block
-
         def body(order, own_ref, got_ref, *outs):
             for i, out in enumerate(outs):
-                cols = slice(i * block, (i + 1) * block)
-                out[...] = own_ref[:, cols] + got_ref[:, cols].astype(F32)
-
-        narrow = whole_spec(rows, count * block)
+                out[...] = own_ref[i] + got_ref[i].astype(F32)
+
+        shape = (self.rows, self.block)
         return call(
-            body, (1,), self.order, [(self.own, narrow), (self.got, narrow)],
-            [((rows, block), F32, whole_spec(rows, block))] * count,
+            body, (1,), self.order, self.given(), [(shape, F32, whole_spec(*shape))] * self.count
         )
 
 
@@ -298,7 +250,7 @@
         ),
         out_shape=[jax.ShapeDtypeStruct(s, t) for s, t, _ in outs],
         compiler_params=pltpu.CompilerParams(vmem_limit_bytes=VMEM_LIMIT),
-        cost_estimate=pl.CostEstimate(flops=flops // 32, bytes_accessed=moved // 32, transcendentals=0),
+        cost_estimate=pl.CostEstimate(flops=flops // 4, bytes_accessed=moved // 4, transcendentals=0),
     )(order, *[a for a, _ in ins])
 
 
@@ -520,6 +472,7 @@
 
 
 def row_mix_body(size, order, q_ref, k_ref, v_ref, cos_ref, sin_ref, col_ref, row_ref, mix_ref):
+    q_ref, k_ref, v_ref = q_ref.at[0], k_ref.at[0], v_ref.at[0]
     cos, sin = cos_ref[...], sin_ref[...]
     col, row = col_ref[...], row_ref[...]
     each = q_ref.shape[1] // HEAD_DIM
@@ -541,8 +494,10 @@
 
 def row_mix_back_body(
     size, order, q_ref, k_ref, v_ref, dm_ref, cos_ref, sin_ref, col_ref, row_ref,
-    dq_ref, dk_ref, dv_ref,
+    d_ref,
 ):
+    q_ref, k_ref, v_ref = q_ref.at[0], k_ref.at[0], v_ref.at[0]
+    dq_ref, dk_ref, dv_ref = d_ref.at[0, 0], d_ref.at[0, 1], d_ref.at[0, 2]
     cos, sin = cos_ref[...], sin_ref[...]
     col, row = col_ref[...], row_ref[...]
     each = q_ref.shape[1] // HEAD_DIM
@@ -590,32 +545,28 @@
 
 def project_body(order, h_ref, *refs):
     h = h_ref[...]
-    refs[16][...] = dot(h, stacked(refs[:8]), NN)
-    refs[17][...] = dot(h, stacked(refs[8:16]), NN)
-
-
-def out_mid_body(order, mix_ref, u_ref, x_ref, *refs):
-    gated_ref, mid_ref, plain = refs[16], refs[17], refs[-1]
+    refs[16][0] = dot(h, stacked(refs[:8]), NN)
+    refs[16][1] = dot(h, stacked(refs[8:16]), NN)
+
+
+def out_mid_body(order, mix_ref, h_in_ref, x_ref, *refs):
+    u_ref, gated_ref, gated_x_ref, mid_ref = refs[16:20]
+    held = refs[-1]
     mix = mix_ref[...].astype(F32)
-    u = u_ref[...]
+    u = dot(h_in_ref[...], stacked(refs[:8]), NN)
+    u_ref[...] = u
     scale = lax.rsqrt(jnp.mean(mix * mix, axis=-1, keepdims=True) + EPS)
-    plain[...] = (mix * scale * (u * sigmoid(u))).astype(BF16)
-    spread(order, plain, (refs[-2], gated_ref))
-    gated = refs[-2][...]
-    half = x_ref.shape[1] // 2
-    low = x_ref[:, :half].astype(F32) + dot(gated, stacked(refs[:8]), NN)
-    high = x_ref[:, half:].astype(F32) + dot(gated, stacked(refs[8:16]), NN)
-    mid_ref[:, :half] = low
-    mid_ref[:, half:] = high
-    power = jnp.sum(low * low, axis=-1, keepdims=True) + jnp.sum(high * high, axis=-1, keepdims=True)
-    scale = lax.rsqrt(power / x_ref.shape[1] + EPS)
-    plain[:, :half] = (low * scale).astype(BF16)
-    plain[:, half:] = (high * scale).astype(BF16)
-    spread(order, plain, refs[18:20])
+    held[...] = (mix * scale * (u * sigmoid(u))).astype(BF16)
+    spread(order, held, (gated_ref, gated_x_ref))
+    mid = x_ref[...].astype(F32) + dot(gated_ref[...], stacked(refs[8:16]), NN)
+    mid_ref[...] = mid
+    scale = lax.rsqrt(jnp.mean(mid * mid, axis=-1, keepdims=True) + EPS)
+    held[...] = (mid * scale).astype(BF16)
+    spread(order, held, refs[20:22])
 
 
 def left_right_body(order, h_ref, *refs):
-    left_ref, right_ref, product_ref = refs[16:19]
+    left_ref, right_ref, product_ref = refs[16:]
     h = h_ref[...]
     left = dot(h, stacked(refs[:8]), NN)
     right = dot(h, stacked(refs[8:16]), NN)
@@ -713,12 +664,8 @@
 
 
 def gate_out_back_body(order, d_ref, mix_ref, u_ref, *refs):
-    du_ref, dm_ref, held = refs[16:]
-    half = d_ref.shape[1] // 2
-    d = d_ref[...]
-    restored(
-        order, dot(d[:, :half], stacked(refs[:8]), NT) + dot(d[:, half:], stacked(refs[8:16]), NT), held
-    )
+    du_ref, dm_ref, held = refs[8:]
+    restored(order, dot(d_ref[...], stacked(refs[:8]), NT), held)
     dg = held[...]
     mix = mix_ref[...].astype(F32)
     u = u_ref[...]
@@ -730,20 +677,15 @@
     dm_ref[...] = (scale * dn - mix * inner).astype(BF16)
 
 
-def in_back_body(order, x_ref, d_mid_ref, *refs):
-    ds, weights, out, grad, held = refs[:4], refs[4:36], refs[36], refs[37], refs[38]
+def in_back_body(order, x_ref, d_mid_ref, du_ref, d_ref, *refs):
+    low, high, gates, (out, grad, held) = refs[:8], refs[8:16], refs[16:24], refs[24:]
     step = pl.program_id(0)
-    value = dot(ds[0][...], stacked(weights[:8]), NT)
-    for i in (1, 2, 3):
-        value += dot(ds[i][...], stacked(weights[8 * i : 8 * i + 8]), NT)
 
     @pl.when(step == 0)
     def _():
-        grad[...] = value
-
-    @pl.when(step > 0)
-    def _():
-        grad[...] += value
+        grad[...] = dot(du_ref[...], stacked(gates), NT)
+
+    grad[...] += dot(d_ref[0, 0], stacked(low), NT) + dot(d_ref[1, 0], stacked(high), NT)
 
     @pl.when(step == pl.num_programs(0) - 1)
     def _():
@@ -752,15 +694,40 @@
         x = x_ref[...].astype(F32)
         scale = lax.rsqrt(jnp.mean(x * x, axis=-1, keepdims=True) + EPS)
         inner = jnp.mean(g * x, axis=-1, keepdims=True) * (scale * scale * scale)
-        out[...] = d_mid_ref[...] + scale * g - x * inner
-
-
-def weight_grads_body(count, order, *refs):
-    for i in range(count):
-        g = dot(refs[2 * i][...], refs[2 * i + 1][...], TN, BF16)
-        half = g.shape[0] // 2
-        refs[2 * count + 2 * i][...] = g[:half]
-        refs[2 * count + 2 * i + 1][...] = g[half:]
+        out[...] = (d_mid_ref[...] + scale * g - x * inner).astype(BF16)
+
+
+def weight_grads_body(order, hx_ref, hy_ref, gx_ref, gy_ref, d_ref, du, db, *outs):
+    held, sems = outs[4:8], outs[8]
+    step = pl.program_id(0)
+    half = hx_ref.shape[1] // 2
+
+    def copies(side):
+        return [
+            pltpu.make_async_copy(held[2 * side + i], outs[2 * side + i], sems.at[2 * side + i])
+            for i in range(2)
+        ]
+
+    def run(side, h, gated):
+        keep, send = held[2 * side], held[2 * side + 1]
+        terms = [(h, d_ref.at[0, i]) for i in range(3)] + [(h, du), (gated, db)]
+        for i, (lhs, d) in enumerate(terms):
+            g = dot(lhs[...], d[...], TN, BF16)
+            cols = slice(i * g.shape[1], (i + 1) * g.shape[1])
+            keep[:, cols] = g[:half]
+            send[:, cols] = g[half:]
+        for copy in copies(side):
+            copy.start()
+
+    @pl.when(step == 0)
+    def _():
+        run(0, hx_ref, gx_ref)
+
+    @pl.when(step == 1)
+    def _():
+        run(1, hy_ref, gy_ref)
+        for copy in copies(0) + copies(1):
+            copy.wait()
 
 
 class Chain:
@@ -962,44 +929,48 @@
     def norm(self, x):
         return self.by_rows(row_norm_body, [(x, self.wide)], [], [BF16, BF16], [BF16])
 
-    def pieces(self, group, half, width, column=None, offset=0):
-        rows = group.pieces[0].shape[0]
-        if column is None:
-            spec = pl.BlockSpec((rows, width), lambda i, *_: (0, offset + i))
-        else:
-            spec = pl.BlockSpec((rows, width), lambda *_: (0, column))
+    def pieces(self, group, half, width=None):
+        rows, whole = group.pieces[half].shape
+        spec = pl.BlockSpec((rows, width or whole), lambda i, *_: (0, i if width else 0))
         return [(a, spec) for a in group.all(half)]
 
-    def project(self, h, att):
+    def thirds(self, which=None, dtype=F32):
         half = self.width // 2
-        out = (self.length, 2 * self.width), F32, pl.BlockSpec((self.length, half), lambda i, *_: (0, i))
+        if which is None:
+            return pl.BlockSpec((2, self.length, half), lambda i, *_: (0, 0, i))
+        pair = 2 * HEAD_DIM
+        each = half // pair
+        return pl.BlockSpec(
+            (1, self.length, pair), lambda i, *_: (i // each, 0, which * each + i % each)
+        )
+
+    def project(self, h, qkv):
+        half = self.width // 2
         return call(
-            project_body, (4,), self.order,
-            [(h, self.all)] + self.pieces(att, 0, half) + self.pieces(att, 1, half), [out, out],
-            flops=4 * self.flops,
-        )
+            project_body, (3,), self.order,
+            [(h, self.all)] + self.pieces(qkv, 0, half) + self.pieces(qkv, 1, half),
+            [((2, self.length, 3 * half), F32, self.thirds())], flops=3 * self.flops,
+        )[0]
 
     def column(self, block, offset=0):
         return pl.BlockSpec((self.length, block), lambda i, *_: (0, offset + i))
 
-    def mix(self, qk, vu):
-        ins = [(qk, self.heads), (qk, self.column(2 * HEAD_DIM, HEADS // 2)), (vu, self.heads)]
+    def mix(self, pre):
         return call(
-            functools.partial(row_mix_body, self.block), (HEADS // 2,), self.order, ins + self.extra,
+            functools.partial(row_mix_body, self.block), (HEADS // 2,), self.order,
+            [(pre, self.thirds(i)) for i in range(3)] + self.extra,
             [((self.length, self.width), BF16, self.heads)], flops=self.flops * 3 // 8,
         )[0]
 
-    def mix_back(self, qk, vu, d_mix):
-        ins = [(qk, self.heads), (qk, self.column(2 * HEAD_DIM, HEADS // 2)), (vu, self.heads)]
+    def mix_back(self, pre, d_mix):
+        pair, half = 2 * HEAD_DIM, self.width // 2
+        each = half // pair
+        spec = pl.BlockSpec((1, 3, self.length, pair), lambda i, *_: (i // each, 0, 0, i % each))
         return call(
             functools.partial(row_mix_back_body, self.block), (HEADS // 2,), self.order,
-            ins + [(d_mix, self.heads)] + self.extra,
-            [((self.length, self.width), BF16, self.heads)] * 3, flops=self.flops,
-        )
-
-    def out_weights(self, att):
-        half = self.width // 2
-        return self.pieces(att, 0, half, 4) + self.pieces(att, 1, half, 4)
+            [(pre, self.thirds(i)) for i in range(3)] + [(d_mix, self.heads)] + self.extra,
+            [((2, 3, self.length, half), BF16, spec)], flops=self.flops,
+        )[0]
 
     def by_rows(self, body, ins, weights, types, scratch):
         step = self.wide.block_shape[0]
@@ -1009,19 +980,17 @@
             scratch=[pltpu.VMEM((step, self.width), t) for t in scratch], flops=self.flops,
         )
 
-    def gate_spec(self):
-        return pl.BlockSpec(self.wide.block_shape, lambda i, *_: (i, 1))
-
-    def out_mid(self, mix, vu, x, att):
+    def out_mid(self, mix, h, x, uo):
         return self.by_rows(
-            out_mid_body, [(mix, self.wide), (vu, self.gate_spec()), (x, self.wide)],
-            self.out_weights(att), [BF16, F32, BF16, BF16], [BF16, BF16],
-        )
-
-    def gate_out_back(self, d_branch, mix, vu, att):
+            out_mid_body, [(mix, self.wide), (h, self.wide), (x, self.wide)],
+            self.pieces(uo, 0) + self.pieces(uo, 1),
+            [F32, BF16, BF16, F32, BF16, BF16], [BF16],
+        )
+
+    def gate_out_back(self, d_branch, mix, u_pre, uo):
         return self.by_rows(
-            gate_out_back_body, [(d_branch, self.wide), (mix, self.wide), (vu, self.gate_spec())],
-            self.out_weights(att), [BF16, BF16], [F32],
+            gate_out_back_body, [(d_branch, self.wide), (mix, self.wide), (u_pre, self.wide)],
+            self.pieces(uo, 1), [BF16, BF16], [F32],
         )
 
     def left_right(self, h, ff):
@@ -1073,29 +1042,30 @@
             flops=6 * self.flops * inner // self.width,
         )
 
-    def in_back(self, x, d_mid, ds, att):
+    def in_back(self, x, d_mid, d, d_u, qkv, uo):
         half = self.width // 2
-        weights = []
-        for which, offset in ((0, 0), (0, 2), (1, 0), (1, 2)):
-            weights += self.pieces(att, which, half, offset=offset)
         full = (self.length, self.width)
+        third = pl.BlockSpec((2, 1, self.length, half), lambda i, *_: (0, i, 0, 0))
         return call(
-            in_back_body, (2,), self.order,
-            [(x, self.all), (d_mid, self.all)] + [(d, self.column(half)) for d in ds] + weights,
-            [(full, F32, self.all)], scratch=[pltpu.VMEM(full, F32)] * 2, flops=4 * self.flops,
+            in_back_body, (3,), self.order,
+            [(x, self.all), (d_mid, self.all), (d_u, self.all), (d, third)]
+            + self.pieces(qkv, 0, half) + self.pieces(qkv, 1, half) + self.pieces(uo, 0),
+            [(full, BF16, self.all)], scratch=[pltpu.VMEM(full, F32)] * 2, flops=4 * self.flops,
         )[0]
 
-    def weight_grads(self, pairs, bits):
+    def weight_grads(self, h_x, h_y, gated_x, gated_y, d, d_u, d_branch):
         half = self.width // 2
-        tall = pl.BlockSpec((half, half), lambda i, *_: (0, i))
-        ins = []
-        for lhs, d in pairs:
-            ins += [(lhs, self.all), (d, self.column(half))]
+        shape = (half, 5 * half)
+        thirds = pl.BlockSpec((1, 3, self.length, half), lambda i, *_: (i, 0, 0, 0))
         got = call(
-            functools.partial(weight_grads_body, len(pairs)), (2,), self.order, ins,
-            [((half, self.width), BF16, tall)] * (2 * len(pairs)), flops=len(pairs) * self.flops,
-        )
-        return Reduce(self.order, got[1::2], got[::2], bits)
+            weight_grads_body, (2,), self.order,
+            [(a, self.all) for a in (h_x, h_y, gated_x, gated_y)]
+            + [(d, thirds), (d_u, self.column(half)), (d_branch, self.column(half))],
+            [(shape, BF16, HBM)] * 4,
+            scratch=[pltpu.VMEM(shape, BF16)] * 4 + [pltpu.SemaphoreType.DMA((4,))],
+            flops=5 * self.flops,
+        )
+        return Reduce(self.order, got[1::2], got[::2], [2, 4])
 
 
 def stepwise(tokens, doc_lengths, cotangent, weights):
@@ -1115,116 +1085,117 @@
     def whole_row(a):
         return exchanged(a).reshape(length, width)
 
-    att = Gather(
-        pack(
-            order, [w_query, w_key, w_value, w_gate, w_out],
-            [[(0, 0, width), (1, 0, width), (4, 0, half)], [(2, 0, width), (3, 0, width), (4, half, half)]],
-        )
+    inner = w_left.shape[1]
+    uo = Gather([w_gate, w_out])
+    uo.first()
+    qkv = Gather(
+        pack(order, [w_query, w_key, w_value], [[(i, at, half) for i in range(3)] for at in (0, half)])
     )
-    att.first()
+    qkv.first()
     v.x = whole_row(tokens)
-    v.down = pack(order, [w_down], [[(0, 0, half)], [(0, half, half)]])
-    v.ff = [w_left, w_right]
-    att.cross("pieces")
-    tick((v, "x"), (v, "down"), (att, "pieces_other"))
+    v.extra = [a for a, _ in row.extra]
+    ff = Gather([w_left, w_right])
+    v.c = cotangent
+    tick((v, "x"), (qkv, "near_x"), (qkv, "near_y"), (uo, "near_x"), (uo, "near_y"), (uo, "pieces"), (v, "c"), (v, "extra"))
+    row.extra = [(a, spec) for a, (_, spec) in zip(v.extra, row.extra)]
+    qkv.second()
+    uo.second()
+    qkv.cross("pieces", "near_x", "near_y")
+    uo.cross("pieces", "near_x", "near_y")
     v.h = row.norm(v.x)
-    tick((att, "near_x"), (att, "near_y"), (v, "ff"), (v, "down"), (v, "h"))
-    att.second()
-    ff = Gather(v.ff)
+    tick((qkv, "far"), (uo, "far"), (v, "h"), (ff, "pieces"))
     ff.first()
-    att.cross("near_x", "near_y")
-    tick((att, "far"), (att, "near_x_other"), (att, "near_y_other"))
-    att.cross("far")
-    tick((att, "far_other"), (v, "h"))
-    v.qk, v.vu = row.project(v.h[0], att)
-    tick((v, "qk"), (v, "vu"))
-    v.c = cotangent
-    tick((v, "c"))
+    ff.cross("pieces")
+    qkv.cross("far")
+    uo.cross("far")
+    v.pre = row.project(v.h[0], qkv)
+    v.mix = row.mix(v.pre)
+    v.u_pre, v.gated, v.gated_x, v.x_mid, *v.h_mid = row.out_mid(v.mix, v.h[0], v.x, uo)
+    v.down = w_down
+    tick((v, "x_mid"), (v, "h_mid"), (ff, "near_x"), (ff, "near_y"), (v, "down"), (v, "c"))
+    ff.second()
     v.c = whole_row(v.c)
-    v.mix = row.mix(v.qk, v.vu)
-    tick((v, "mix"), (ff, "near_x"), (ff, "near_y"), (ff, "pieces"), (v, "down"))
-    ff.second()
-    ff.cross("pieces", "near_x", "near_y")
+    ff.cross("near_x", "near_y")
+    v.down = pack(order, [v.down], [[(0, 0, half)], [(0, half, half)]])
+    tick((ff, "far"), (v, "down"))
     down = Gather(v.down)
+    ff.cross("far")
     down.first()
-    gated, v.x_mid, *v.h_mid = row.out_mid(v.mix, v.vu, v.x, att)
-    tick((v, "x_mid"), (v, "h_mid"), (v, "c"), (ff, "far"))
-    ff.cross("far")
-    tick((v, "c"), (ff, "far_other"), (v, "h_mid"))
-
-    v.left, v.right, v.product = row.left_right(v.h_mid[0], ff)
-    tick((v, "left"), (v, "right"), (v, "product"), (down, "near_x"), (down, "near_y"), (down, "pieces"))
+    down.cross("pieces")
+    h_y, h_x = v.h_mid
+
+    v.left, v.right, v.product = row.left_right(h_y, ff)
+    tick((v, "left"), (v, "right"), (v, "product"), (down, "near_x"), (down, "near_y"), (v, "c"))
     down.second()
-    down.cross("pieces", "near_x", "near_y")
-    r_down = row.down_grad(v.product, v.c)
-    tick((r_down, "sends"), (down, "far"), (v, "left"))
-    r_down.core()
+    down.cross("near_x", "near_y")
+    v.g_down = dot(v.product, v.c, TN, BF16)
+    tick((v, "g_down"), (down, "far"), (v, "left"))
+    v.sum_down = lax.psum_scatter(v.g_down, "rows", scatter_dimension=0, tiled=True)
     down.cross("far")
-    tick((r_down, "theirs"), (down, "far_other"), (v, "left"))
-    r_down.join()
-    tick((r_down, "totals"), (v, "left"))
-    r_down.first()
+    tick((down, "far_other"), (v, "left"))
     keep_l, send_l, keep_r, send_r, v.d_mid, v.d_branch, v.act = row.feed_back(
-        v.left, v.right, v.product, v.h_mid[1], v.h_mid[0], v.c, v.x_mid, ff, down
+        v.left, v.right, v.product, h_x, h_y, v.c, v.x_mid, ff, down
     )
     r_ff = Reduce(order, [send_l, send_r], [keep_l, keep_r], [2, 4])
-    tick((r_ff, "sends"), (v, "d_mid"), (v, "d_branch"), (v, "act"), (r_down, "got"))
+    tick((r_ff, "sends"), (v, "d_mid"), (v, "d_branch"), (v, "act"))
     r_ff.core()
-    r_down.join_first()
-    tick((r_down, "parts"), (v, "d_branch"), (v, "act"))
-    r_down.second()
+    v.d_u, v.d_mix = row.gate_out_back(v.d_branch, v.mix, v.u_pre, uo)
+    tick((r_ff, "theirs"), (v, "d_u"), (v, "d_mix"))
+    r_ff.join()
+    tick((r_ff, "totals"), (v, "act"), (v, "d_mix"))
+    r_ff.first()
     v.act = exchanged(v.act)
-    v.d_u, v.d_mix = row.gate_out_back(v.d_branch, v.mix, v.vu, att)
-    tick((r_ff, "theirs"), (v, "d_u"), (v, "d_mix"), (r_down, "got_last"))
-    r_ff.join()
-    tick((r_ff, "totals"), (v, "d_mix"))
-    r_ff.first()
-    v.d_q, v.d_k, v.d_v = row.mix_back(v.qk, v.vu, v.d_mix)
-    tick((v, "d_q"), (v, "d_k"), (v, "d_v"), (v, "act"), (r_down, "own"), (r_down, "got_last"))
-    s_down = SettleWide(order, [jnp.concatenate(r_down.own, axis=1)], [jnp.concatenate(r_down.got_last, axis=1)])
-    tick((s_down, "out"), (s_down, "own"), (v, "d_q"))
+    v.d = row.mix_back(v.pre, v.d_mix)
+    tick((v, "d"), (v, "sum_down"))
+    s_down = Settle(order, [v.sum_down], None, half // 2, [lambda z: z * (half // 2)])
+    tick((v, "d"), (s_down, "out"))
     s_down.pass_on(1)
-    r_att = row.weight_grads(
-        [(v.h[1], v.d_q), (v.h[0], v.d_k), (v.h[1], v.d_v), (v.h[0], v.d_u), (gated, v.d_branch)],
-        [2, 4, 2, 4, 2],
-    )
-    tick((r_att, "sends"), (r_ff, "got"), (s_down, "got"))
+    r_att = row.weight_grads(v.h[1], v.h[0], v.gated_x, v.gated, v.d, v.d_u, v.d_branch)
+    tick((r_att, "sends"), (r_ff, "got"), (v, "act"), (v, "d"))
     r_att.core()
     r_ff.join_first()
-    tick((r_ff, "parts"), (r_att, "theirs"), (s_down, "got"))
+    tick((r_att, "theirs"), (r_ff, "parts"), (v, "d"), (s_down, "got"))
     r_ff.second()
+    s_down.join()
+    tick((s_down, "out"), (r_att, "theirs"), (v, "d"))
+    s_down.pass_on(2)
     r_att.join()
-    s_down.join()
-    tick((r_att, "totals"), (s_down, "out"), (v, "d_q"))
+    v.back = row.in_back(v.x, v.d_mid, v.d, v.d_u, qkv, uo)
+    tick((r_att, "totals"), (r_ff, "got_last"), (r_ff, "own"), (v, "back"), (s_down, "got"))
     r_att.first()
-    s_down.pass_on(2)
-    v.input_grad = row.in_back(v.x, v.d_mid, [v.d_q, v.d_k, v.d_v, v.d_u], att)
-    tick((v, "input_grad"), (r_ff, "got_last"), (s_down, "got"))
-    r_ff.join_second()
-    s_ff = Settle(r_ff.sums, head)
-    tick((s_ff, "out"), (s_ff, "own"), (v, "input_grad"))
+    v.back = exchanged(v.back)
+    quarter = inner // 4
+    s_ff = r_ff.settle(quarter, [lambda z: z * quarter, lambda z: inner + z * quarter])
+    tick((s_ff, "out"))
     s_ff.pass_on(1)
-    tick((r_att, "got"), (v, "input_grad"))
+    (v.g_down,) = s_down.result()
+    tick((r_att, "got"), (v, "g_down"))
     r_att.join_first()
-    tick((r_att, "parts"), (s_ff, "got"), (v, "input_grad"))
+    tick((r_att, "parts"), (s_ff, "got"), (v, "back"))
     r_att.second()
     s_ff.join()
-    (g_down,) = s_down.result()
-    tick((s_ff, "out"), (v, "input_grad"))
+    v.back = v.back.astype(F32)
+    tick((s_ff, "out"), (v, "back"))
     s_ff.pass_on(2)
-    back = exchanged(v.input_grad.astype(BF16))
     tick((r_att, "got_last"), (r_att, "own"))
-    s_att = SettleWide(order, r_att.own, r_att.got_last)
-    tick((s_att, "out"), (s_att, "own"))
+    s_att = r_att.settle(
+        half // 2,
+        [
+            lambda z, i=i: (z // 2) * 5 * half + i * half + (z % 2) * (half // 2)
+            for i in range(5)
+        ],
+    )
+    tick((s_att, "out"), (s_ff, "got"))
     s_att.pass_on(1)
-    tick((s_att, "got"), (s_ff, "got"))
+    v.g_ff = s_ff.result()
+    tick((s_att, "got"), (v, "g_ff"))
     s_att.join()
     tick((s_att, "out"))
     s_att.pass_on(2)
-    g_left, g_right = s_ff.result()
     g_query, g_key, g_value, g_gate, g_out = s_att.result()
+    g_left, g_right = v.g_ff
     return (
-        v.act, back.astype(F32), g_query, g_key, g_value, g_gate, g_out, g_left, g_right, g_down
+        v.act, v.back, g_query, g_key, g_value, g_gate, g_out, g_left, g_right, v.g_down
     )
 
 

time: 428 us -> 416 us (0.972); the launches traced: 426 us -> 408 us
  Pallas kernels: 179 us -> 156 us
  waiting for transfers between devices: 133 us -> 117 us
  other arithmetic: 11.6 us -> 27.4 us
  between operations: 1.3 us -> 14.9 us
  local copies, waits for them, and re-layouts: 27.1 us -> 16.1 us
  matrix products: 0 us -> 6.81 us
  starting transfers between devices: 74.8 us -> 70 us
    pallas_call x25 -> x21, Pallas kernels: 179 us -> 156 us  [call(): pl.pallas_call(body, grid_spec=pltpu.PrefetchScalarGridSpec(num_scalar_pr...]
    convert_element_type x3 -> x8, other arithmetic: 4.19 us -> 25.3 us  [the longest x7 23.7 us: added(): functools.reduce(lambda a, b: a + b, [t.astype(F32) for t in terms])]
    all_to_all x4, waiting for transfers between devices: 14.8 us -> 0.01 us  [exchanged(): return lax.all_to_all(a.reshape(4, size, width), 'heads', 0, 0, tiled=True)]
    unnamed x121 -> x107, local copies, waits for them, and re-layouts: 19.8 us -> 9.99 us
    ppermute x69 -> x68, waiting for transfers between devices: 87.5 us -> 80.3 us  [swap(): return lax.ppermute(value, 'rows', [(i, i ^ bit) for i in range(size)])]
    dot_general x0 -> x1, matrix products: none -> 6.81 us  [dot(): lax.dot_general(a, b, (dims, ((), ())), preferred_element_type=F32)]
    ppermute x6, waiting for transfers between devices: 30.3 us -> 37 us  [pass_on(): self.got = lax.ppermute(self.out, 'heads', [(i, i ^ bit) for i in range(4)])]
    ppermute x69 -> x68, starting transfers between devices: 45.6 us -> 39.8 us  [swap(): return lax.ppermute(value, 'rows', [(i, i ^ bit) for i in range(size)])]
  transfers between devices with their start and end apart: 79 -> 79, of which waited for: 34 -> 32; matrix products, arithmetic and copies ran while one was open for 4% -> 10% of each run, Pallas kernels for 42% -> 36%
where the time goes in v3:
time: 416 us; the launch traced here: 408 us
  Pallas kernels  156 us (38%)
  waiting for transfers between devices  117 us (28%)
  starting transfers between devices  70 us (17%)
  other arithmetic  27.4 us (7%)
  local copies, waits for them, and re-layouts  16.1 us (4%)
  between operations  14.9 us (4%)
  matrix products  6.81 us (2%)
    pallas_call x21, Pallas kernels, call(): pl.pallas_call(body, grid_spec=pltpu.PrefetchScalarGridSpec(num_scalar_pr...  156 us
    ppermute x68, waiting for transfers between devices, swap(): return lax.ppermute(value, 'rows', [(i, i ^ bit) for i in range(size)])  80.3 us
    ppermute x68, starting transfers between devices, swap(): return lax.ppermute(value, 'rows', [(i, i ^ bit) for i in range(size)])  39.8 us
    ppermute x6, waiting for transfers between devices, pass_on(): self.got = lax.ppermute(self.out, 'heads', [(i, i ^ bit) for i in range(4)])  37 us
    convert_element_type x7, other arithmetic, added(): functools.reduce(lambda a, b: a + b, [t.astype(F32) for t in terms])  23.7 us
    all_to_all x4, starting transfers between devices, exchanged(): return lax.all_to_all(a.reshape(4, size, width), 'heads', 0, 0, tiled=True)  19.6 us
    ppermute x6, starting transfers between devices, pass_on(): self.got = lax.ppermute(self.out, 'heads', [(i, i ^ bit) for i in range(4)])  10.4 us
    unnamed x107, local copies, waits for them, and re-layouts  9.99 us
  transfers between devices with their start and end apart: 79, of which 32 were waited for; matrix products, arithmetic and copies ran while one was open for 10% of the time, Pallas kernels for 36%

profile of v3, /device:TPU:0, one launch (start us, length us, event | category | flops | bytes accessed | tf_op | source)
XLA Modules:
  0.0 408.4 jit_solution(11231654777206726928)
XLA Ops:
  7.2 6.5 %all-to-all-start = ((bf16[4,128,1024]{2,1,0:T(8,128)(2,1)}), bf16[4,128,1024]{2,1,0:T(8,128)(2,1)S(1)}, u32[]{:S(2)}, u32[]{:S(2)}) async-start(bf16[4,128,1024]{2,1,0:T(8,128)(2,1)} %param.11), calls=%async_computation | async-start | bytes 2097152 | tf_op jit(solution)/shard_map/all_to_all | solution.py:1083
  30.3 8.2 %collective-permute-done.2.refs_2_ = bf16[128,1536]{1,0:T(8,128)(2,1)S(1)} collective-permute-done((bf16[128,1536]{1,0:T(8,128)(2,1)}, bf16[128,1536]{1,0:T(8,128)(2,1)S(1)}, u32[]{:S(2)}, u32[]{:S(2)}) %collective-permute-start.2) | collective-permute-done | bytes 393248 | tf_op jit(solution)/shard_map/ppermute | solution.py:38
  38.6 6.7 %collective-permute-done.3.refs_10_ = bf16[128,1536]{1,0:T(8,128)(2,1)} collective-permute-done((bf16[128,1536]{1,0:T(8,128)(2,1)}, bf16[128,1536]{1,0:T(8,128)(2,1)}, u32[]{:S(2)}, u32[]{:S(2)}) %collective-permute-start.3) | collective-permute-done | bytes 393248 | tf_op jit(solution)/shard_map/ppermute | solution.py:38
  51.1 5.2 %collective-permute-done.10.refs_3_.refs_19_ = bf16[128,1024]{1,0:T(8,128)(2,1)S(1)} collective-permute-done((bf16[128,1024]{1,0:T(8,128)(2,1)}, bf16[128,1024]{1,0:T(8,128)(2,1)S(1)}, u32[]{:S(2)}, u32[]{:S(2)}) %collective-permute-start.10) | collective-permute-done | bytes 262176 | tf_op jit(solution)/shard_map/ppermute | solution.py:38
  56.3 9.5 %collective-permute-done.11.refs_11_.refs_3_ = bf16[128,1024]{1,0:T(8,128)(2,1)S(1)} collective-permute-done((bf16[128,1024]{1,0:T(8,128)(2,1)}, bf16[128,1024]{1,0:T(8,128)(2,1)S(1)}, u32[]{:S(2)}, u32[]{:S(2)}) %collective-permute-start.11) | collective-permute-done | bytes 262176 | tf_op jit(solution)/shard_map/ppermute | solution.py:38
  66.5 3.5 shard_map.187
  78.6 9.4 %shard_map.188.q_ref.k_ref.v_ref = f32[2,512,1536]{2,1,0:T(8,128)} custom-call(s32[12]{0:T(128)} %stack.51.order, bf16[512,1024]{1,0:T(8,128)(2,1)} %get-tuple-element.188.h_ref.h_in_ref.hy_ref, bf16[128,1536]{1,0:T(8,128)(2,1)} %get-tuple-element.177.refs_0_, bf16[128,1536]{1,0:T(8,128)(2,1)} %copy-done.15, bf16[128,1536]{1,0:T(8,128)(2,1)} %copy-done.14, ...), custom_call_target="tpu_custom_call" | custom-call | flops 805306368 | bytes 3407872 | tf_op jit(solution)/shard_map/pallas_call | solution.py:242
  88.0 8.4 %shard_map.189.mix_ref = bf16[512,1024]{1,0:T(8,128)(2,1)} custom-call(s32[12]{0:T(128)} %stack.51.order, f32[2,512,1536]{2,1,0:T(8,128)} %shard_map.188.q_ref.k_ref.v_ref, f32[2,512,1536]{2,1,0:T(8,128)} %shard_map.188.q_ref.k_ref.v_ref, f32[2,512,1536]{2,1,0:T(8,128)} %shard_map.188.q_ref.k_ref.v_ref, f32[512,128]{1,0:T(8,128)} %get-tuple-element.193.cos_ref, ...), custom_call_target="tpu_custom_call" | custom-call | flops 100663296 | bytes 5112832 | tf_op jit(solution)/shard_map/pallas_call | solution.py:242
  96.4 9.4 %shard_map.190 = (f32[512,1024]{1,0:T(8,128)}, bf16[512,1024]{1,0:T(8,128)(2,1)}, bf16[512,1024]{1,0:T(8,128)(2,1)}, f32[512,1024]{1,0:T(8,128)}, bf16[512,1024]{1,0:T(8,128)(2,1)}, /*index=5*/bf16[512,1024]{1,0:T(8,128)(2,1)}) custom-call(s32[12]{0:T(128)} %stack.51.order, bf16[512,1024]{1,0:T(8,128)(2,1)} %shard_map.189.mix_ref, ...), custom_call_target="tpu_custom_call" | custom-call | flops 268435456 | bytes 3932160 | tf_op jit(solution)/shard_map/pallas_call | solution.py:242
  108.1 4.8 %all-to-all-start.1 = ((bf16[4,128,1024]{2,1,0:T(8,128)(2,1)}), bf16[4,128,1024]{2,1,0:T(8,128)(2,1)S(1)}, u32[]{:S(2)}, u32[]{:S(2)}) async-start(bf16[4,128,1024]{2,1,0:T(8,128)(2,1)} %param.13), calls=%async_computation.1 | async-start | bytes 2097152 | tf_op jit(solution)/shard_map/all_to_all | solution.py:1083
  115.7 8.9 %collective-permute-done.32.refs_3_ = bf16[128,2816]{1,0:T(8,128)(2,1)} collective-permute-done((bf16[128,2816]{1,0:T(8,128)(2,1)}, bf16[128,2816]{1,0:T(8,128)(2,1)}, u32[]{:S(2)}, u32[]{:S(2)}) %collective-permute-start.32) | collective-permute-done | bytes 720928 | tf_op jit(solution)/shard_map/ppermute | solution.py:38
  133.3 12.2 %shard_map.192 = (bf16[512,2816]{1,0:T(8,128)(2,1)}, bf16[512,2816]{1,0:T(8,128)(2,1)}, bf16[512,2816]{1,0:T(8,128)(2,1)}) custom-call(s32[12]{0:T(128)} %stack.51.order, bf16[512,1024]{1,0:T(8,128)(2,1)} %get-tuple-element.212.h_ref.hy_ref, bf16[128,2816]{1,0:T(8,128)(2,1)} %refs_0_.5, bf16[128,2816]{1,0:T(8,128)(2,1)} %collective-permute-done.28.refs_1_, ...), custom_call_target="tpu_custom_call" | custom-call | flops 1476395008 | bytes 5308416 | tf_op jit(solution)/shard_map/pallas_call | solution.py:242
  150.0 6.8 %convolution_convert_fusion = bf16[2816,1024]{1,0:T(8,128)(2,1)} fusion(bf16[512,2816]{1,0:T(8,128)(2,1)} %get-tuple-element.230.product_ref, bf16[512,1024]{1,0:T(8,128)(2,1)S(1)} %bitcast.27), kind=kOutput, calls=%fused_computation | convolution fusion | flops 2955673600 | bytes 9699328 | tf_op jit(solution)/shard_map/dot_general | solution.py:29
  165.5 36.3 %shard_map.193 = (bf16[512,2816]{1,0:T(8,128)(2,1)}, bf16[512,2816]{1,0:T(8,128)(2,1)}, bf16[512,2816]{1,0:T(8,128)(2,1)}, bf16[512,2816]{1,0:T(8,128)(2,1)}, f3...) custom-call(s32[12]{0:T(128)} %stack.51.order, ...), custom_call_target="tpu_custom_call" | custom-call | flops 4429185024 | bytes 11730944 | tf_op jit(solution)/shard_map/pallas_call | solution.py:242
  202.4 7.1 %shard_map.194 = (bf16[512,1024]{1,0:T(8,128)(2,1)}, bf16[512,1024]{1,0:T(8,128)(2,1)}) custom-call(s32[12]{0:T(128)} %stack.51.order, bf16[512,1024]{1,0:T(8,128)(2,1)} %get-tuple-element.257.d_ref.db, bf16[512,1024]{1,0:T(8,128)(2,1)} %shard_map.189.mix_ref, f32[512,1024]{1,0:T(8,128)} %get-tuple-element.258.u_ref, bf16[128,1024]{1,0:T(8,128)(2,1)} %refs_0_.6, ...), custom_call_target="tpu_custom_call" | custom-call | flops 268435456 | bytes 2097152 | tf_op jit(solution)/shard_map/pallas_call | solution.py:242
  211.6 4.5 %add_convert_fusion = (bf16[256,2816]{1,0:T(8,128)(2,1)}, bf16[256,2816]{1,0:T(8,128)(2,1)}) fusion(bf16[512,2816]{1,0:T(8,128)(2,1)} %collective-permute-done.57, bf16[512,2816]{1,0:T(8,128)(2,1)} %get-tuple-element.263, bf16[512,2816]{1,0:T(8,128)(2,1)} %collective-permute-done.56, bf16[512,2816]{1,0:T(8,128)(2,1)S(1)} %copy-done.4), kind=kLoop, calls=%fused_computation.1 | loop fusion | flops 5767168 | bytes 8650752 | tf_op jit(solution)/shard_map/convert_element_type | solution.py:125
  216.1 4.8 %all-to-all-start.2 = ((bf16[4,128,1024]{2,1,0:T(8,128)(2,1)}), bf16[4,128,1024]{2,1,0:T(8,128)(2,1)S(1)}, u32[]{:S(2)}, u32[]{:S(2)}) async-start(bf16[4,128,1024]{2,1,0:T(8,128)(2,1)} %bitcast.18), calls=%async_computation.3 | async-start | bytes 2097152 | tf_op jit(solution)/shard_map/all_to_all | solution.py:1083
  222.9 11.1 %shard_map.195.d_ref = bf16[2,3,512,512]{3,2,1,0:T(8,128)(2,1)} custom-call(s32[12]{0:T(128)} %stack.51.order, f32[2,512,1536]{2,1,0:T(8,128)} %shard_map.188.q_ref.k_ref.v_ref, f32[2,512,1536]{2,1,0:T(8,128)} %shard_map.188.q_ref.k_ref.v_ref, f32[2,512,1536]{2,1,0:T(8,128)} %shard_map.188.q_ref.k_ref.v_ref, bf16[512,1024]{1,0:T(8,128)(2,1)} %get-tuple-element.268.dm_ref, ...), custom_call_target="tpu_custom_call" | custom-call | flops 268435456 | bytes 5899264 | tf_op jit(solution)/shard_map/pallas_call | solution.py:242
  237.2 11.9 %shard_map.197 = (bf16[512,2560]{1,0:T(8,128)(2,1)}, bf16[512,2560]{1,0:T(8,128)(2,1)}, bf16[512,2560]{1,0:T(8,128)(2,1)}, bf16[512,2560]{1,0:T(8,128)(2,1)}) custom-call(s32[12]{0:T(128)} %stack.51.order, bf16[512,1024]{1,0:T(8,128)(2,1)} %get-tuple-element.187.hx_ref, bf16[512,1024]{1,0:T(8,128)(2,1)} %get-tuple-element.188.h_ref.h_in_ref.hy_ref, ...), custom_call_target="tpu_custom_call" | custom-call | flops 1342177280 | bytes 4980736 | tf_op jit(solution)/shard_map/pallas_call | solution.py:242
  249.1 5.5 %collective-permute-done.58 = bf16[256,2816]{1,0:T(8,128)(2,1)S(1)} collective-permute-done((bf16[256,2816]{1,0:T(8,128)(2,1)}, bf16[256,2816]{1,0:T(8,128)(2,1)S(1)}, u32[]{:S(2)}, u32[]{:S(2)}) %collective-permute-start.58) | collective-permute-done | bytes 1441824 | tf_op jit(solution)/shard_map/ppermute | solution.py:38
  257.4 3.6 add_convert_fusion.4
  281.0 12.1 %shard_map.199 = bf16[512,1024]{1,0:T(8,128)(2,1)} custom-call(s32[12]{0:T(128)} %stack.51.order, bf16[512,1024]{1,0:T(8,128)(2,1)} %bitcast.26, f32[512,1024]{1,0:T(8,128)} %get-tuple-element.299.d_mid_ref, bf16[512,1024]{1,0:T(8,128)(2,1)} %get-tuple-element.274.du.du_ref, bf16[2,3,512,512]{3,2,1,0:T(8,128)(2,1)} %shard_map.195.d_ref, ...), custom_call_target="tpu_custom_call" | custom-call | flops 1073741824 | bytes 4194304 | tf_op jit(solution)/shard_map/pallas_call | solution.py:242
  295.5 3.5 all-to-all-start.3
  299.0 4.7 %shard_map.200 = (f32[4,128,704]{2,1,0:T(8,128)}, bf16[4,128,704]{2,1,0:T(8,128)(2,1)}) custom-call(s32[12]{0:T(128)} %stack.51.order, bf16[128,2816]{1,0:T(8,128)(2,1)} %get-tuple-element.302.refs_0_, bf16[128,2816]{1,0:T(8,128)(2,1)} %copy-done.26, bf16[128,2816]{1,0:T(8,128)(2,1)} %get-tuple-element.304.refs_2_, bf16[128,2816]{1,0:T(8,128)(2,1)} %copy-done.27), custom_call_target="tpu_custom_call" | custom-call | bytes 1261568 | tf_op jit(solution)/shard_map/pallas_call | solution.py:242
  310.6 12.7 %collective-permute-done.66 = bf16[256,2560]{1,0:T(8,128)(2,1)S(1)} collective-permute-done((bf16[256,2560]{1,0:T(8,128)(2,1)}, bf16[256,2560]{1,0:T(8,128)(2,1)S(1)}, u32[]{:S(2)}, u32[]{:S(2)}) %collective-permute-start.66) | collective-permute-done | bytes 1310752 | tf_op jit(solution)/shard_map/ppermute | solution.py:38
  323.7 3.7 add_convert_fusion.8
  338.4 3.4 shard_map.202
  348.7 4.0 shard_map.203
  352.7 7.2 %collective-permute-done.71.got_ref = bf16[2,128,704]{2,1,0:T(8,128)(2,1)S(1)} collective-permute-done((bf16[2,128,704]{2,1,0:T(8,128)(2,1)}, bf16[2,128,704]{2,1,0:T(8,128)(2,1)S(1)}, u32[]{:S(2)}, u32[]{:S(2)}) %collective-permute-start.71) | collective-permute-done | bytes 360480 | tf_op jit(solution)/shard_map/ppermute | solution.py:200
  363.4 12.8 %collective-permute-done.72.got_ref = bf16[10,128,256]{2,1,0:T(8,128)(2,1)S(1)} collective-permute-done((bf16[10,128,256]{2,1,0:T(8,128)(2,1)}, bf16[10,128,256]{2,1,0:T(8,128)(2,1)S(1)}, u32[]{:S(2)}, u32[]{:S(2)}) %collective-permute-start.72) | collective-permute-done | bytes 655392 | tf_op jit(solution)/shard_map/ppermute | solution.py:200
  377.1 3.2 shard_map.205
  383.6 13.1 %collective-permute-done.73.got_ref = bf16[5,128,256]{2,1,0:T(8,128)(2,1)S(1)} collective-permute-done((bf16[5,128,256]{2,1,0:T(8,128)(2,1)}, bf16[5,128,256]{2,1,0:T(8,128)(2,1)S(1)}, u32[]{:S(2)}, u32[]{:S(2)}) %collective-permute-start.73) | collective-permute-done | bytes 327712 | tf_op jit(solution)/shard_map/ppermute | solution.py:200
  (275 shorter events, 128.9 us)
Async XLA Ops:
  7.2 38.1 %all-to-all-start = ((bf16[4,128,1024]{2,1,0:T(8,128)(2,1)}), bf16[4,128,1024]{2,1,0:T(8,128)(2,1)S(1)}, u32[]{:S(2)}, u32[]{:S(2)}) async-start(bf16[4,128,1024]{2,1,0:T(8,128)(2,1)} %param.11), calls=%async_computation | async-start | bytes 2097152 | tf_op jit(solution)/shard_map/all_to_all | solution.py:1083
  21.3 17.2 %collective-permute-start.2 = (bf16[128,1536]{1,0:T(8,128)(2,1)}, bf16[128,1536]{1,0:T(8,128)(2,1)S(1)}, u32[]{:S(2)}, u32[]{:S(2)}) collective-permute-start(bf16[128,1536]{1,0:T(8,128)(2,1)} %get-tuple-element.177.refs_0_), channel_id=1, source_target_pairs={{0,16},{4,20},{8,24},{12,28},{16,0},{20,4},{24,8},{28,12},{1,17},{... | collective-permute-start | bytes 1179656 | tf_op jit(solution)/shard_map/ppermute | solution.py:38
  26.2 19.1 %collective-permute-start.3 = (bf16[128,1536]{1,0:T(8,128)(2,1)}, bf16[128,1536]{1,0:T(8,128)(2,1)}, u32[]{:S(2)}, u32[]{:S(2)}) collective-permute-start(bf16[128,1536]{1,0:T(8,128)(2,1)} %get-tuple-element.178.refs_8_), channel_id=1, source_target_pairs={{0,16},{4,20},{8,24},{12,28},{16,0},{20,4},{24,8},{28,12},{1,17},{... | collective-permute-start | bytes 1179656 | tf_op jit(solution)/shard_map/ppermute | solution.py:38
  28.6 16.7 %collective-permute-start.1 = (bf16[128,1536]{1,0:T(8,128)(2,1)}, bf16[128,1536]{1,0:T(8,128)(2,1)}, u32[]{:S(2)}, u32[]{:S(2)}) collective-permute-start(bf16[128,1536]{1,0:T(8,128)(2,1)} %get-tuple-element.178.refs_8_), channel_id=1, source_target_pairs={{0,8},{4,12},{8,0},{12,4},{16,24},{20,28},{24,16},{28,20},{1,9},{5... | collective-permute-start | bytes 1179656 | tf_op jit(solution)/shard_map/ppermute | solution.py:38
  48.4 17.3 %collective-permute-start.8 = (bf16[128,1536]{1,0:T(8,128)(2,1)S(1)}, bf16[128,1536]{1,0:T(8,128)(2,1)S(1)}, u32[]{:S(2)}, u32[]{:S(2)}) collective-permute-start(bf16[128,1536]{1,0:T(8,128)(2,1)S(1)} %collective-permute-done.refs_1_), channel_id=1, source_target_pairs={{0,16},{4,20},{8,24},{12,28},{16,0},{20,4},{24,8},{28,12},{1,17},{... | collective-permute-start | bytes 1179656 | tf_op jit(solution)/shard_map/ppermute | solution.py:38
  49.0 17.3 %collective-permute-start.9 = (bf16[128,1536]{1,0:T(8,128)(2,1)}, bf16[128,1536]{1,0:T(8,128)(2,1)}, u32[]{:S(2)}, u32[]{:S(2)}) collective-permute-start(bf16[128,1536]{1,0:T(8,128)(2,1)} %collective-permute-done.3.refs_10_), channel_id=1, source_target_pairs={{0,8},{4,12},{8,0},{12,4},{16,24},{20,28},{24,16},{28,20},{1,9},{5... | collective-permute-start | bytes 1179656 | tf_op jit(solution)/shard_map/ppermute | solution.py:38
  51.1 19.4 %collective-permute-start.14 = (bf16[128,1536]{1,0:T(8,128)(2,1)S(1)}, bf16[128,1536]{1,0:T(8,128)(2,1)}, u32[]{:S(2)}, u32[]{:S(2)}) collective-permute-start(bf16[128,1536]{1,0:T(8,128)(2,1)S(1)} %collective-permute-done.2.refs_2_), channel_id=1, source_target_pairs={{0,4},{4,0},{8,12},{12,8},{16,20},{20,16},{24,28},{28,24},{1,5},{5... | collective-permute-start | bytes 1179656 | tf_op jit(solution)/shard_map/ppermute | solution.py:38
  70.6 35.2 %collective-permute-start.30 = (bf16[128,2816]{1,0:T(8,128)(2,1)S(1)}, bf16[128,2816]{1,0:T(8,128)(2,1)S(1)}, u32[]{:S(2)}, u32[]{:S(2)}) collective-permute-start(bf16[128,2816]{1,0:T(8,128)(2,1)S(1)} %copy-done.6), channel_id=1, source_target_pairs={{0,16},{4,20},{8,24},{12,28},{16,0},{20,4},{24,8},{28,12},{1,17},{... | collective-permute-start | bytes 2162696 | tf_op jit(solution)/shard_map/ppermute | solution.py:38
  71.7 34.0 %collective-permute-start.28 = (bf16[128,2816]{1,0:T(8,128)(2,1)S(1)}, bf16[128,2816]{1,0:T(8,128)(2,1)}, u32[]{:S(2)}, u32[]{:S(2)}) collective-permute-start(bf16[128,2816]{1,0:T(8,128)(2,1)S(1)} %copy-done.6), channel_id=1, source_target_pairs={{0,8},{4,12},{8,0},{12,4},{16,24},{20,28},{24,16},{28,20},{1,9},{5... | collective-permute-start | bytes 2162696 | tf_op jit(solution)/shard_map/ppermute | solution.py:38
  72.3 33.5 %collective-permute-start.31 = (bf16[128,2816]{1,0:T(8,128)(2,1)S(1)}, bf16[128,2816]{1,0:T(8,128)(2,1)}, u32[]{:S(2)}, u32[]{:S(2)}) collective-permute-start(bf16[128,2816]{1,0:T(8,128)(2,1)S(1)} %copy-done.7), channel_id=1, source_target_pairs={{0,16},{4,20},{8,24},{12,28},{16,0},{20,4},{24,8},{28,12},{1,17},{... | collective-permute-start | bytes 2162696 | tf_op jit(solution)/shard_map/ppermute | solution.py:38
  73.1 32.7 %collective-permute-start.29 = (bf16[128,2816]{1,0:T(8,128)(2,1)S(1)}, bf16[128,2816]{1,0:T(8,128)(2,1)S(1)}, u32[]{:S(2)}, u32[]{:S(2)}) collective-permute-start(bf16[128,2816]{1,0:T(8,128)(2,1)S(1)} %copy-done.7), channel_id=1, source_target_pairs={{0,8},{4,12},{8,0},{12,4},{16,24},{20,28},{24,16},{28,20},{1,9},{5... | collective-permute-start | bytes 2162696 | tf_op jit(solution)/shard_map/ppermute | solution.py:38
  77.5 18.8 %collective-permute-start.27 = (bf16[128,1024]{1,0:T(8,128)(2,1)}, bf16[128,1024]{1,0:T(8,128)(2,1)}, u32[]{:S(2)}, u32[]{:S(2)}) collective-permute-start(bf16[128,1024]{1,0:T(8,128)(2,1)} %copy-done.25), channel_id=1, source_target_pairs={{0,4},{4,0},{8,12},{12,8},{16,20},{20,16},{24,28},{28,24},{1,5},{5... | collective-permute-start | bytes 786440 | tf_op jit(solution)/shard_map/ppermute | solution.py:38
  105.8 18.8 %collective-permute-start.32 = (bf16[128,2816]{1,0:T(8,128)(2,1)}, bf16[128,2816]{1,0:T(8,128)(2,1)}, u32[]{:S(2)}, u32[]{:S(2)}) collective-permute-start(bf16[128,2816]{1,0:T(8,128)(2,1)} %collective-permute-done.28.refs_1_), channel_id=1, source_target_pairs={{0,16},{4,20},{8,24},{12,28},{16,0},{20,4},{24,8},{28,12},{1,17},{... | collective-permute-start | bytes 2162696 | tf_op jit(solution)/shard_map/ppermute | solution.py:38
  107.1 18.4 %collective-permute-start.33 = (bf16[128,2816]{1,0:T(8,128)(2,1)}, bf16[128,2816]{1,0:T(8,128)(2,1)}, u32[]{:S(2)}, u32[]{:S(2)}) collective-permute-start(bf16[128,2816]{1,0:T(8,128)(2,1)} %collective-permute-done.31.refs_10_), channel_id=1, source_target_pairs={{0,8},{4,12},{8,0},{12,4},{16,24},{20,28},{24,16},{28,20},{1,9},{5... | collective-permute-start | bytes 2162696 | tf_op jit(solution)/shard_map/ppermute | solution.py:38
  107.6 17.9 %collective-permute-start.34 = (bf16[128,2816]{1,0:T(8,128)(2,1)S(1)}, bf16[128,2816]{1,0:T(8,128)(2,1)}, u32[]{:S(2)}, u32[]{:S(2)}) collective-permute-start(bf16[128,2816]{1,0:T(8,128)(2,1)S(1)} %copy-done.6), channel_id=1, source_target_pairs={{0,4},{4,0},{8,12},{12,8},{16,20},{20,16},{24,28},{28,24},{1,5},{5... | collective-permute-start | bytes 2162696 | tf_op jit(solution)/shard_map/ppermute | solution.py:38
  107.6 18.4 %collective-permute-start.38 = (bf16[128,2816]{1,0:T(8,128)(2,1)S(1)}, bf16[128,2816]{1,0:T(8,128)(2,1)}, u32[]{:S(2)}, u32[]{:S(2)}) collective-permute-start(bf16[128,2816]{1,0:T(8,128)(2,1)S(1)} %copy-done.7), channel_id=1, source_target_pairs={{0,4},{4,0},{8,12},{12,8},{16,20},{20,16},{24,28},{28,24},{1,5},{5... | collective-permute-start | bytes 2162696 | tf_op jit(solution)/shard_map/ppermute | solution.py:38
  108.1 18.0 %collective-permute-start.36 = (bf16[128,2816]{1,0:T(8,128)(2,1)S(1)}, bf16[128,2816]{1,0:T(8,128)(2,1)}, u32[]{:S(2)}, u32[]{:S(2)}) collective-permute-start(bf16[128,2816]{1,0:T(8,128)(2,1)S(1)} %collective-permute-done.30.refs_2_), channel_id=1, source_target_pairs={{0,4},{4,0},{8,12},{12,8},{16,20},{20,16},{24,28},{28,24},{1,5},{5... | collective-permute-start | bytes 2162696 | tf_op jit(solution)/shard_map/ppermute | solution.py:38
  108.1 40.5 %all-to-all-start.1 = ((bf16[4,128,1024]{2,1,0:T(8,128)(2,1)}), bf16[4,128,1024]{2,1,0:T(8,128)(2,1)S(1)}, u32[]{:S(2)}, u32[]{:S(2)}) async-start(bf16[4,128,1024]{2,1,0:T(8,128)(2,1)} %param.13), calls=%async_computation.1 | async-start | bytes 2097152 | tf_op jit(solution)/shard_map/all_to_all | solution.py:1083
  112.9 121.1 %reduce-scatter.2.cloned.1.call-start = ((), (), s32[]{:S(2)}) async-start(), calls=%async_computation.5 | async-start | bytes 6488064 | tf_op jit(solution)/shard_map/reduce_scatter | solution.py:1133
  130.9 16.8 %collective-permute-start.45 = (bf16[352,512]{1,0:T(8,128)(2,1)}, bf16[352,512]{1,0:T(8,128)(2,1)}, u32[]{:S(2)}, u32[]{:S(2)}) collective-permute-start(bf16[352,512]{1,0:T(8,128)(2,1)} %get-tuple-element.227.refs_24_), channel_id=1, source_target_pairs={{0,16},{4,20},{8,24},{12,28},{16,0},{20,4},{24,8},{28,12},{1,17},{... | collective-permute-start | bytes 1081352 | tf_op jit(solution)/shard_map/ppermute | solution.py:38
  131.8 16.8 %collective-permute-start.43 = (bf16[352,512]{1,0:T(8,128)(2,1)}, bf16[352,512]{1,0:T(8,128)(2,1)}, u32[]{:S(2)}, u32[]{:S(2)}) collective-permute-start(bf16[352,512]{1,0:T(8,128)(2,1)} %get-tuple-element.227.refs_24_), channel_id=1, source_target_pairs={{0,8},{4,12},{8,0},{12,4},{16,24},{20,28},{24,16},{28,20},{1,9},{5... | collective-permute-start | bytes 1081352 | tf_op jit(solution)/shard_map/ppermute | solution.py:38
  216.1 39.0 %all-to-all-start.2 = ((bf16[4,128,1024]{2,1,0:T(8,128)(2,1)}), bf16[4,128,1024]{2,1,0:T(8,128)(2,1)S(1)}, u32[]{:S(2)}, u32[]{:S(2)}) async-start(bf16[4,128,1024]{2,1,0:T(8,128)(2,1)} %bitcast.18), calls=%async_computation.3 | async-start | bytes 2097152 | tf_op jit(solution)/shard_map/all_to_all | solution.py:1083
  220.9 33.6 %collective-permute-start.58 = (bf16[256,2816]{1,0:T(8,128)(2,1)}, bf16[256,2816]{1,0:T(8,128)(2,1)S(1)}, u32[]{:S(2)}, u32[]{:S(2)}) collective-permute-start(bf16[256,2816]{1,0:T(8,128)(2,1)} %get-tuple-element.277), channel_id=1, source_target_pairs={{0,8},{4,12},{8,0},{12,4},{16,24},{20,28},{24,16},{28,20},{1,9},{5... | collective-permute-start | bytes 4325384 | tf_op jit(solution)/shard_map/ppermute | solution.py:38
  221.8 33.3 %collective-permute-start.59 = (bf16[256,2816]{1,0:T(8,128)(2,1)}, bf16[256,2816]{1,0:T(8,128)(2,1)}, u32[]{:S(2)}, u32[]{:S(2)}) collective-permute-start(bf16[256,2816]{1,0:T(8,128)(2,1)} %get-tuple-element.278), channel_id=1, source_target_pairs={{0,16},{4,20},{8,24},{12,28},{16,0},{20,4},{24,8},{28,12},{1,17},{... | collective-permute-start | bytes 4325384 | tf_op jit(solution)/shard_map/ppermute | solution.py:38
  269.7 23.3 %collective-permute-start.65 = (bf16[1,352,256]{2,1,0:T(8,128)(2,1)}, bf16[1,352,256]{2,1,0:T(8,128)(2,1)S(1)}, u32[]{:S(2)}, u32[]{:S(2)}) collective-permute-start(bf16[1,352,256]{2,1,0:T(8,128)(2,1)} %get-tuple-element.301), channel_id=1, source_target_pairs={{0,2},{1,3},{2,0},{3,1},{4,6},{5,7},{6,4},{7,5},{8,10},{9,11},{10,... | collective-permute-start | bytes 540680 | tf_op jit(solution)/shard_map/ppermute | solution.py:200
  272.3 20.7 %collective-permute-start.63 = (bf16[128,2816]{1,0:T(8,128)(2,1)}, bf16[128,2816]{1,0:T(8,128)(2,1)S(1)}, u32[]{:S(2)}, u32[]{:S(2)}) collective-permute-start(bf16[128,2816]{1,0:T(8,128)(2,1)} %get-tuple-element.297), channel_id=1, source_target_pairs={{0,16},{4,20},{8,24},{12,28},{16,0},{20,4},{24,8},{28,12},{1,17},{... | collective-permute-start | bytes 2162696 | tf_op jit(solution)/shard_map/ppermute | solution.py:38
  273.5 19.6 %collective-permute-start.64 = (bf16[128,2816]{1,0:T(8,128)(2,1)S(1)}, bf16[128,2816]{1,0:T(8,128)(2,1)S(1)}, u32[]{:S(2)}, u32[]{:S(2)}) collective-permute-start(bf16[128,2816]{1,0:T(8,128)(2,1)S(1)} %get-tuple-element.298), channel_id=1, source_target_pairs={{0,8},{4,12},{8,0},{12,4},{16,24},{20,28},{24,16},{28,20},{1,9},{5... | collective-permute-start | bytes 2162696 | tf_op jit(solution)/shard_map/ppermute | solution.py:38
  294.0 29.2 %collective-permute-start.66 = (bf16[256,2560]{1,0:T(8,128)(2,1)}, bf16[256,2560]{1,0:T(8,128)(2,1)S(1)}, u32[]{:S(2)}, u32[]{:S(2)}) collective-permute-start(bf16[256,2560]{1,0:T(8,128)(2,1)} %add_convert_fusion.3), channel_id=1, source_target_pairs={{0,8},{4,12},{8,0},{12,4},{16,24},{20,28},{24,16},{28,20},{1,9},{5... | collective-permute-start | bytes 3932168 | tf_op jit(solution)/shard_map/ppermute | solution.py:38
  294.6 29.1 %collective-permute-start.67 = (bf16[256,2560]{1,0:T(8,128)(2,1)}, bf16[256,2560]{1,0:T(8,128)(2,1)}, u32[]{:S(2)}, u32[]{:S(2)}) collective-permute-start(bf16[256,2560]{1,0:T(8,128)(2,1)} %add_convert_fusion.2), channel_id=1, source_target_pairs={{0,16},{4,20},{8,24},{12,28},{16,0},{20,4},{24,8},{28,12},{1,17},{... | collective-permute-start | bytes 3932168 | tf_op jit(solution)/shard_map/ppermute | solution.py:38
  295.5 36.5 %all-to-all-start.3 = ((bf16[4,128,1024]{2,1,0:T(8,128)(2,1)}), bf16[4,128,1024]{2,1,0:T(8,128)(2,1)S(1)}, u32[]{:S(2)}, u32[]{:S(2)}) async-start(bf16[4,128,1024]{2,1,0:T(8,128)(2,1)} %bitcast.29), calls=%async_computation.4 | async-start | bytes 2097152 | tf_op jit(solution)/shard_map/all_to_all | solution.py:1083
  306.0 26.0 %collective-permute-start.68 = (bf16[4,128,704]{1,2,0:T(8,128)(2,1)}, bf16[4,128,704]{1,2,0:T(8,128)(2,1)}, u32[]{:S(2)}, u32[]{:S(2)}) collective-permute-start(bf16[4,128,704]{1,2,0:T(8,128)(2,1)} %copy.35), channel_id=1, source_target_pairs={{0,1},{1,0},{2,3},{3,2},{4,5},{5,4},{6,7},{7,6},{8,9},{9,8},{10,11... | collective-permute-start | bytes 2162696 | tf_op jit(solution)/shard_map/ppermute | solution.py:200
  341.8 18.1 %collective-permute-start.71 = (bf16[2,128,704]{2,1,0:T(8,128)(2,1)}, bf16[2,128,704]{2,1,0:T(8,128)(2,1)S(1)}, u32[]{:S(2)}, u32[]{:S(2)}) collective-permute-start(bf16[2,128,704]{2,1,0:T(8,128)(2,1)} %get-tuple-element.327), channel_id=1, source_target_pairs={{0,2},{1,3},{2,0},{3,1},{4,6},{5,7},{6,4},{7,5},{8,10},{9,11},{10,... | collective-permute-start | bytes 1081352 | tf_op jit(solution)/shard_map/ppermute | solution.py:200
  (99 other events, 950.0 us)
Sparse Core Ops, SparseCore 0:
  158.8 58.9 reduce-scatter.1

commit v4 on v3

--- a/solution.py
+++ b/solution.py
@@ -141,37 +141,33 @@
 
     def join_first(self):
         rows = self.keeps[0].shape[0] // 4
-        self.own, self.parts = (
-            [
-                added(k[at : at + rows], t[at : at + rows], g[at : at + rows])
-                for k, t, g in zip(self.keeps, self.theirs, self.got)
-            ]
-            for at in (0, rows)
-        )
+        terms = list(zip(self.keeps, self.theirs, self.got))
+        self.parts = [added(*(a[rows : 2 * rows] for a in t)) for t in terms]
+        self.own = [list(t) for t in terms]
 
     def second(self):
         self.got_last = [swap(p, 6 - b, 8) for p, b in zip(self.parts, self.bits)]
 
     def settle(self, block, starts):
-        return Settle(self.order, self.own, self.got_last, block, starts)
+        return Settle(self.order, [t + [g] for t, g in zip(self.own, self.got_last)], block, starts)
 
 
 class Settle:
-    def __init__(self, order, parts, got, block, starts):
+    def __init__(self, order, parts, block, starts):
         self.order, self.block, self.count = order, block, len(starts)
-        rows = self.rows = parts[0].shape[0]
-        widths = [p.shape[1] for p in parts]
-        each = 2 if got else 1
+        rows = self.rows = parts[0][-1].shape[0]
+        widths = [p[-1].shape[1] for p in parts]
+        counts = [len(p) for p in parts]
 
         def body(order, *refs):
-            own, out, held = refs[each * len(parts) :]
-            at = 0
-            for i, width in enumerate(widths):
-                total = refs[each * i][...].astype(F32)
-                if got:
-                    total += refs[each * i + 1][...].astype(F32)
+            own, out, held = refs[sum(counts) :]
+            at, first = 0, 0
+            for width, count in zip(widths, counts):
+                total = refs[first][...].astype(F32)
+                for ref in refs[first + 1 : first + count]:
+                    total += ref[...].astype(F32)
                 held[:, at : at + width] = total
-                at += width
+                at, first = at + width, first + count
             for z in range(4):
 
                 @pl.when(order[8] == z)
@@ -183,15 +179,16 @@
                             out[2 * i + j] = held[:, theirs : theirs + block].astype(BF16)
 
         self.own, self.out = call(
-            body, (1,), order,
-            [(a, whole_spec(*a.shape)) for terms in zip(parts, *([got] if got else [])) for a in terms],
-            [self.entry(2 * self.count, F32), self.entry(2 * self.count, BF16)],
-            scratch=[pltpu.VMEM((rows, sum(widths)), F32)],
-        )
-
-    def entry(self, count, dtype):
+            body, (2,), order,
+            [(a, pl.BlockSpec((rows // 2, a.shape[1]), lambda i, *_: (i, 0))) for p in parts for a in p],
+            [self.entry(2 * self.count, F32, 2), self.entry(2 * self.count, BF16, 2)],
+            scratch=[pltpu.VMEM((rows // 2, sum(widths)), F32)],
+        )
+
+    def entry(self, count, dtype, steps=1):
         shape = (count, self.rows, self.block)
-        return shape, dtype, pl.BlockSpec(shape, lambda *_: (0, 0, 0))
+        spec = pl.BlockSpec((count, self.rows // steps, self.block), lambda i, *_: (0, i, 0))
+        return shape, dtype, spec
 
     def given(self):
         return [(a, pl.BlockSpec(a.shape, lambda *_: (0, 0, 0))) for a in (self.own, self.got)]
@@ -212,14 +209,7 @@
         )
 
     def result(self):
-        def body(order, own_ref, got_ref, *outs):
-            for i, out in enumerate(outs):
-                out[...] = own_ref[i] + got_ref[i].astype(F32)
-
-        shape = (self.rows, self.block)
-        return call(
-            body, (1,), self.order, self.given(), [(shape, F32, whole_spec(*shape))] * self.count
-        )
+        return [self.own[i] + self.got[i].astype(F32) for i in range(self.count)]
 
 
 def at_block(order_ref, index, width):
@@ -1092,11 +1082,11 @@
         pack(order, [w_query, w_key, w_value], [[(i, at, half) for i in range(3)] for at in (0, half)])
     )
     qkv.first()
-    v.x = whole_row(tokens)
+    v.x = whole_row(after(tokens, uo.near_x[0]))
     v.extra = [a for a, _ in row.extra]
     ff = Gather([w_left, w_right])
     v.c = cotangent
-    tick((v, "x"), (qkv, "near_x"), (qkv, "near_y"), (uo, "near_x"), (uo, "near_y"), (uo, "pieces"), (v, "c"), (v, "extra"))
+    tick((qkv, "near_x"), (qkv, "near_y"), (uo, "near_x"), (uo, "near_y"), (uo, "pieces"), (v, "c"), (v, "extra"))
     row.extra = [(a, spec) for a, (_, spec) in zip(v.extra, row.extra)]
     qkv.second()
     uo.second()
@@ -1146,38 +1136,39 @@
     r_ff.first()
     v.act = exchanged(v.act)
     v.d = row.mix_back(v.pre, v.d_mix)
-    tick((v, "d"), (v, "sum_down"))
-    s_down = Settle(order, [v.sum_down], None, half // 2, [lambda z: z * (half // 2)])
-    tick((v, "d"), (s_down, "out"))
-    s_down.pass_on(1)
+    tick((v, "d"))
+    v.back = row.in_back(v.x, v.d_mid, v.d, v.d_u, qkv, uo)
+    tick((v, "back"), (v, "d"), (v, "act"))
+    v.back = exchanged(v.back)
     r_att = row.weight_grads(v.h[1], v.h[0], v.gated_x, v.gated, v.d, v.d_u, v.d_branch)
-    tick((r_att, "sends"), (r_ff, "got"), (v, "act"), (v, "d"))
+    tick((r_att, "sends"), (r_ff, "got"), (v, "sum_down"))
     r_att.core()
     r_ff.join_first()
-    tick((r_att, "theirs"), (r_ff, "parts"), (v, "d"), (s_down, "got"))
+    tick((r_att, "theirs"), (r_ff, "parts"), (v, "sum_down"))
     r_ff.second()
-    s_down.join()
-    tick((s_down, "out"), (r_att, "theirs"), (v, "d"))
-    s_down.pass_on(2)
     r_att.join()
-    v.back = row.in_back(v.x, v.d_mid, v.d, v.d_u, qkv, uo)
-    tick((r_att, "totals"), (r_ff, "got_last"), (r_ff, "own"), (v, "back"), (s_down, "got"))
+    sum_down = after(v.sum_down, *r_att.totals)
+    s_down = Settle(order, [[sum_down]], half // 2, [lambda z: z * (half // 2)])
+    tick((r_att, "totals"), (r_ff, "got_last"), (s_down, "out"))
     r_att.first()
-    v.back = exchanged(v.back)
+    s_down.pass_on(1)
     quarter = inner // 4
     s_ff = r_ff.settle(quarter, [lambda z: z * quarter, lambda z: inner + z * quarter])
-    tick((s_ff, "out"))
+    tick((s_ff, "out"), (s_down, "got"))
     s_ff.pass_on(1)
+    s_down.join()
+    tick((s_down, "out"), (v, "back"))
+    v.back = v.back.astype(F32)
+    tick((s_down, "out"), (s_ff, "got"), (v, "back"))
+    s_down.pass_on(2)
+    s_ff.join()
+    tick((s_ff, "out"), (r_att, "got"), (s_down, "got"))
+    s_ff.pass_on(2)
+    r_att.join_first()
+    tick((r_att, "parts"), (s_down, "got"))
+    r_att.second()
     (v.g_down,) = s_down.result()
-    tick((r_att, "got"), (v, "g_down"))
-    r_att.join_first()
-    tick((r_att, "parts"), (s_ff, "got"), (v, "back"))
-    r_att.second()
-    s_ff.join()
-    v.back = v.back.astype(F32)
-    tick((s_ff, "out"), (v, "back"))
-    s_ff.pass_on(2)
-    tick((r_att, "got_last"), (r_att, "own"))
+    tick((r_att, "got_last"), (v, "g_down"))
     s_att = r_att.settle(
         half // 2,
         [

time: 416 us -> 396 us (0.952)
  Pallas kernels: 156 us -> 148 us
  waiting for transfers between devices: 117 us -> 110 us
    ppermute x68, waiting for transfers between devices: 80.3 us -> 70.2 us  [swap(): return lax.ppermute(value, 'rows', [(i, i ^ bit) for i in range(size)])]
    pallas_call x21 -> x18, Pallas kernels: 156 us -> 148 us  [call(): pl.pallas_call(body, grid_spec=pltpu.PrefetchScalarGridSpec(num_scalar_pr...]
    convert_element_type x7, other arithmetic: 23.7 us -> 18.8 us  [added(): functools.reduce(lambda a, b: a + b, [t.astype(F32) for t in terms])]
    unnamed x107 -> x105, local copies, waits for them, and re-layouts: 9.99 us -> 9.26 us
  transfers between devices with their start and end apart: 79 -> 79, of which waited for: 32 -> 30; matrix products, arithmetic and copies ran while one was open for 10% -> 9% of each run, Pallas kernels for 36% -> 37%
where the time goes in v4:
time: 396 us; the launch traced here: 389 us
  Pallas kernels  148 us (37%)
  waiting for transfers between devices  110 us (28%)
  starting transfers between devices  68.7 us (17%)
  other arithmetic  26.5 us (7%)
  between operations  15 us (4%)
  local copies, waits for them, and re-layouts  14.2 us (4%)
  matrix products  6.82 us (2%)
    pallas_call x18, Pallas kernels, call(): pl.pallas_call(body, grid_spec=pltpu.PrefetchScalarGridSpec(num_scalar_pr...  148 us
    ppermute x68, waiting for transfers between devices, swap(): return lax.ppermute(value, 'rows', [(i, i ^ bit) for i in range(size)])  70.2 us
    ppermute x68, starting transfers between devices, swap(): return lax.ppermute(value, 'rows', [(i, i ^ bit) for i in range(size)])  41.7 us
    ppermute x6, waiting for transfers between devices, pass_on(): self.got = lax.ppermute(self.out, 'heads', [(i, i ^ bit) for i in range(4)])  38.4 us
    all_to_all x4, starting transfers between devices, exchanged(): return lax.all_to_all(a.reshape(4, size, width), 'heads', 0, 0, tiled=True)  19.3 us
    convert_element_type x7, other arithmetic, added(): functools.reduce(lambda a, b: a + b, [t.astype(F32) for t in terms])  18.8 us
    unnamed x105, local copies, waits for them, and re-layouts  9.26 us
  transfers between devices with their start and end apart: 79, of which 30 were waited for; matrix products, arithmetic and copies ran while one was open for 9% of the time, Pallas kernels for 37%

profile of v4, /device:TPU:0, one launch (start us, length us, event | category | flops | bytes accessed | tf_op | source)
XLA Modules:
  0.0 388.9 jit_solution(7503382155683429789)
XLA Ops:
  7.2 3.0 collective-permute-start
  19.6 4.9 %all-to-all-start = ((bf16[4,128,1024]{2,1,0:T(8,128)(2,1)}), bf16[4,128,1024]{2,1,0:T(8,128)(2,1)S(1)}, u32[]{:S(2)}, u32[]{:S(2)}) async-start(bf16[4,128,1024]{2,1,0:T(8,128)(2,1)} %param.11), calls=%async_computation | async-start | bytes 2097152 | tf_op jit(solution)/shard_map/all_to_all | solution.py:1073
  28.9 4.9 %collective-permute-done.3.refs_2_ = bf16[128,1536]{1,0:T(8,128)(2,1)} collective-permute-done((bf16[128,1536]{1,0:T(8,128)(2,1)}, bf16[128,1536]{1,0:T(8,128)(2,1)}, u32[]{:S(2)}, u32[]{:S(2)}) %collective-permute-start.3) | collective-permute-done | bytes 393248 | tf_op jit(solution)/shard_map/ppermute | solution.py:38
  33.9 6.9 %collective-permute-done.4.refs_10_ = bf16[128,1536]{1,0:T(8,128)(2,1)} collective-permute-done((bf16[128,1536]{1,0:T(8,128)(2,1)S(1)}, bf16[128,1536]{1,0:T(8,128)(2,1)}, u32[]{:S(2)}, u32[]{:S(2)}) %collective-permute-start.4) | collective-permute-done | bytes 393248 | tf_op jit(solution)/shard_map/ppermute | solution.py:38
  46.5 5.2 %collective-permute-done.10.refs_3_.refs_19_ = bf16[128,1024]{1,0:T(8,128)(2,1)S(1)} collective-permute-done((bf16[128,1024]{1,0:T(8,128)(2,1)}, bf16[128,1024]{1,0:T(8,128)(2,1)S(1)}, u32[]{:S(2)}, u32[]{:S(2)}) %collective-permute-start.10) | collective-permute-done | bytes 262176 | tf_op jit(solution)/shard_map/ppermute | solution.py:38
  51.7 9.5 %collective-permute-done.11.refs_11_.refs_3_ = bf16[128,1024]{1,0:T(8,128)(2,1)S(1)} collective-permute-done((bf16[128,1024]{1,0:T(8,128)(2,1)}, bf16[128,1024]{1,0:T(8,128)(2,1)S(1)}, u32[]{:S(2)}, u32[]{:S(2)}) %collective-permute-start.11) | collective-permute-done | bytes 262176 | tf_op jit(solution)/shard_map/ppermute | solution.py:38
  62.9 3.5 shard_map.187
  74.9 9.5 %shard_map.188.q_ref.k_ref.v_ref = f32[2,512,1536]{2,1,0:T(8,128)} custom-call(s32[12]{0:T(128)} %stack.51.order, bf16[512,1024]{1,0:T(8,128)(2,1)} %get-tuple-element.175.h_ref.h_in_ref.hy_ref, bf16[128,1536]{1,0:T(8,128)(2,1)} %get-tuple-element.166.refs_0_, bf16[128,1536]{1,0:T(8,128)(2,1)} %collective-permute-done.1.refs_1_, ...), custom_call_target="tpu_custom_call" | custom-call | flops 805306368 | bytes 3407872 | tf_op jit(solution)/shard_map/pallas_call | solution.py:232
  84.5 8.3 %shard_map.189.mix_ref = bf16[512,1024]{1,0:T(8,128)(2,1)} custom-call(s32[12]{0:T(128)} %stack.51.order, f32[2,512,1536]{2,1,0:T(8,128)} %shard_map.188.q_ref.k_ref.v_ref, f32[2,512,1536]{2,1,0:T(8,128)} %shard_map.188.q_ref.k_ref.v_ref, f32[2,512,1536]{2,1,0:T(8,128)} %shard_map.188.q_ref.k_ref.v_ref, f32[512,128]{1,0:T(8,128)} %get-tuple-element.180.cos_ref, ...), custom_call_target="tpu_custom_call" | custom-call | flops 100663296 | bytes 5112832 | tf_op jit(solution)/shard_map/pallas_call | solution.py:232
  92.8 9.4 %shard_map.190 = (f32[512,1024]{1,0:T(8,128)}, bf16[512,1024]{1,0:T(8,128)(2,1)}, bf16[512,1024]{1,0:T(8,128)(2,1)}, f32[512,1024]{1,0:T(8,128)}, bf16[512,1024]{1,0:T(8,128)(2,1)}, /*index=5*/bf16[512,1024]{1,0:T(8,128)(2,1)}) custom-call(s32[12]{0:T(128)} %stack.51.order, bf16[512,1024]{1,0:T(8,128)(2,1)} %shard_map.189.mix_ref, ...), custom_call_target="tpu_custom_call" | custom-call | flops 268435456 | bytes 3932160 | tf_op jit(solution)/shard_map/pallas_call | solution.py:232
  104.5 4.9 %all-to-all-start.1 = ((bf16[4,128,1024]{2,1,0:T(8,128)(2,1)}), bf16[4,128,1024]{2,1,0:T(8,128)(2,1)S(1)}, u32[]{:S(2)}, u32[]{:S(2)}) async-start(bf16[4,128,1024]{2,1,0:T(8,128)(2,1)} %param.13), calls=%async_computation.1 | async-start | bytes 2097152 | tf_op jit(solution)/shard_map/all_to_all | solution.py:1073
  112.2 8.8 %collective-permute-done.32.refs_3_ = bf16[128,2816]{1,0:T(8,128)(2,1)} collective-permute-done((bf16[128,2816]{1,0:T(8,128)(2,1)}, bf16[128,2816]{1,0:T(8,128)(2,1)}, u32[]{:S(2)}, u32[]{:S(2)}) %collective-permute-start.32) | collective-permute-done | bytes 720928 | tf_op jit(solution)/shard_map/ppermute | solution.py:38
  129.7 12.2 %shard_map.192 = (bf16[512,2816]{1,0:T(8,128)(2,1)}, bf16[512,2816]{1,0:T(8,128)(2,1)}, bf16[512,2816]{1,0:T(8,128)(2,1)}) custom-call(s32[12]{0:T(128)} %stack.51.order, bf16[512,1024]{1,0:T(8,128)(2,1)} %get-tuple-element.197.h_ref.hy_ref, bf16[128,2816]{1,0:T(8,128)(2,1)} %refs_0_.5, bf16[128,2816]{1,0:T(8,128)(2,1)} %collective-permute-done.28.refs_1_, ...), custom_call_target="tpu_custom_call" | custom-call | flops 1476395008 | bytes 5308416 | tf_op jit(solution)/shard_map/pallas_call | solution.py:232
  146.4 6.8 %convolution_convert_fusion = bf16[2816,1024]{1,0:T(8,128)(2,1)} fusion(bf16[512,2816]{1,0:T(8,128)(2,1)} %get-tuple-element.215.product_ref, bf16[512,1024]{1,0:T(8,128)(2,1)S(1)} %bitcast.43), kind=kOutput, calls=%fused_computation | convolution fusion | flops 2955673600 | bytes 9699328 | tf_op jit(solution)/shard_map/dot_general | solution.py:29
  162.0 36.3 %shard_map.193 = (bf16[512,2816]{1,0:T(8,128)(2,1)}, bf16[512,2816]{1,0:T(8,128)(2,1)}, bf16[512,2816]{1,0:T(8,128)(2,1)}, bf16[512,2816]{1,0:T(8,128)(2,1)}, f3...) custom-call(s32[12]{0:T(128)} %stack.51.order, ...), custom_call_target="tpu_custom_call" | custom-call | flops 4429185024 | bytes 11730944 | tf_op jit(solution)/shard_map/pallas_call | solution.py:232
  198.9 7.1 %shard_map.194 = (bf16[512,1024]{1,0:T(8,128)(2,1)}, bf16[512,1024]{1,0:T(8,128)(2,1)}) custom-call(s32[12]{0:T(128)} %stack.51.order, bf16[512,1024]{1,0:T(8,128)(2,1)} %get-tuple-element.242.d_ref.db, bf16[512,1024]{1,0:T(8,128)(2,1)} %shard_map.189.mix_ref, f32[512,1024]{1,0:T(8,128)} %get-tuple-element.243.u_ref, bf16[128,1024]{1,0:T(8,128)(2,1)} %refs_0_.6, ...), custom_call_target="tpu_custom_call" | custom-call | flops 268435456 | bytes 2097152 | tf_op jit(solution)/shard_map/pallas_call | solution.py:232
  208.1 4.5 %add_convert_fusion = (bf16[256,2816]{1,0:T(8,128)(2,1)}, bf16[256,2816]{1,0:T(8,128)(2,1)}) fusion(bf16[512,2816]{1,0:T(8,128)(2,1)} %collective-permute-done.57.refs_5_, bf16[512,2816]{1,0:T(8,128)(2,1)} %get-tuple-element.250.refs_4_, bf16[512,2816]{1,0:T(8,128)(2,1)} %collective-permute-done.56.refs_1_, bf16[512,2816]{1,0:T(8,128)(2,1)S(1)} %copy-done.3), kind=kLoop, calls=%fused_computation.1 | loop fusion | flops 5767168 | bytes 8650752 | tf_op jit(solution)/shard_map/convert_element_type | solution.py:125
  212.6 5.1 %all-to-all-start.2 = ((bf16[4,128,1024]{2,1,0:T(8,128)(2,1)}), bf16[4,128,1024]{2,1,0:T(8,128)(2,1)}, u32[]{:S(2)}, u32[]{:S(2)}) async-start(bf16[4,128,1024]{2,1,0:T(8,128)(2,1)} %bitcast.46), calls=%async_computation.2 | async-start | bytes 2097152 | tf_op jit(solution)/shard_map/all_to_all | solution.py:1073
  219.8 11.1 %shard_map.195.d_ref = bf16[2,3,512,512]{3,2,1,0:T(8,128)(2,1)} custom-call(s32[12]{0:T(128)} %stack.51.order, f32[2,512,1536]{2,1,0:T(8,128)} %shard_map.188.q_ref.k_ref.v_ref, f32[2,512,1536]{2,1,0:T(8,128)} %shard_map.188.q_ref.k_ref.v_ref, f32[2,512,1536]{2,1,0:T(8,128)} %shard_map.188.q_ref.k_ref.v_ref, bf16[512,1024]{1,0:T(8,128)(2,1)} %get-tuple-element.255.dm_ref, ...), custom_call_target="tpu_custom_call" | custom-call | flops 268435456 | bytes 5899264 | tf_op jit(solution)/shard_map/pallas_call | solution.py:232
  230.9 12.0 %shard_map.196 = bf16[512,1024]{1,0:T(8,128)(2,1)} custom-call(s32[12]{0:T(128)} %stack.51.order, bf16[512,1024]{1,0:T(8,128)(2,1)} %bitcast.42, f32[512,1024]{1,0:T(8,128)} %get-tuple-element.239.d_mid_ref, bf16[512,1024]{1,0:T(8,128)(2,1)} %get-tuple-element.247.du_ref.du, bf16[2,3,512,512]{3,2,1,0:T(8,128)(2,1)} %shard_map.195.d_ref, ...), custom_call_target="tpu_custom_call" | custom-call | flops 1073741824 | bytes 4194304 | tf_op jit(solution)/shard_map/pallas_call | solution.py:232
  243.9 11.9 %shard_map.197 = (bf16[512,2560]{1,0:T(8,128)(2,1)}, bf16[512,2560]{1,0:T(8,128)(2,1)}, bf16[512,2560]{1,0:T(8,128)(2,1)}, bf16[512,2560]{1,0:T(8,128)(2,1)}) custom-call(s32[12]{0:T(128)} %stack.51.order, bf16[512,1024]{1,0:T(8,128)(2,1)} %get-tuple-element.258.hx_ref, bf16[512,1024]{1,0:T(8,128)(2,1)} %get-tuple-element.175.h_ref.h_in_ref.hy_ref, ...), custom_call_target="tpu_custom_call" | custom-call | flops 1342177280 | bytes 4980736 | tf_op jit(solution)/shard_map/pallas_call | solution.py:232
  256.4 4.5 %all-to-all-start.3 = ((bf16[4,128,1024]{2,1,0:T(8,128)(2,1)}), bf16[4,128,1024]{2,1,0:T(8,128)(2,1)}, u32[]{:S(2)}, u32[]{:S(2)}) async-start(bf16[4,128,1024]{2,1,0:T(8,128)(2,1)} %bitcast.45), calls=%async_computation.4 | async-start | bytes 2097152 | tf_op jit(solution)/shard_map/all_to_all | solution.py:1073
  276.6 8.0 %collective-permute-done.62.refs_3_ = bf16[128,2816]{1,0:T(8,128)(2,1)S(1)} collective-permute-done((bf16[128,2816]{1,0:T(8,128)(2,1)}, bf16[128,2816]{1,0:T(8,128)(2,1)S(1)}, u32[]{:S(2)}, u32[]{:S(2)}) %collective-permute-start.62) | collective-permute-done | bytes 720928 | tf_op jit(solution)/shard_map/ppermute | solution.py:38
  289.2 4.8 %shard_map.199 = (f32[4,128,704]{2,1,0:T(8,128)}, bf16[4,128,704]{2,1,0:T(8,128)(2,1)}) custom-call(s32[12]{0:T(128)} %stack.51.order, bf16[512,2816]{1,0:T(8,128)(2,1)} %get-tuple-element.248.refs_0_, bf16[512,2816]{1,0:T(8,128)(2,1)} %collective-permute-done.56.refs_1_, bf16[256,2816]{1,0:T(8,128)(2,1)} %collective-permute-done.58.refs_2_, ...), custom_call_target="tpu_custom_call" | custom-call | bytes 4505600 | tf_op jit(solution)/shard_map/pallas_call | solution.py:232
  305.4 8.4 %collective-permute-done.65 = bf16[4,128,704]{1,2,0:T(8,128)(2,1)S(1)} collective-permute-done((bf16[4,128,704]{1,2,0:T(8,128)(2,1)}, bf16[4,128,704]{1,2,0:T(8,128)(2,1)S(1)}, u32[]{:S(2)}, u32[]{:S(2)}) %collective-permute-start.65) | collective-permute-done | bytes 720928 | tf_op jit(solution)/shard_map/ppermute | solution.py:197
  313.8 3.2 collective-permute-start.68
  318.2 3.4 shard_map.201
  330.6 7.1 %collective-permute-done.69.refs_3_ = bf16[128,2560]{1,0:T(8,128)(2,1)S(1)} collective-permute-done((bf16[128,2560]{1,0:T(8,128)(2,1)S(1)}, bf16[128,2560]{1,0:T(8,128)(2,1)S(1)}, u32[]{:S(2)}, u32[]{:S(2)}) %collective-permute-start.69) | collective-permute-done | bytes 655392 | tf_op jit(solution)/shard_map/ppermute | solution.py:38
  340.0 4.5 %shard_map.202 = (f32[10,128,256]{2,1,0:T(8,128)}, bf16[10,128,256]{2,1,0:T(8,128)(2,1)}) custom-call(s32[12]{0:T(128)} %stack.51.order, bf16[512,2560]{1,0:T(8,128)(2,1)} %get-tuple-element.273.refs_0_, bf16[512,2560]{1,0:T(8,128)(2,1)} %collective-permute-done.60.refs_1_, bf16[256,2560]{1,0:T(8,128)(2,1)} %collective-permute-done.66.refs_2_, ...), custom_call_target="tpu_custom_call" | custom-call | bytes 4096000 | tf_op jit(solution)/shard_map/pallas_call | solution.py:232
  344.7 14.3 %collective-permute-done.72.got_ref = bf16[10,128,256]{2,1,0:T(8,128)(2,1)S(1)} collective-permute-done((bf16[10,128,256]{2,1,0:T(8,128)(2,1)}, bf16[10,128,256]{2,1,0:T(8,128)(2,1)S(1)}, u32[]{:S(2)}, u32[]{:S(2)}) %collective-permute-start.72) | collective-permute-done | bytes 655392 | tf_op jit(solution)/shard_map/ppermute | solution.py:197
  359.8 3.2 shard_map.203
  364.8 12.6 %collective-permute-done.73 = bf16[5,128,256]{2,1,0:T(8,128)(2,1)S(1)} collective-permute-done((bf16[5,128,256]{2,1,0:T(8,128)(2,1)}, bf16[5,128,256]{2,1,0:T(8,128)(2,1)S(1)}, u32[]{:S(2)}, u32[]{:S(2)}) %collective-permute-start.73) | collective-permute-done | bytes 327712 | tf_op jit(solution)/shard_map/ppermute | solution.py:197
  (273 shorter events, 114.1 us)
Async XLA Ops:
  10.2 16.1 %collective-permute-start.6 = (bf16[128,1024]{1,0:T(8,128)(2,1)}, bf16[128,1024]{1,0:T(8,128)(2,1)}, u32[]{:S(2)}, u32[]{:S(2)}) collective-permute-start(bf16[128,1024]{1,0:T(8,128)(2,1)} %refs_16_), channel_id=1, source_target_pairs={{0,16},{4,20},{8,24},{12,28},{16,0},{20,4},{24,8},{28,12},{1,17},{... | collective-permute-start | bytes 786440 | tf_op jit(solution)/shard_map/ppermute | solution.py:38
  11.8 16.2 %collective-permute-start.5 = (bf16[128,1024]{1,0:T(8,128)(2,1)}, bf16[128,1024]{1,0:T(8,128)(2,1)}, u32[]{:S(2)}, u32[]{:S(2)}) collective-permute-start(bf16[128,1024]{1,0:T(8,128)(2,1)} %refs_0_.6), channel_id=1, source_target_pairs={{0,8},{4,12},{8,0},{12,4},{16,24},{20,28},{24,16},{28,20},{1,9},{5... | collective-permute-start | bytes 786440 | tf_op jit(solution)/shard_map/ppermute | solution.py:38
  12.3 16.5 %collective-permute-start.7 = (bf16[128,1024]{1,0:T(8,128)(2,1)}, bf16[128,1024]{1,0:T(8,128)(2,1)}, u32[]{:S(2)}, u32[]{:S(2)}) collective-permute-start(bf16[128,1024]{1,0:T(8,128)(2,1)} %refs_0_.6), channel_id=1, source_target_pairs={{0,16},{4,20},{8,24},{12,28},{16,0},{20,4},{24,8},{28,12},{1,17},{... | collective-permute-start | bytes 786440 | tf_op jit(solution)/shard_map/ppermute | solution.py:38
  15.8 18.0 %collective-permute-start.3 = (bf16[128,1536]{1,0:T(8,128)(2,1)}, bf16[128,1536]{1,0:T(8,128)(2,1)}, u32[]{:S(2)}, u32[]{:S(2)}) collective-permute-start(bf16[128,1536]{1,0:T(8,128)(2,1)} %get-tuple-element.166.refs_0_), channel_id=1, source_target_pairs={{0,16},{4,20},{8,24},{12,28},{16,0},{20,4},{24,8},{28,12},{1,17},{... | collective-permute-start | bytes 1179656 | tf_op jit(solution)/shard_map/ppermute | solution.py:38
  19.6 42.3 %all-to-all-start = ((bf16[4,128,1024]{2,1,0:T(8,128)(2,1)}), bf16[4,128,1024]{2,1,0:T(8,128)(2,1)S(1)}, u32[]{:S(2)}, u32[]{:S(2)}) async-start(bf16[4,128,1024]{2,1,0:T(8,128)(2,1)} %param.11), calls=%async_computation | async-start | bytes 2097152 | tf_op jit(solution)/shard_map/all_to_all | solution.py:1073
  43.9 17.3 %collective-permute-start.8 = (bf16[128,1536]{1,0:T(8,128)(2,1)}, bf16[128,1536]{1,0:T(8,128)(2,1)S(1)}, u32[]{:S(2)}, u32[]{:S(2)}) collective-permute-start(bf16[128,1536]{1,0:T(8,128)(2,1)} %collective-permute-done.1.refs_1_), channel_id=1, source_target_pairs={{0,16},{4,20},{8,24},{12,28},{16,0},{20,4},{24,8},{28,12},{1,17},{... | collective-permute-start | bytes 1179656 | tf_op jit(solution)/shard_map/ppermute | solution.py:38
  44.4 17.2 %collective-permute-start.9 = (bf16[128,1536]{1,0:T(8,128)(2,1)}, bf16[128,1536]{1,0:T(8,128)(2,1)S(1)}, u32[]{:S(2)}, u32[]{:S(2)}) collective-permute-start(bf16[128,1536]{1,0:T(8,128)(2,1)} %collective-permute-done.4.refs_10_), channel_id=1, source_target_pairs={{0,8},{4,12},{8,0},{12,4},{16,24},{20,28},{24,16},{28,20},{1,9},{5... | collective-permute-start | bytes 1179656 | tf_op jit(solution)/shard_map/ppermute | solution.py:38
  45.0 16.2 %collective-permute-start.11 = (bf16[128,1024]{1,0:T(8,128)(2,1)}, bf16[128,1024]{1,0:T(8,128)(2,1)S(1)}, u32[]{:S(2)}, u32[]{:S(2)}) collective-permute-start(bf16[128,1024]{1,0:T(8,128)(2,1)} %collective-permute-done.7.refs_10_.refs_2_), channel_id=1, source_target_pairs={{0,8},{4,12},{8,0},{12,4},{16,24},{20,28},{24,16},{28,20},{1,9},{5... | collective-permute-start | bytes 786440 | tf_op jit(solution)/shard_map/ppermute | solution.py:38
  46.5 20.4 %collective-permute-start.14 = (bf16[128,1536]{1,0:T(8,128)(2,1)}, bf16[128,1536]{1,0:T(8,128)(2,1)}, u32[]{:S(2)}, u32[]{:S(2)}) collective-permute-start(bf16[128,1536]{1,0:T(8,128)(2,1)} %collective-permute-done.3.refs_2_), channel_id=1, source_target_pairs={{0,4},{4,0},{8,12},{12,8},{16,20},{20,16},{24,28},{28,24},{1,5},{5... | collective-permute-start | bytes 1179656 | tf_op jit(solution)/shard_map/ppermute | solution.py:38
  67.0 35.2 %collective-permute-start.30 = (bf16[128,2816]{1,0:T(8,128)(2,1)S(1)}, bf16[128,2816]{1,0:T(8,128)(2,1)S(1)}, u32[]{:S(2)}, u32[]{:S(2)}) collective-permute-start(bf16[128,2816]{1,0:T(8,128)(2,1)S(1)} %copy-done.7), channel_id=1, source_target_pairs={{0,16},{4,20},{8,24},{12,28},{16,0},{20,4},{24,8},{28,12},{1,17},{... | collective-permute-start | bytes 2162696 | tf_op jit(solution)/shard_map/ppermute | solution.py:38
  68.2 34.0 %collective-permute-start.28 = (bf16[128,2816]{1,0:T(8,128)(2,1)S(1)}, bf16[128,2816]{1,0:T(8,128)(2,1)}, u32[]{:S(2)}, u32[]{:S(2)}) collective-permute-start(bf16[128,2816]{1,0:T(8,128)(2,1)S(1)} %copy-done.7), channel_id=1, source_target_pairs={{0,8},{4,12},{8,0},{12,4},{16,24},{20,28},{24,16},{28,20},{1,9},{5... | collective-permute-start | bytes 2162696 | tf_op jit(solution)/shard_map/ppermute | solution.py:38
  68.7 33.5 %collective-permute-start.31 = (bf16[128,2816]{1,0:T(8,128)(2,1)S(1)}, bf16[128,2816]{1,0:T(8,128)(2,1)}, u32[]{:S(2)}, u32[]{:S(2)}) collective-permute-start(bf16[128,2816]{1,0:T(8,128)(2,1)S(1)} %copy-done.8), channel_id=1, source_target_pairs={{0,16},{4,20},{8,24},{12,28},{16,0},{20,4},{24,8},{28,12},{1,17},{... | collective-permute-start | bytes 2162696 | tf_op jit(solution)/shard_map/ppermute | solution.py:38
  69.6 32.7 %collective-permute-start.29 = (bf16[128,2816]{1,0:T(8,128)(2,1)S(1)}, bf16[128,2816]{1,0:T(8,128)(2,1)S(1)}, u32[]{:S(2)}, u32[]{:S(2)}) collective-permute-start(bf16[128,2816]{1,0:T(8,128)(2,1)S(1)} %copy-done.8), channel_id=1, source_target_pairs={{0,8},{4,12},{8,0},{12,4},{16,24},{20,28},{24,16},{28,20},{1,9},{5... | collective-permute-start | bytes 2162696 | tf_op jit(solution)/shard_map/ppermute | solution.py:38
  73.9 18.9 %collective-permute-start.27 = (bf16[128,1024]{1,0:T(8,128)(2,1)}, bf16[128,1024]{1,0:T(8,128)(2,1)}, u32[]{:S(2)}, u32[]{:S(2)}) collective-permute-start(bf16[128,1024]{1,0:T(8,128)(2,1)} %copy-done.28), channel_id=1, source_target_pairs={{0,4},{4,0},{8,12},{12,8},{16,20},{20,16},{24,28},{28,24},{1,5},{5... | collective-permute-start | bytes 786440 | tf_op jit(solution)/shard_map/ppermute | solution.py:38
  102.3 18.8 %collective-permute-start.32 = (bf16[128,2816]{1,0:T(8,128)(2,1)}, bf16[128,2816]{1,0:T(8,128)(2,1)}, u32[]{:S(2)}, u32[]{:S(2)}) collective-permute-start(bf16[128,2816]{1,0:T(8,128)(2,1)} %collective-permute-done.28.refs_1_), channel_id=1, source_target_pairs={{0,16},{4,20},{8,24},{12,28},{16,0},{20,4},{24,8},{28,12},{1,17},{... | collective-permute-start | bytes 2162696 | tf_op jit(solution)/shard_map/ppermute | solution.py:38
  103.5 18.4 %collective-permute-start.33 = (bf16[128,2816]{1,0:T(8,128)(2,1)}, bf16[128,2816]{1,0:T(8,128)(2,1)}, u32[]{:S(2)}, u32[]{:S(2)}) collective-permute-start(bf16[128,2816]{1,0:T(8,128)(2,1)} %collective-permute-done.31.refs_10_), channel_id=1, source_target_pairs={{0,8},{4,12},{8,0},{12,4},{16,24},{20,28},{24,16},{28,20},{1,9},{5... | collective-permute-start | bytes 2162696 | tf_op jit(solution)/shard_map/ppermute | solution.py:38
  104.0 17.9 %collective-permute-start.34 = (bf16[128,2816]{1,0:T(8,128)(2,1)S(1)}, bf16[128,2816]{1,0:T(8,128)(2,1)}, u32[]{:S(2)}, u32[]{:S(2)}) collective-permute-start(bf16[128,2816]{1,0:T(8,128)(2,1)S(1)} %copy-done.7), channel_id=1, source_target_pairs={{0,4},{4,0},{8,12},{12,8},{16,20},{20,16},{24,28},{28,24},{1,5},{5... | collective-permute-start | bytes 2162696 | tf_op jit(solution)/shard_map/ppermute | solution.py:38
  104.0 18.4 %collective-permute-start.38 = (bf16[128,2816]{1,0:T(8,128)(2,1)S(1)}, bf16[128,2816]{1,0:T(8,128)(2,1)}, u32[]{:S(2)}, u32[]{:S(2)}) collective-permute-start(bf16[128,2816]{1,0:T(8,128)(2,1)S(1)} %copy-done.8), channel_id=1, source_target_pairs={{0,4},{4,0},{8,12},{12,8},{16,20},{20,16},{24,28},{28,24},{1,5},{5... | collective-permute-start | bytes 2162696 | tf_op jit(solution)/shard_map/ppermute | solution.py:38
  104.5 18.0 %collective-permute-start.36 = (bf16[128,2816]{1,0:T(8,128)(2,1)S(1)}, bf16[128,2816]{1,0:T(8,128)(2,1)}, u32[]{:S(2)}, u32[]{:S(2)}) collective-permute-start(bf16[128,2816]{1,0:T(8,128)(2,1)S(1)} %collective-permute-done.30.refs_2_), channel_id=1, source_target_pairs={{0,4},{4,0},{8,12},{12,8},{16,20},{20,16},{24,28},{28,24},{1,5},{5... | collective-permute-start | bytes 2162696 | tf_op jit(solution)/shard_map/ppermute | solution.py:38
  104.5 40.5 %all-to-all-start.1 = ((bf16[4,128,1024]{2,1,0:T(8,128)(2,1)}), bf16[4,128,1024]{2,1,0:T(8,128)(2,1)S(1)}, u32[]{:S(2)}, u32[]{:S(2)}) async-start(bf16[4,128,1024]{2,1,0:T(8,128)(2,1)} %param.13), calls=%async_computation.1 | async-start | bytes 2097152 | tf_op jit(solution)/shard_map/all_to_all | solution.py:1073
  109.4 146.4 %reduce-scatter.2.cloned.1.call-start = ((), (), s32[]{:S(2)}) async-start(), calls=%async_computation.5 | async-start | bytes 6488064 | tf_op jit(solution)/shard_map/reduce_scatter | solution.py:1123
  125.6 16.3 %collective-permute-start.44 = (bf16[352,512]{1,0:T(8,128)(2,1)}, bf16[352,512]{1,0:T(8,128)(2,1)S(1)}, u32[]{:S(2)}, u32[]{:S(2)}) collective-permute-start(bf16[352,512]{1,0:T(8,128)(2,1)} %get-tuple-element.211.refs_16_), channel_id=1, source_target_pairs={{0,16},{4,20},{8,24},{12,28},{16,0},{20,4},{24,8},{28,12},{1,17},{... | collective-permute-start | bytes 1081352 | tf_op jit(solution)/shard_map/ppermute | solution.py:38
  127.3 16.8 %collective-permute-start.45 = (bf16[352,512]{1,0:T(8,128)(2,1)}, bf16[352,512]{1,0:T(8,128)(2,1)}, u32[]{:S(2)}, u32[]{:S(2)}) collective-permute-start(bf16[352,512]{1,0:T(8,128)(2,1)} %get-tuple-element.212.refs_24_), channel_id=1, source_target_pairs={{0,16},{4,20},{8,24},{12,28},{16,0},{20,4},{24,8},{28,12},{1,17},{... | collective-permute-start | bytes 1081352 | tf_op jit(solution)/shard_map/ppermute | solution.py:38
  128.2 16.8 %collective-permute-start.43 = (bf16[352,512]{1,0:T(8,128)(2,1)}, bf16[352,512]{1,0:T(8,128)(2,1)}, u32[]{:S(2)}, u32[]{:S(2)}) collective-permute-start(bf16[352,512]{1,0:T(8,128)(2,1)} %get-tuple-element.212.refs_24_), channel_id=1, source_target_pairs={{0,8},{4,12},{8,0},{12,4},{16,24},{20,28},{24,16},{28,20},{1,9},{5... | collective-permute-start | bytes 1081352 | tf_op jit(solution)/shard_map/ppermute | solution.py:38
  212.6 31.2 %all-to-all-start.2 = ((bf16[4,128,1024]{2,1,0:T(8,128)(2,1)}), bf16[4,128,1024]{2,1,0:T(8,128)(2,1)}, u32[]{:S(2)}, u32[]{:S(2)}) async-start(bf16[4,128,1024]{2,1,0:T(8,128)(2,1)} %bitcast.46), calls=%async_computation.2 | async-start | bytes 2097152 | tf_op jit(solution)/shard_map/all_to_all | solution.py:1073
  217.7 38.1 %collective-permute-start.58 = (bf16[256,2816]{1,0:T(8,128)(2,1)}, bf16[256,2816]{1,0:T(8,128)(2,1)}, u32[]{:S(2)}, u32[]{:S(2)}) collective-permute-start(bf16[256,2816]{1,0:T(8,128)(2,1)} %get-tuple-element.264), channel_id=1, source_target_pairs={{0,8},{4,12},{8,0},{12,4},{16,24},{20,28},{24,16},{28,20},{1,9},{5... | collective-permute-start | bytes 4325384 | tf_op jit(solution)/shard_map/ppermute | solution.py:38
  218.7 37.1 %collective-permute-start.59 = (bf16[256,2816]{1,0:T(8,128)(2,1)}, bf16[256,2816]{1,0:T(8,128)(2,1)}, u32[]{:S(2)}, u32[]{:S(2)}) collective-permute-start(bf16[256,2816]{1,0:T(8,128)(2,1)} %get-tuple-element.265), channel_id=1, source_target_pairs={{0,16},{4,20},{8,24},{12,28},{16,0},{20,4},{24,8},{28,12},{1,17},{... | collective-permute-start | bytes 4325384 | tf_op jit(solution)/shard_map/ppermute | solution.py:38
  256.4 46.2 %all-to-all-start.3 = ((bf16[4,128,1024]{2,1,0:T(8,128)(2,1)}), bf16[4,128,1024]{2,1,0:T(8,128)(2,1)}, u32[]{:S(2)}, u32[]{:S(2)}) async-start(bf16[4,128,1024]{2,1,0:T(8,128)(2,1)} %bitcast.45), calls=%async_computation.4 | async-start | bytes 2097152 | tf_op jit(solution)/shard_map/all_to_all | solution.py:1073
  266.3 18.4 %collective-permute-start.62 = (bf16[128,2816]{1,0:T(8,128)(2,1)}, bf16[128,2816]{1,0:T(8,128)(2,1)S(1)}, u32[]{:S(2)}, u32[]{:S(2)}) collective-permute-start(bf16[128,2816]{1,0:T(8,128)(2,1)} %add_convert_fusion.5), channel_id=1, source_target_pairs={{0,16},{4,20},{8,24},{12,28},{16,0},{20,4},{24,8},{28,12},{1,17},{... | collective-permute-start | bytes 2162696 | tf_op jit(solution)/shard_map/ppermute | solution.py:38
  267.7 18.2 %collective-permute-start.63 = (bf16[128,2816]{1,0:T(8,128)(2,1)}, bf16[128,2816]{1,0:T(8,128)(2,1)}, u32[]{:S(2)}, u32[]{:S(2)}) collective-permute-start(bf16[128,2816]{1,0:T(8,128)(2,1)} %add_convert_fusion.4), channel_id=1, source_target_pairs={{0,8},{4,12},{8,0},{12,4},{16,24},{20,28},{24,16},{28,20},{1,9},{5... | collective-permute-start | bytes 2162696 | tf_op jit(solution)/shard_map/ppermute | solution.py:38
  285.8 36.7 %collective-permute-start.66 = (bf16[256,2560]{1,0:T(8,128)(2,1)}, bf16[256,2560]{1,0:T(8,128)(2,1)}, u32[]{:S(2)}, u32[]{:S(2)}) collective-permute-start(bf16[256,2560]{1,0:T(8,128)(2,1)} %add_convert_fusion.3), channel_id=1, source_target_pairs={{0,8},{4,12},{8,0},{12,4},{16,24},{20,28},{24,16},{28,20},{1,9},{5... | collective-permute-start | bytes 3932168 | tf_op jit(solution)/shard_map/ppermute | solution.py:38
  286.4 36.2 %collective-permute-start.67 = (bf16[256,2560]{1,0:T(8,128)(2,1)}, bf16[256,2560]{1,0:T(8,128)(2,1)}, u32[]{:S(2)}, u32[]{:S(2)}) collective-permute-start(bf16[256,2560]{1,0:T(8,128)(2,1)} %add_convert_fusion.2), channel_id=1, source_target_pairs={{0,16},{4,20},{8,24},{12,28},{16,0},{20,4},{24,8},{28,12},{1,17},{... | collective-permute-start | bytes 3932168 | tf_op jit(solution)/shard_map/ppermute | solution.py:38
  (98 other events, 954.8 us)
Sparse Core Ops, SparseCore 0:
  155.3 58.9 reduce-scatter.1
